TPU v7x, 128 devices: a whole 4x4x4 slice. The times are simulated.
128 devices in a mesh: gx: 16 (over y_hi, z, core), gy: 8 (over y_lo, x).
Axes of the slice: x: 4, y: 4 (y_hi: 2, y_lo: 2; y = y_hi * 2 + y_lo), z: 4, core: 2. Of those that a mesh axis runs over, the one named last changes fastest.
Arguments:
- flow_pops: float32 [19, 512, 16384], P(None, 'gx', 'gy'), may hold values from 0 to 1, as said below
- heat_pops: float32 [7, 512, 16384], P(None, 'gx', 'gy'), may hold values from 0 to 1, as said below
- solid_flag: int32 [512, 16384], P('gx', 'gy'), may hold values 0 or 1
- brick_temp: float32 [256, 512], P(('gx', 'gy')), may hold values from 2 to 6
- brick_ids: int32 [256], replicated, may hold values from 0 to 255, each once
- brick_links: int32 [256, 6], replicated, may hold values from -1 to 255, as said below
- face_cell: int32 [131072], replicated, may hold values from 0 to 65535
- face_owner: int32 [131072, 1], replicated, may hold values from 0 to 127; in each aligned block of 1024 rows (0 to 1023, 1024 to 2047, ...) at most 16 rows name the same one
- face_spot: int32 [131072], replicated, may hold values from 0 to 1023
Outputs:
- flow_out: float32 [19, 512, 16384], P(None, 'gx', 'gy')
- heat_out: float32 [7, 512, 16384], P(None, 'gx', 'gy')
- brick_out: float32 [256, 512], P(('gx', 'gy'))
Inputs may be any that keep to these rules, and one draw needn't show every extreme that they name: `flow_pops`: each population f_i is its lattice weight times a factor within 0.55 to 1.45. `heat_pops`: each population g_j is its lattice weight times a factor within 0.3 to 1.7. `brick_ids`: A permutation of the brick numbers. `brick_links`: -1 marks a side with no neighbour; links are mutual: if a names b on side s, b names a on the other side of that axis. `face_owner`: among the 1024 faces of one fluid device, no device is named more than 16 times.
All inputs are finite; a program needn't handle non-finite values. No bound on the sum of `solid_flag` on one device may be relied on, other than what follows from the above.
Results may differ from a plain program's by a relative error of at most 0.0003.
Values sent between devices are 32-bit elements; how exact they have to be, the bound alone decides.
A program may use at most 192 MiB of HBM per device.

v0:
```python
import jax
import jax.numpy as jnp
from jax import lax
from jax.sharding import PartitionSpec as P

NZ = 32
STEPS = 2
BE = 8


VELOCITY = [
    (0, 0, 0),
    (1, 0, 0),
    (-1, 0, 0),
    (0, 1, 0),
    (0, -1, 0),
    (0, 0, 1),
    (0, 0, -1),
    (1, 1, 0),
    (-1, -1, 0),
    (1, -1, 0),
    (-1, 1, 0),
    (1, 0, 1),
    (-1, 0, -1),
    (1, 0, -1),
    (-1, 0, 1),
    (0, 1, 1),
    (0, -1, -1),
    (0, 1, -1),
    (0, -1, 1),
]
OPPOSITE = [0, 2, 1, 4, 3, 6, 5, 8, 7, 10, 9, 12, 11, 14, 13, 16, 15, 18, 17]
WEIGHTS_FLOW = [1.0 / 3.0] + [1.0 / 18.0] * 6 + [1.0 / 36.0] * 12
WEIGHTS_HEAT = [0.25] + [0.125] * 6
SIDE_SWAP = [1, 0, 3, 2, 5, 4]
TAU_FLOW = 0.8
TAU_HEAT = 0.9
BUOYANCY = 0.002
HEAT_REF = 1.0
WALL_COEF = 0.1
BRICK_LOSS = 0.5
COND_BASE = 0.04
COND_SLOPE = 0.1
LATENT = 2.0
MELT = 4.0
MELT_WIDTH = 0.5
EXACT = lax.Precision.HIGHEST


def with_halo(block, sides, width):
    for axis, dim in sides:
        count = lax.axis_size(axis)
        forward = [(i, i + 1) for i in range(count - 1)]
        backward = [(target, source) for source, target in forward]
        low = lax.ppermute(
            lax.slice_in_dim(block, block.shape[dim] - width, None, axis=dim), axis, forward
        )
        high = lax.ppermute(lax.slice_in_dim(block, 0, width, axis=dim), axis, backward)
        block = jnp.concatenate([low, block, high], axis=dim)
    return block


def dotted(vector, velocity):
    terms = [velocity[a] * vector[a] for a in range(3) if velocity[a] != 0]
    if not terms:
        return jnp.zeros_like(vector[0])
    return sum(terms[1:], terms[0])


def collide(flow_pops, heat_pops, solid_mask):
    density = jnp.sum(flow_pops, axis=0)
    momentum = [
        sum((VELOCITY[i][a] * flow_pops[i] for i in range(19) if VELOCITY[i][a] != 0))
        for a in range(3)
    ]
    velocity = [m / density for m in momentum]
    fluid_temp = jnp.sum(heat_pops, axis=0)
    forcing = BUOYANCY * (fluid_temp - HEAT_REF)
    shifted = [velocity[0], velocity[1], velocity[2] + TAU_FLOW * forcing / density]
    speed_sq = shifted[0] * shifted[0] + shifted[1] * shifted[1] + shifted[2] * shifted[2]
    relaxed_flow = []
    for i in range(19):
        along = dotted(shifted, VELOCITY[i])
        equilibrium = (
            WEIGHTS_FLOW[i] * density * (1.0 + 3.0 * along + 4.5 * along * along - 1.5 * speed_sq)
        )
        relaxed = flow_pops[i] - (flow_pops[i] - equilibrium) / TAU_FLOW
        relaxed_flow.append(jnp.where(solid_mask, flow_pops[OPPOSITE[i]], relaxed))
    relaxed_heat = []
    for j in range(7):
        along = dotted(velocity, VELOCITY[j])
        equilibrium = WEIGHTS_HEAT[j] * fluid_temp * (1.0 + 4.0 * along)
        relaxed = heat_pops[j] - (heat_pops[j] - equilibrium) / TAU_HEAT
        relaxed_heat.append(jnp.where(solid_mask, heat_pops[OPPOSITE[j]], relaxed))
    return (jnp.stack(relaxed_flow), jnp.stack(relaxed_heat), fluid_temp)


def propagate_flat(extended, velocities, row_count, flat_width):
    depth_pos = lax.broadcasted_iota(jnp.int32, (row_count, flat_width), 1) % NZ
    moved = []
    for i, v in enumerate(velocities):
        start = (1 - v[1]) * NZ
        piece = extended[i, 1 - v[0] : 1 - v[0] + row_count, start : start + flat_width]
        if v[2] == 1:
            piece = jnp.where(depth_pos == 0, 0.0, jnp.roll(piece, 1, axis=1))
        elif v[2] == -1:
            piece = jnp.where(depth_pos == NZ - 1, 0.0, jnp.roll(piece, -1, axis=1))
        moved.append(piece)
    return jnp.stack(moved)


def brick_faces(bricks):
    count = bricks.shape[0]
    cube = bricks.reshape(count, BE, BE, BE)
    layers = [
        cube[:, 0],
        cube[:, -1],
        cube[:, :, 0],
        cube[:, :, -1],
        cube[:, :, :, 0],
        cube[:, :, :, -1],
    ]
    return jnp.stack(layers, axis=1).reshape(count, 6, BE * BE)


def fill_ghosts(every_face, own_faces, link_slot, linked):
    swap = jnp.array(SIDE_SWAP, jnp.int32)
    remote = every_face[link_slot, swap[None, :]]
    return jnp.where(linked[:, :, None], remote, own_faces)


def conduct(bricks, ghost, loss):
    count = bricks.shape[0]
    cube = bricks.reshape(count, BE, BE, BE)
    sides = ghost.reshape(count, 6, BE, BE)
    beside = [
        jnp.concatenate([sides[:, 0][:, None], cube[:, :-1]], axis=1),
        jnp.concatenate([cube[:, 1:], sides[:, 1][:, None]], axis=1),
        jnp.concatenate([sides[:, 2][:, :, None], cube[:, :, :-1]], axis=2),
        jnp.concatenate([cube[:, :, 1:], sides[:, 3][:, :, None]], axis=2),
        jnp.concatenate([sides[:, 4][..., None], cube[..., :-1]], axis=3),
        jnp.concatenate([cube[..., 1:], sides[:, 5][..., None]], axis=3),
    ]
    conduct_here = COND_BASE * (1.0 + COND_SLOPE * cube)
    spread = sum(
        (
            0.5 * (conduct_here + COND_BASE * (1.0 + COND_SLOPE * other)) * (other - cube)
            for other in beside
        )
    )
    phase = jax.nn.sigmoid((cube - MELT) / MELT_WIDTH)
    capacity = 1.0 + LATENT * phase * (1.0 - phase) / MELT_WIDTH
    updated = cube + (spread - BRICK_LOSS * loss.reshape(cube.shape)) / capacity
    return updated.reshape(count, BE * BE * BE)


def body(
    flow_pops,
    heat_pops,
    solid_flag,
    brick_temp,
    brick_ids,
    brick_links,
    face_cell,
    face_owner,
    face_spot,
):
    grid_rows = lax.axis_size("gx")
    grid_cols = lax.axis_size("gy")
    devices = grid_rows * grid_cols
    device_id = lax.axis_index("gx") * grid_cols + lax.axis_index("gy")
    block_rows = flow_pops.shape[1]
    flat_width = flow_pops.shape[2]
    cell_count = block_rows * flat_width
    flow_now = flow_pops
    heat_now = heat_pops
    solid_mask = solid_flag == 1
    per_device = face_cell.shape[0] // devices
    capacity = max(2, 2 * per_device // devices)
    owners = face_owner[:, 0]
    own_cell = lax.dynamic_slice_in_dim(face_cell, device_id * per_device, per_device)
    own_owner = lax.dynamic_slice_in_dim(owners, device_id * per_device, per_device)
    targets = jnp.arange(devices, dtype=jnp.int32)
    onehot = (own_owner[:, None] == targets[None, :]).astype(jnp.int32)
    own_rank = jnp.sum(jnp.cumsum(onehot, axis=0) * onehot, axis=1) - 1
    send_slot = own_owner * capacity + own_rank
    slot_table = (
        send_slot[:, None] == jnp.arange(devices * capacity, dtype=jnp.int32)[None, :]
    ).astype(jnp.float32)
    mine = (owners == device_id).astype(jnp.int32).reshape(devices, per_device)
    recv_rank = jnp.where(mine == 1, jnp.cumsum(mine, axis=1) - 1, capacity)
    sources = jnp.broadcast_to(targets[:, None], (devices, per_device))
    recv_spot = (
        jnp.zeros((devices, capacity), jnp.int32)
        .at[sources, recv_rank]
        .set(face_spot.reshape(devices, per_device), mode="drop")
    )
    recv_live = (
        jnp.zeros((devices, capacity), jnp.float32).at[sources, recv_rank].set(1.0, mode="drop")
    )
    cell_row = own_cell // flat_width
    cell_col = own_cell % flat_width
    row_table = (cell_row[:, None] == jnp.arange(block_rows, dtype=jnp.int32)[None, :]).astype(
        jnp.float32
    )
    col_table = (cell_col[:, None] == jnp.arange(flat_width, dtype=jnp.int32)[None, :]).astype(
        jnp.float32
    )
    bricks_here = brick_temp.shape[0]
    brick_cells = bricks_here * brick_temp.shape[1]
    spot_table = (
        recv_spot.reshape(-1)[:, None] == jnp.arange(brick_cells, dtype=jnp.int32)[None, :]
    ).astype(jnp.float32)
    all_bricks = brick_ids.shape[0]
    slot_of = (
        jnp.zeros((all_bricks,), jnp.int32)
        .at[brick_ids]
        .set(jnp.arange(all_bricks, dtype=jnp.int32))
    )
    own_slots = device_id * bricks_here + jnp.arange(bricks_here, dtype=jnp.int32)
    own_links = brick_links[brick_ids[own_slots]]
    link_slot = slot_of[jnp.maximum(own_links, 0)]
    linked = own_links >= 0
    brick_now = brick_temp
    every_velocity = VELOCITY + VELOCITY[:7]
    weights_heat = jnp.array(WEIGHTS_HEAT, jnp.float32).reshape(7, 1, 1)
    for step_index in range(STEPS):
        relaxed_flow, relaxed_heat, fluid_temp = collide(flow_now, heat_now, solid_mask)
        face_temp = fluid_temp.reshape(cell_count)[own_cell]
        outgoing = jnp.dot(face_temp, slot_table, precision=EXACT).reshape(devices, capacity)
        arrived = lax.all_to_all(outgoing, ("gx", "gy"), split_axis=0, concat_axis=0, tiled=True)
        flat_brick = brick_now.reshape(-1)
        wall_flux = WALL_COEF * (flat_brick[recv_spot] - arrived) * recv_live
        brick_loss = jnp.dot(wall_flux.reshape(-1), spot_table, precision=EXACT).reshape(
            brick_now.shape
        )
        returned = lax.all_to_all(wall_flux, ("gx", "gy"), split_axis=0, concat_axis=0, tiled=True)
        face_flux = jnp.dot(slot_table, returned.reshape(-1), precision=EXACT)
        heat_gain = jnp.dot((row_table * face_flux[:, None]).T, col_table, precision=EXACT)
        relaxed_heat = relaxed_heat + weights_heat * heat_gain[None]
        combined = jnp.concatenate([relaxed_flow, relaxed_heat], axis=0)
        widened = with_halo(combined, (("gx", 1),), 1)
        extended = with_halo(widened, (("gy", 2),), NZ)
        moved = propagate_flat(extended, every_velocity, block_rows, flat_width)
        flow_now = moved[:19]
        heat_now = moved[19:]
        faces_here = brick_faces(brick_now)
        every_face = lax.all_gather(
            faces_here.reshape(bricks_here, 6 * BE * BE), ("gx", "gy"), axis=0, tiled=True
        ).reshape(all_bricks, 6, BE * BE)
        ghost = fill_ghosts(every_face, faces_here, link_slot, linked)
        brick_now = conduct(brick_now, ghost, brick_loss)
    return (flow_now, heat_now, brick_now)


def solution(mesh):
    return jax.shard_map(
        body,
        mesh=mesh,
        in_specs=(
            P(None, "gx", "gy"),
            P(None, "gx", "gy"),
            P("gx", "gy"),
            P(("gx", "gy"), None),
            P(),
            P(),
            P(),
            P(),
            P(),
        ),
        out_specs=(P(None, "gx", "gy"), P(None, "gx", "gy"), P(("gx", "gy"), None)),
        check_vma=False,
    )
```

profile of v0, /device:TPU:1, one launch (start us, length us, event | category | flops | bytes accessed | tf_op | source)
XLA Modules:
  0.0 1933.5 jit_solution(13445770210953103342)
XLA Ops:
  8.7 6.1 gather_fusion.1
  18.3 12.0 all-to-all-start
  40.7 479.1 %scatter_custom_fusion.1 = s32[2048]{0:T(1024)S(1)} fusion(s32[131072]{0:T(1024)S(1)} %bitcast.850, s32[131072]{0:T(1024)} %param.20, s32[]{:T(128)} %constant.220.clone.1), kind=kCustom, calls=%fused_computation.700 | custom fusion | bytes 8704
  522.4 303.4 %all-gather = f32[128,2,384]{2,1,0:T(2,128)S(1)} all-gather(f32[1,2,384]{2,1,0:T(2,128)S(1)} %reshape.2177), channel_id=1, replica_groups=mesh['gx'=16,'gy'=8] {'gx','gy'}, dimensions={0}, use_global_device_ids=true | all-gather | bytes 396288 | tf_op jit(solution)/shard_map/all_gather | solution.py:248
  850.4 8.6 gather_fusion
  859.1 479.4 %scatter_custom_fusion.2 = f32[2048]{0:T(1024)S(1)} fusion(s32[131072]{0:T(1024)} %bitcast.851, f32[131072]{0:T(1024)S(1)} %broadcast.1893, f32[]{:T(128)} %constant.197.clone.1), kind=kCustom, calls=%fused_computation.698 | custom fusion | bytes 8704
  1342.3 27.9 %fusion.2 = f32[1,2,8,8,8]{4,0,3,2,1:T(1,128)S(1)} fusion(s32[2,8,8,8]{3,2,1,0:T(8,128)S(1)} %copy-done.83, s32[2048]{0:T(1024)S(1)} %eq.337, f32[2048,1,1,1,1]{0,1,2,3,4:T(1,128)S(1)} %reshape.2189), kind=kOutput, calls=%fused_computation.14 | convolution fusion | flops 27262976 | bytes 24576 | tf_op jit(solution)/shard_map/dot_general | solution.py:234
  1372.8 311.9 %all-gather.1 = f32[128,2,384]{2,1,0:T(2,128)S(1)} all-gather(f32[1,2,384]{2,1,0:T(2,128)S(1)} %reshape.2179), channel_id=1, replica_groups=mesh['gx'=16,'gy'=8] {'gx','gy'}, dimensions={0}, use_global_device_ids=true | all-gather | bytes 396288 | tf_op jit(solution)/shard_map/all_gather | solution.py:248
  1686.3 20.6 %all-to-all-start.1 = ((f32[128,1,16]{2,1,0:T(1,128)}), f32[128,1,16]{2,1,0:T(1,128)S(1)}, u32[]{:S(2)}, u32[]{:S(2)}) async-start(f32[128,1,16]{2,1,0:T(1,128)} %bitcast.72), calls=%async_computation.1 | async-start | bytes 131072 | tf_op jit(solution)/shard_map/all_to_all | solution.py:237
  1709.1 8.6 gather_fusion.6
  1719.9 3.8 fusion.8
  1731.6 3.8 collective-permute-start
  1738.2 4.4 collective-permute-done.1
  1744.3 3.9 collective-permute-start.2
  1755.0 4.8 collective-permute-done.3
  1776.7 10.6 gather_fusion.7
  1787.4 4.0 fusion.7
  1792.9 13.3 all-to-all-start.2
  1825.0 27.9 %fusion = f32[1,2,8,8,8]{4,0,3,2,1:T(1,128)S(1)} fusion(s32[2,8,8,8]{3,2,1,0:T(8,128)S(1)} %copy-done.84, s32[2048]{0:T(1024)S(1)} %copy-done.92, f32[2048,1,1,1,1]{0,1,2,3,4:T(1,128)S(1)} %reshape.2195), kind=kOutput, calls=%fused_computation.12 | convolution fusion | flops 27262976 | bytes 24576 | tf_op jit(solution)/shard_map/dot_general | solution.py:234
  1852.9 10.1 all-to-all-start.3
  1864.0 8.6 all-to-all-done.3
  1873.5 3.8 fusion.6
  1891.9 4.4 collective-permute-done.5
  1906.6 4.1 collective-permute-done.7
  (494 shorter events, 165.1 us)
Async XLA Ops:
  18.3 1321.6 %all-to-all-start = ((f32[128,1,16]{2,1,0:T(1,128)}), f32[128,1,16]{2,1,0:T(1,128)}, u32[]{:S(2)}, u32[]{:S(2)}) async-start(f32[128,1,16]{2,1,0:T(1,128)} %bitcast.67), calls=%async_computation | async-start | bytes 131072 | tf_op jit(solution)/shard_map/all_to_all | solution.py:231
  34.0 795.5 %copy-start.102 = (pred[2,6]{1,0:T(4,128)(4,1)}, pred[2,6]{1,0:T(4,128)(4,1)S(1)}, u32[]{:S(2)}) copy-start(pred[2,6]{1,0:T(4,128)(4,1)S(1)} %broadcast_compare_fusion.1) | copy-start | bytes 40
  35.3 1715.6 %copy-start.12 = (s32[2048]{0:T(1024)}, s32[2048]{0:T(1024)S(1)}, u32[]{:S(2)}) copy-start(s32[2048]{0:T(1024)S(1)} %fusion.395) | copy-start | bytes 24580
  35.4 1715.6 %copy-start.15 = (s32[2048]{0:T(1024)}, s32[2048]{0:T(1024)S(1)}, u32[]{:S(2)}) copy-start(s32[2048]{0:T(1024)S(1)} %iota_and_fusion) | copy-start | bytes 24580
  37.7 484.5 %copy-start.106 = (s32[6]{0:T(128)S(1)}, s32[6]{0:T(128)}, u32[]{:S(2)}) copy-start(s32[6]{0:T(128)} %constant.287) | copy-start | bytes 76
  40.7 479.2 %copy-start.53 = (s32[16,8,8,128]{3,1,2,0:T(8,128)}, s32[16,8,8,128]{3,1,2,0:T(8,128)S(1)}, u32[]{:S(2)}) copy-start(s32[16,8,8,128]{3,1,2,0:T(8,128)S(1)} %copy.311) | copy-start | bytes 1572868
  847.5 903.5 %copy-start.33 = (pred[2048]{0:T(1024)(128)(4,1)}, pred[2048]{0:T(1024)(128)(4,1)S(1)}, u32[]{:S(2)}) copy-start(pred[2048]{0:T(1024)(128)(4,1)S(1)} %fusion.398) | copy-start | bytes 6148
  850.4 491.9 %copy-start.83 = (s32[2,8,8,8]{3,2,1,0:T(8,128)S(1)}, s32[2,8,8,8]{3,2,1,0:T(8,128)}, u32[]{:S(2)}) copy-start(s32[2,8,8,8]{3,2,1,0:T(8,128)} %multiply_add_fusion.2) | copy-start | bytes 12292
  859.0 511.2 %copy-start.74 = (f32[2,8,8,7]{3,2,1,0:T(8,128)S(1)}, f32[2,8,8,7]{3,2,1,0:T(8,128)}, u32[]{:S(2)}) copy-start(f32[2,8,8,7]{3,2,1,0:T(8,128)} %get-tuple-element.127) | copy-start | bytes 10756
  859.0 511.2 %copy-start.75 = (f32[2,8,8,7]{3,2,1,0:T(8,128)S(1)}, f32[2,8,8,7]{3,2,1,0:T(8,128)}, u32[]{:S(2)}) copy-start(f32[2,8,8,7]{3,2,1,0:T(8,128)} %get-tuple-element.128) | copy-start | bytes 10756
  859.0 511.2 %copy-start.79 = (f32[2,7,8,8]{3,2,1,0:T(8,128)S(1)}, f32[2,7,8,8]{3,2,1,0:T(8,128)}, u32[]{:S(2)}) copy-start(f32[2,7,8,8]{3,2,1,0:T(8,128)} %get-tuple-element.123) | copy-start | bytes 10756
  859.0 511.2 %copy-start.80 = (f32[2,7,8,8]{3,2,1,0:T(8,128)S(1)}, f32[2,7,8,8]{3,2,1,0:T(8,128)}, u32[]{:S(2)}) copy-start(f32[2,7,8,8]{3,2,1,0:T(8,128)} %get-tuple-element.124) | copy-start | bytes 10756
  1338.9 346.5 %copy-start.91 = (s32[2048]{0:T(1024)}, s32[2048]{0:T(1024)S(1)}, u32[]{:S(2)}) copy-start(s32[2048]{0:T(1024)S(1)} %eq.337) | copy-start | bytes 24580
  1686.3 32.2 %all-to-all-start.1 = ((f32[128,1,16]{2,1,0:T(1,128)}), f32[128,1,16]{2,1,0:T(1,128)S(1)}, u32[]{:S(2)}, u32[]{:S(2)}) async-start(f32[128,1,16]{2,1,0:T(1,128)} %bitcast.72), calls=%async_computation.1 | async-start | bytes 131072 | tf_op jit(solution)/shard_map/all_to_all | solution.py:237
  1731.6 6.6 collective-permute-start
  1735.4 7.2 collective-permute-start.1
  1744.3 9.4 collective-permute-start.2
  1749.3 10.6 collective-permute-start.3
  1792.9 29.6 %all-to-all-start.2 = ((f32[128,1,16]{2,1,0:T(1,128)}), f32[128,1,16]{2,1,0:T(1,128)}, u32[]{:S(2)}, u32[]{:S(2)}) async-start(f32[128,1,16]{2,1,0:T(1,128)} %bitcast.852), calls=%async_computation.2 | async-start | bytes 131072 | tf_op jit(solution)/shard_map/all_to_all | solution.py:231
  1852.9 19.7 %all-to-all-start.3 = ((f32[128,1,16]{2,1,0:T(1,128)}), f32[128,1,16]{2,1,0:T(1,128)S(1)}, u32[]{:S(2)}, u32[]{:S(2)}) async-start(f32[128,1,16]{2,1,0:T(1,128)} %bitcast.146), calls=%async_computation.3 | async-start | bytes 131072 | tf_op jit(solution)/shard_map/all_to_all | solution.py:237
  1886.1 5.9 collective-permute-start.4
  1889.2 7.2 collective-permute-start.5
  1898.0 8.3 collective-permute-start.6
  1900.3 10.4 collective-permute-start.7
  (99 other events, 1874.4 us)
where the time goes:
time: 1950 us; the launch traced here: 1930 us
  local copies, waits for them, and re-layouts  1040 us (53%)
  blocking collectives  615 us (32%)
  other arithmetic  90.6 us (5%)
  matrix products  76.7 us (4%)
  starting transfers between devices  75.6 us (4%)
  waiting for transfers between devices  29.3 us (2%)
    unnamed x250, local copies, waits for them, and re-layouts  966 us
    all_gather x2, blocking collectives, body(): lax.all_gather(faces_here.reshape(bricks_here, 6 * BE * BE), ('gx', 'gy')...  615 us
    unnamed x73, other arithmetic  63.3 us
    dot_general x2, matrix products, body(): jnp.dot(wall_flux.reshape(-1), spot_table, precision=EXACT)  55.7 us
  transfers between devices with their start and end apart: 12, of which 8 were waited for; matrix products, arithmetic and copies ran while one was open for 54% of the time, Pallas kernels for 0%

commit v1 on v0

--- a/solution.py
+++ b/solution.py
@@ -189,15 +189,11 @@
     ).astype(jnp.float32)
     mine = (owners == device_id).astype(jnp.int32).reshape(devices, per_device)
     recv_rank = jnp.where(mine == 1, jnp.cumsum(mine, axis=1) - 1, capacity)
-    sources = jnp.broadcast_to(targets[:, None], (devices, per_device))
-    recv_spot = (
-        jnp.zeros((devices, capacity), jnp.int32)
-        .at[sources, recv_rank]
-        .set(face_spot.reshape(devices, per_device), mode="drop")
-    )
-    recv_live = (
-        jnp.zeros((devices, capacity), jnp.float32).at[sources, recv_rank].set(1.0, mode="drop")
-    )
+    ranks = jnp.arange(capacity, dtype=jnp.int32)[None, :, None]
+    chosen = recv_rank[:, None, :] == ranks
+    spots = face_spot.reshape(devices, 1, per_device)
+    recv_spot = jnp.sum(jnp.where(chosen, spots, 0), axis=2)
+    recv_live = jnp.sum(jnp.where(chosen, 1.0, 0.0), axis=2)
     cell_row = own_cell // flat_width
     cell_col = own_cell % flat_width
     row_table = (cell_row[:, None] == jnp.arange(block_rows, dtype=jnp.int32)[None, :]).astype(
@@ -245,8 +241,13 @@
         flow_now = moved[:19]
         heat_now = moved[19:]
         faces_here = brick_faces(brick_now)
-        every_face = lax.all_gather(
-            faces_here.reshape(bricks_here, 6 * BE * BE), ("gx", "gy"), axis=0, tiled=True
+        own_copy = faces_here.reshape(1, bricks_here * 6 * BE * BE)
+        every_face = lax.all_to_all(
+            jnp.broadcast_to(own_copy, (devices, own_copy.shape[1])),
+            ("gx", "gy"),
+            split_axis=0,
+            concat_axis=0,
+            tiled=True,
         ).reshape(all_bricks, 6, BE * BE)
         ghost = fill_ghosts(every_face, faces_here, link_slot, linked)
         brick_now = conduct(brick_now, ghost, brick_loss)

time: 1950 us -> 415 us (0.21)
  the two profiles are of different devices: /device:TPU:1 before, /device:TPU:22 now
where the time goes in v1:
time: 415 us; the launch traced here: 410 us
  other arithmetic  121 us (29%)
  local copies, waits for them, and re-layouts  89.9 us (22%)
  starting transfers between devices  85.7 us (21%)
  matrix products  78 us (19%)
  waiting for transfers between devices  31.9 us (8%)
    unnamed x70, other arithmetic  63 us
    dot_general x2, matrix products, body(): jnp.dot(wall_flux.reshape(-1), spot_table, precision=EXACT)  57 us
    another operation x5, other arithmetic  23.6 us
    ppermute x4, starting transfers between devices, with_halo(): lax.ppermute(lax.slice_in_dim(block, 0, width, axis=dim), axis, backward)  20.4 us
    all_to_all x2, starting transfers between devices, body(): lax.all_to_all(outgoing, ('gx', 'gy'), split_axis=0, concat_axis=0, tiled...  19.9 us
    gather x6, local copies, waits for them, and re-layouts, body(): wall_flux = WALL_COEF * (flat_brick[recv_spot] - arrived) * recv_live  17.6 us
    all_to_all x2, starting transfers between devices, body(): lax.all_to_all(wall_flux, ('gx', 'gy'), split_axis=0, concat_axis=0, tile...  17.5 us
    all_to_all x2, starting transfers between devices, body(): lax.all_to_all(jnp.broadcast_to(own_copy, (devices, own_copy.shape[1])),...  17.5 us
  transfers between devices with their start and end apart: 14, of which 10 were waited for; matrix products, arithmetic and copies ran while one was open for 41% of the time, Pallas kernels for 0%

profile of v1, /device:TPU:22, one launch (start us, length us, event | category | flops | bytes accessed | tf_op | source)
XLA Modules:
  0.0 409.6 jit_solution(13498241374448458616)
XLA Ops:
  8.7 6.1 %gather_fusion.1 = f32[1024]{0:T(1024)S(1)} fusion(f32[65536]{0:T(1024)S(1)} %bitcast.807, s32[1024]{0:T(1024)S(1)} %get-tuple-element.113), kind=kCustom, calls=%fused_computation.1 | custom fusion | bytes 12288 | tf_op jit(solution)/shard_map/gather | solution.py:225
  18.4 11.1 %all-to-all-start = ((f32[128,1,16]{2,1,0:T(1,128)}), f32[128,1,16]{2,1,0:T(1,128)}, u32[]{:S(2)}, u32[]{:S(2)}) async-start(f32[128,1,16]{2,1,0:T(1,128)} %bitcast.65), calls=%async_computation | async-start | bytes 131072 | tf_op jit(solution)/shard_map/all_to_all | solution.py:227
  37.4 23.3 %fusion.432 = s32[128,8,128]{0,1,2:T(8,128)S(1)} fusion(s32[128,8,128]{0,1,2:T(8,128)S(1)} %copy.348), kind=kOutput, calls=%fused_computation.730 | output fusion | flops 16646144 | bytes 1048576 | tf_op jit(solution)/shard_map/reduce-window.2
  93.2 8.6 %gather_fusion = f32[2048]{0:T(1024)S(1)} fusion(f32[1024]{0:T(1024)S(1)} %bitcast.802, s32[2048]{0:T(1024)S(1)} %broadcast_clamp_fusion), kind=kCustom, calls=%fused_computation | custom fusion | bytes 24576 | tf_op jit(solution)/shard_map/gather | solution.py:229
  106.6 10.2 %all-to-all-start.1 = ((f32[128,1,16]{2,1,0:T(1,128)}), f32[128,1,16]{2,1,0:T(1,128)S(1)}, u32[]{:S(2)}, u32[]{:S(2)}) async-start(f32[128,1,16]{2,1,0:T(1,128)} %copy.355), calls=%async_computation.1 | async-start | bytes 131072 | tf_op jit(solution)/shard_map/all_to_all | solution.py:233
  116.9 28.5 %fusion.2 = f32[1,2,8,8,8]{4,0,3,2,1:T(1,128)} fusion(f32[2048,1,1,1,1]{0,1,4,3,2:T(1,128)S(1)} %bitcast.858, s32[2,8,8,8]{3,2,1,0:T(8,128)S(1)} %copy-done.87, s32[2048]{0:T(1024)S(1)} %eq.347), kind=kOutput, calls=%fused_computation.12 | convolution fusion | flops 27262976 | bytes 24576 | tf_op jit(solution)/shard_map/dot_general | solution.py:230
  146.4 3.8 fusion.8
  160.2 7.5 %collective-permute-start.1 = (f32[26,1,2048]{2,1,0:T(1,128)S(1)}, f32[26,1,2048]{2,1,0:T(1,128)S(1)}, u32[]{:S(2)}, u32[]{:S(2)}) collective-permute-start(f32[26,1,2048]{2,1,0:T(1,128)S(1)} %get-tuple-element.104), channel_id=1, source_target_pairs={{8,0},{16,8},{24,16},{32,24},{40,32},{48,40},{56,48},{64,56},{72,6... | collective-permute-start | bytes 638984 | tf_op jit(solution)/shard_map/ppermute | solution.py:58
  180.9 3.6 collective-permute-done.2
  185.8 4.8 %collective-permute-done.3 = f32[26,34,32]{1,2,0:T(8,128)S(1)} collective-permute-done((f32[26,34,32]{1,2,0:T(8,128)}, f32[26,34,32]{1,2,0:T(8,128)S(1)}, u32[]{:S(2)}, u32[]{:S(2)}) %collective-permute-start.3) | collective-permute-done | bytes 113184 | tf_op jit(solution)/shard_map/ppermute | solution.py:58
  207.4 10.6 %gather_fusion.7 = f32[1024]{0:T(1024)} fusion(f32[65536]{0:T(1024)S(1)} %add_add_fusion.1, s32[1024]{0:T(1024)} %copy-done.89), kind=kCustom, calls=%fused_computation.7 | custom fusion | bytes 12288 | tf_op jit(solution)/shard_map/gather | solution.py:225
  218.0 4.0 fusion.7
  223.4 8.8 %all-to-all-start.3 = ((f32[128,1,16]{2,1,0:T(1,128)}), f32[128,1,16]{2,1,0:T(1,128)}, u32[]{:S(2)}, u32[]{:S(2)}) async-start(f32[128,1,16]{2,1,0:T(1,128)} %bitcast.840), calls=%async_computation.3 | async-start | bytes 131072 | tf_op jit(solution)/shard_map/all_to_all | solution.py:227
  249.5 9.8 %all-to-all-start.2 = ((f32[128,1,768]{2,1,0:T(1,128)}), f32[128,1,768]{2,1,0:T(1,128)S(1)}, u32[]{:S(2)}, u32[]{:S(2)}) async-start(f32[128,1,768]{2,1,0:T(1,128)} %broadcast_in_dim.133), calls=%async_computation.2 | async-start | bytes 786432 | tf_op jit(solution)/shard_map/all_to_all | solution.py:245
  263.7 4.8 %all-to-all-done.2 = f32[128,1,768]{2,1,0:T(1,128)S(1)} async-done(((f32[128,1,768]{2,1,0:T(1,128)}), f32[128,1,768]{2,1,0:T(1,128)S(1)}, u32[]{:S(2)}, u32[]{:S(2)}) %all-to-all-start.2) | async-done | bytes 393248 | tf_op jit(solution)/shard_map/all_to_all | solution.py:245
  273.7 8.8 %gather_fusion.6 = f32[2048]{0:T(1024)S(1)} fusion(f32[1024]{0:T(1024)S(1)} %reshape_reshape.2, s32[2048]{0:T(1024)S(1)} %copy-done.32), kind=kCustom, calls=%fused_computation.6 | custom fusion | bytes 24576 | tf_op jit(solution)/shard_map/gather | solution.py:229
  282.6 28.5 %fusion = f32[1,2,8,8,8]{4,0,3,2,1:T(1,128)} fusion(f32[2048,1,1,1,1]{0,1,4,3,2:T(1,128)S(1)} %bitcast.857, s32[2,8,8,8]{3,2,1,0:T(8,128)S(1)} %copy-done.88, s32[2048]{0:T(1024)S(1)} %copy-done.98), kind=kOutput, calls=%fused_computation.10 | convolution fusion | flops 27262976 | bytes 24576 | tf_op jit(solution)/shard_map/dot_general | solution.py:230
  312.0 7.3 %all-to-all-start.4 = ((f32[128,1,16]{2,1,0:T(1,128)}), f32[128,1,16]{2,1,0:T(1,128)S(1)}, u32[]{:S(2)}, u32[]{:S(2)}) async-start(f32[128,1,16]{2,1,0:T(1,128)} %copy.373), calls=%async_computation.4 | async-start | bytes 131072 | tf_op jit(solution)/shard_map/all_to_all | solution.py:233
  319.4 6.4 %all-to-all-done.4 = f32[128,1,16]{2,1,0:T(1,128)S(1)} async-done(((f32[128,1,16]{2,1,0:T(1,128)}), f32[128,1,16]{2,1,0:T(1,128)S(1)}, u32[]{:S(2)}, u32[]{:S(2)}) %all-to-all-start.4) | async-done | bytes 8224 | tf_op jit(solution)/shard_map/all_to_all | solution.py:233
  326.8 7.7 %all-to-all-start.5 = ((f32[128,1,768]{2,1,0:T(1,128)}), f32[128,1,768]{2,1,0:T(1,128)S(1)}, u32[]{:S(2)}, u32[]{:S(2)}) async-start(f32[128,1,768]{2,1,0:T(1,128)} %broadcast_in_dim.138), calls=%async_computation.5 | async-start | bytes 786432 | tf_op jit(solution)/shard_map/all_to_all | solution.py:245
  335.5 3.8 fusion.6
  342.6 3.3 constant_dynamic-update-slice_fusion.7
  351.8 7.1 %collective-permute-start.5 = (f32[26,1,2048]{2,1,0:T(1,128)S(1)}, f32[26,1,2048]{2,1,0:T(1,128)S(1)}, u32[]{:S(2)}, u32[]{:S(2)}) collective-permute-start(f32[26,1,2048]{2,1,0:T(1,128)S(1)} %get-tuple-element.102), channel_id=1, source_target_pairs={{8,0},{16,8},{24,16},{32,24},{40,32},{48,40},{56,48},{64,56},{72,6... | collective-permute-start | bytes 638984 | tf_op jit(solution)/shard_map/ppermute | solution.py:58
  376.2 5.0 %collective-permute-done.7 = f32[26,34,32]{1,2,0:T(8,128)} collective-permute-done((f32[26,34,32]{1,2,0:T(8,128)S(1)}, f32[26,34,32]{1,2,0:T(8,128)}, u32[]{:S(2)}, u32[]{:S(2)}) %collective-permute-start.7) | collective-permute-done | bytes 113184 | tf_op jit(solution)/shard_map/ppermute | solution.py:58
  (512 shorter events, 182.7 us)
Async XLA Ops:
  18.4 84.3 %all-to-all-start = ((f32[128,1,16]{2,1,0:T(1,128)}), f32[128,1,16]{2,1,0:T(1,128)}, u32[]{:S(2)}, u32[]{:S(2)}) async-start(f32[128,1,16]{2,1,0:T(1,128)} %bitcast.65), calls=%async_computation | async-start | bytes 131072 | tf_op jit(solution)/shard_map/all_to_all | solution.py:227
  37.1 142.1 %copy-start.12 = (s32[2048]{0:T(1024)}, s32[2048]{0:T(1024)S(1)}, u32[]{:S(2)}) copy-start(s32[2048]{0:T(1024)S(1)} %fusion.393) | copy-start | bytes 24580
  37.1 142.1 %copy-start.15 = (s32[2048]{0:T(1024)}, s32[2048]{0:T(1024)S(1)}, u32[]{:S(2)}) copy-start(s32[2048]{0:T(1024)S(1)} %iota_and_fusion) | copy-start | bytes 24580
  90.1 89.2 %copy-start.34 = (pred[2048]{0:T(1024)(128)(4,1)}, pred[2048]{0:T(1024)(128)(4,1)S(1)}, u32[]{:S(2)}) copy-start(pred[2048]{0:T(1024)(128)(4,1)S(1)} %fusion.396) | copy-start | bytes 6148
  101.8 44.6 %copy-start.100 = (s32[1024,1]{0,1:T(1,128)S(1)}, s32[1024,1]{0,1:T(1,128)}, u32[]{:S(2)}) copy-start(s32[1024,1]{0,1:T(1,128)} %copy-done.99) | copy-start | bytes 12292
  101.8 48.5 %copy-start.102 = (s32[1024]{0:T(1024)S(1)}, s32[1024]{0:T(1024)}, u32[]{:S(2)}) copy-start(s32[1024]{0:T(1024)} %get-tuple-element.47) | copy-start | bytes 12292
  101.8 48.5 %copy-start.104 = (s32[1024]{0:T(1024)S(1)}, s32[1024]{0:T(1024)}, u32[]{:S(2)}) copy-start(s32[1024]{0:T(1024)} %get-tuple-element.114) | copy-start | bytes 12292
  106.6 38.8 %all-to-all-start.1 = ((f32[128,1,16]{2,1,0:T(1,128)}), f32[128,1,16]{2,1,0:T(1,128)S(1)}, u32[]{:S(2)}, u32[]{:S(2)}) async-start(f32[128,1,16]{2,1,0:T(1,128)} %copy.355), calls=%async_computation.1 | async-start | bytes 131072 | tf_op jit(solution)/shard_map/all_to_all | solution.py:233
  158.1 10.8 %collective-permute-start = (f32[26,1,2048]{2,1,0:T(1,128)S(1)}, f32[26,1,2048]{2,1,0:T(1,128)S(1)}, u32[]{:S(2)}, u32[]{:S(2)}) collective-permute-start(f32[26,1,2048]{2,1,0:T(1,128)S(1)} %get-tuple-element.105), channel_id=1, source_target_pairs={{0,8},{8,16},{16,24},{24,32},{32,40},{40,48},{48,56},{56,64},{64,7... | collective-permute-start | bytes 638984 | tf_op jit(solution)/shard_map/ppermute | solution.py:55
  160.2 10.5 %collective-permute-start.1 = (f32[26,1,2048]{2,1,0:T(1,128)S(1)}, f32[26,1,2048]{2,1,0:T(1,128)S(1)}, u32[]{:S(2)}, u32[]{:S(2)}) collective-permute-start(f32[26,1,2048]{2,1,0:T(1,128)S(1)} %get-tuple-element.104), channel_id=1, source_target_pairs={{8,0},{16,8},{24,16},{32,24},{40,32},{48,40},{56,48},{64,56},{72,6... | collective-permute-start | bytes 638984 | tf_op jit(solution)/shard_map/ppermute | solution.py:58
  172.4 12.1 %collective-permute-start.2 = (f32[26,34,32]{1,2,0:T(8,128)S(1)}, f32[26,34,32]{1,2,0:T(8,128)}, u32[]{:S(2)}, u32[]{:S(2)}) collective-permute-start(f32[26,34,32]{1,2,0:T(8,128)S(1)} %copy.403), channel_id=1, source_target_pairs={{0,1},{1,2},{2,3},{3,4},{4,5},{5,6},{6,7},{8,9},{9,10},{10,11},{11... | collective-permute-start | bytes 339464 | tf_op jit(solution)/shard_map/ppermute | solution.py:55
  176.5 14.0 %collective-permute-start.3 = (f32[26,34,32]{1,2,0:T(8,128)}, f32[26,34,32]{1,2,0:T(8,128)S(1)}, u32[]{:S(2)}, u32[]{:S(2)}) collective-permute-start(f32[26,34,32]{1,2,0:T(8,128)} %copy.404), channel_id=1, source_target_pairs={{1,0},{2,1},{3,2},{4,3},{5,4},{6,5},{7,6},{9,8},{10,9},{11,10},{12... | collective-permute-start | bytes 339464 | tf_op jit(solution)/shard_map/ppermute | solution.py:58
  223.4 25.1 %all-to-all-start.3 = ((f32[128,1,16]{2,1,0:T(1,128)}), f32[128,1,16]{2,1,0:T(1,128)}, u32[]{:S(2)}, u32[]{:S(2)}) async-start(f32[128,1,16]{2,1,0:T(1,128)} %bitcast.840), calls=%async_computation.3 | async-start | bytes 131072 | tf_op jit(solution)/shard_map/all_to_all | solution.py:227
  249.5 19.0 %all-to-all-start.2 = ((f32[128,1,768]{2,1,0:T(1,128)}), f32[128,1,768]{2,1,0:T(1,128)S(1)}, u32[]{:S(2)}, u32[]{:S(2)}) async-start(f32[128,1,768]{2,1,0:T(1,128)} %broadcast_in_dim.133), calls=%async_computation.2 | async-start | bytes 786432 | tf_op jit(solution)/shard_map/all_to_all | solution.py:245
  273.7 37.5 %copy-start.81 = (f32[128,16]{0,1:T(8,128)S(1)}, f32[128,16]{0,1:T(8,128)}, u32[]{:S(2)}) copy-start(f32[128,16]{0,1:T(8,128)} %copy-done.80) | copy-start | bytes 24580
  282.5 53.0 %copy-start.101 = (s32[1024,1]{0,1:T(1,128)S(1)}, s32[1024,1]{0,1:T(1,128)}, u32[]{:S(2)}) copy-start(s32[1024,1]{0,1:T(1,128)} %copy-done.99) | copy-start | bytes 12292
  282.5 56.8 %copy-start.103 = (s32[1024]{0:T(1024)S(1)}, s32[1024]{0:T(1024)}, u32[]{:S(2)}) copy-start(s32[1024]{0:T(1024)} %get-tuple-element.47) | copy-start | bytes 12292
  282.5 56.8 %copy-start.105 = (s32[1024]{0:T(1024)S(1)}, s32[1024]{0:T(1024)}, u32[]{:S(2)}) copy-start(s32[1024]{0:T(1024)} %get-tuple-element.114) | copy-start | bytes 12292
  312.0 13.9 %all-to-all-start.4 = ((f32[128,1,16]{2,1,0:T(1,128)}), f32[128,1,16]{2,1,0:T(1,128)S(1)}, u32[]{:S(2)}, u32[]{:S(2)}) async-start(f32[128,1,16]{2,1,0:T(1,128)} %copy.373), calls=%async_computation.4 | async-start | bytes 131072 | tf_op jit(solution)/shard_map/all_to_all | solution.py:233
  326.8 77.9 %all-to-all-start.5 = ((f32[128,1,768]{2,1,0:T(1,128)}), f32[128,1,768]{2,1,0:T(1,128)S(1)}, u32[]{:S(2)}, u32[]{:S(2)}) async-start(f32[128,1,768]{2,1,0:T(1,128)} %broadcast_in_dim.138), calls=%async_computation.5 | async-start | bytes 786432 | tf_op jit(solution)/shard_map/all_to_all | solution.py:245
  349.8 10.8 %collective-permute-start.4 = (f32[26,1,2048]{2,1,0:T(1,128)S(1)}, f32[26,1,2048]{2,1,0:T(1,128)S(1)}, u32[]{:S(2)}, u32[]{:S(2)}) collective-permute-start(f32[26,1,2048]{2,1,0:T(1,128)S(1)} %get-tuple-element.103), channel_id=1, source_target_pairs={{0,8},{8,16},{16,24},{24,32},{32,40},{40,48},{48,56},{56,64},{64,7... | collective-permute-start | bytes 638984 | tf_op jit(solution)/shard_map/ppermute | solution.py:55
  351.8 10.5 %collective-permute-start.5 = (f32[26,1,2048]{2,1,0:T(1,128)S(1)}, f32[26,1,2048]{2,1,0:T(1,128)S(1)}, u32[]{:S(2)}, u32[]{:S(2)}) collective-permute-start(f32[26,1,2048]{2,1,0:T(1,128)S(1)} %get-tuple-element.102), channel_id=1, source_target_pairs={{8,0},{16,8},{24,16},{32,24},{40,32},{48,40},{56,48},{64,56},{72,6... | collective-permute-start | bytes 638984 | tf_op jit(solution)/shard_map/ppermute | solution.py:58
  364.0 12.0 %collective-permute-start.6 = (f32[26,34,32]{1,2,0:T(8,128)S(1)}, f32[26,34,32]{1,2,0:T(8,128)S(1)}, u32[]{:S(2)}, u32[]{:S(2)}) collective-permute-start(f32[26,34,32]{1,2,0:T(8,128)S(1)} %copy.405), channel_id=1, source_target_pairs={{0,1},{1,2},{2,3},{3,4},{4,5},{5,6},{6,7},{8,9},{9,10},{10,11},{11... | collective-permute-start | bytes 339464 | tf_op jit(solution)/shard_map/ppermute | solution.py:55
  367.3 14.0 %collective-permute-start.7 = (f32[26,34,32]{1,2,0:T(8,128)S(1)}, f32[26,34,32]{1,2,0:T(8,128)}, u32[]{:S(2)}, u32[]{:S(2)}) collective-permute-start(f32[26,34,32]{1,2,0:T(8,128)S(1)} %copy.406), channel_id=1, source_target_pairs={{1,0},{2,1},{3,2},{4,3},{5,4},{6,5},{7,6},{9,8},{10,9},{11,10},{12... | collective-permute-start | bytes 339464 | tf_op jit(solution)/shard_map/ppermute | solution.py:58
  (105 other events, 1191.7 us)

commit v2 on v0

v2 whole, which is shorter than its diff:
```python
import functools

import jax
import jax.numpy as jnp
from jax import lax
from jax.experimental import pallas as pl
from jax.experimental.pallas import tpu as pltpu
from jax.sharding import PartitionSpec as P

MESH = pl.DeviceIdType.MESH
F32, BF16, I32 = jnp.float32, jnp.bfloat16, jnp.int32

VELOCITY = [
    (0, 0, 0),
    (1, 0, 0),
    (-1, 0, 0),
    (0, 1, 0),
    (0, -1, 0),
    (0, 0, 1),
    (0, 0, -1),
    (1, 1, 0),
    (-1, -1, 0),
    (1, -1, 0),
    (-1, 1, 0),
    (1, 0, 1),
    (-1, 0, -1),
    (1, 0, -1),
    (-1, 0, 1),
    (0, 1, 1),
    (0, -1, -1),
    (0, 1, -1),
    (0, -1, 1),
]
SIDE_SWAP = [1, 0, 3, 2, 5, 4]
WEIGHTS_HEAT = [0.25] + [0.125] * 6
TAU_FLOW, TAU_HEAT = 0.8, 0.9
BUOYANCY = 0.002
WALL_COEF = 0.1
BRICK_LOSS = 0.5
COND_BASE, COND_SLOPE = 0.04, 0.1
LATENT, MELT, MELT_WIDTH = 2.0, 4.0, 0.5

GX, GY = 16, 8
DEV = GX * GY
CAP = 16
ROWS, TILES, NZ = 32, 16, 32
PITCH = 48
TALL = (TILES + 2) * PITCH
SLOTS = CAP * DEV

ORDER = [9, 1, 11, 13, 20, 7, 3, 15, 17, 22, 10, 2, 12, 14, 21, 8, 4, 16, 18, 23]
ORDER += [0, 5, 6, 19, 24, 25]
PLACE = {pop: at for at, pop in enumerate(ORDER)}
ALL_VELOCITY = VELOCITY + VELOCITY[:7]
XP, YP, XM, YM = ORDER[0:6], ORDER[5:11], ORDER[10:16], ORDER[15:20] + [9]
CORNERS = [(7, 1, 1), (8, -1, -1), (9, 1, -1), (10, -1, 1)]


def iota(shape, dim):
    return lax.broadcasted_iota(I32, shape, dim)


def lane_pick(rows, index):
    return jnp.take_along_axis(rows, index, axis=1, mode="promise_in_bounds")


def tables_kernel(
    owners,
    spots,
    cells,
    id_col,
    links,
    id_row,
    arow_ref,
    lrow_ref,
    lcol_ref,
    oh_cell,
    brow_ref,
    blrow_ref,
    blcol_ref,
    oh_brick,
    pick_ref,
    key,
    val,
    packed,
    by_slot,
):
    x, y = lax.axis_index("gx"), lax.axis_index("gy")
    me = x * GY + y
    square = (128, 128)
    lane = iota(square, 1)
    wide_row, wide_lane = iota((128, 256), 0), iota((128, 256), 1)
    prefix = jnp.where((wide_row <= wide_lane), 1.0, 0.0).astype(BF16)

    def compact(get):
        before = jnp.zeros(square, F32)
        for b in range(8):
            mask, value = get(b)
            counts = jnp.dot(
                jnp.where(mask, 1.0, 0.0).astype(BF16), prefix, preferred_element_type=F32
            )
            key[b] = jnp.where(mask, counts[:, :128] + before, 0.0)
            val[b] = value
            before = before + counts[:, 128:]

        @pl.loop(0, 16)
        def _(c):
            rows = pl.ds(pl.multiple_of(c * 8, 8), 8)
            keys = [key[b, rows, :] for b in range(8)]
            vals = [val[b, rows, :] for b in range(8)]
            at = iota((8, 128), 1)
            out = jnp.zeros((8, 128), F32)
            for r in range(CAP):
                hit = jnp.zeros((8, 128), F32)
                for b in range(8):
                    hit = jnp.where(keys[b] == float(r + 1), vals[b], hit)
                out = jnp.where(at == r, jnp.sum(hit, axis=1, keepdims=True), out)
            packed[rows, :] = out

        return packed[...]

    own_rows = pl.ds(pl.multiple_of(me * 8, 8), 8)
    own_owner = owners[own_rows, :]
    own_cell = cells[own_rows, :].astype(F32) + 1.0
    row_index = iota(square, 0)
    table = compact(
        lambda b: (
            row_index == own_owner[b : b + 1, :],
            jnp.broadcast_to(own_cell[b : b + 1, :], square),
        )
    )

    def split_cell(c):
        c = c.astype(I32) - 1
        live = c >= 0
        a = ((c >> 7) & 15) * ROWS + (c >> 11)
        return jnp.where(live, a, -1), c & 127, live

    a, low, live = split_cell(table)
    lcol_ref[...] = jnp.where(live, low, -1)
    a, low, live = split_cell(jnp.transpose(table)[:CAP, :])
    arow_ref[...] = a
    lrow_ref[...] = jnp.where(live, low, 0)
    for r in range(CAP):
        for q in range(4):
            part = iota(square, 0) + q * 128 == a[r : r + 1, :]
            oh_cell[q * 128 : (q + 1) * 128, r * 128 : (r + 1) * 128] = jnp.where(
                part, 1.0, 0.0
            ).astype(BF16)

    def from_device(b):
        rows = pl.ds(b, 128, stride=8)
        return owners[rows, :] == me, spots[rows, :].astype(F32) + 1.0

    table = compact(from_device)

    def split_spot(c):
        c = c.astype(I32) - 1
        live = c >= 0
        return jnp.where(live, c >> 6, -1), c & 63, live

    a, low, live = split_spot(table)
    blcol_ref[...] = jnp.where(live, low, -1)
    a, low, live = split_spot(jnp.transpose(table)[:CAP, :])
    brow_ref[...] = a
    blrow_ref[...] = jnp.where(live, low, 0)
    for r in range(CAP):
        part = iota((16, 128), 0) == a[r : r + 1, :]
        oh_brick[:, r * 128 : (r + 1) * 128] = jnp.where(part, 1.0, 0.0).astype(BF16)

    chosen = jnp.where(id_col[...] == iota((256, 256), 1), 1.0, 0.0).astype(BF16)
    by_slot[...] = jnp.dot(
        chosen, links[...].astype(F32).astype(BF16), preferred_element_type=F32
    )
    at = iota((16, 128), 1)
    to_x = iota((16, 128), 0)
    ids = id_row[...].astype(F32)
    for b in range(2):
        named = by_slot[pl.ds(2 * y + b, 16, stride=16), :]
        for s in range(6):
            j = s * 2 + b
            n = named[:, s : s + 1]
            side = (at & 15) >> 1
            remote = (n == ids) & (side == SIDE_SWAP[s])
            own = (n < 0.0) & (to_x == x) & (at == y * 16 + j)
            pick_ref[j * 16 : (j + 1) * 16, :] = jnp.where(remote | own, 1.0, 0.0).astype(BF16)


def collide(f, g, solid):
    pairs = [(1, 2), (3, 4), (5, 6), (7, 8), (9, 10), (11, 12), (13, 14), (15, 16), (17, 18)]
    total = {a: f[a] + f[b] for a, b in pairs}
    diff = {a: f[a] - f[b] for a, b in pairs}
    density = f[0] + (
        (total[1] + total[3])
        + (total[5] + total[7])
        + (total[9] + total[11])
        + (total[13] + total[15])
        + total[17]
    )
    inverse = 1.0 / density
    ux = (diff[1] + diff[7] + diff[9] + diff[11] + diff[13]) * inverse
    uy = (diff[3] + diff[7] - diff[9] + diff[15] + diff[17]) * inverse
    uz = (diff[5] + diff[11] - diff[13] + diff[15] - diff[17]) * inverse
    temp = g[0] + ((g[1] + g[2]) + (g[3] + g[4]) + (g[5] + g[6]))
    sz = uz + (TAU_FLOW * BUOYANCY) * (temp - 1.0) * inverse
    base = 1.0 - 1.5 * (ux * ux + uy * uy + sz * sz)
    keep = 1.0 - 1.0 / TAU_FLOW
    along_of = {1: ux, 3: uy, 5: sz, 7: ux + uy, 9: ux - uy}
    along_of.update({11: ux + sz, 13: ux - sz, 15: uy + sz, 17: uy - sz})
    out_f = [None] * 19
    k0 = density * (1.0 / 3.0 / TAU_FLOW)
    out_f[0] = jnp.where(solid, f[0], keep * f[0] + k0 * base)
    scale = {1: density * (1.0 / 18.0 / TAU_FLOW), 7: density * (1.0 / 36.0 / TAU_FLOW)}
    for a, b in pairs:
        k = scale[1 if a < 7 else 7]
        along = along_of[a]
        even = k * (base + 4.5 * (along * along))
        odd = (3.0 * k) * along
        out_f[a] = jnp.where(solid, f[b], (even + odd) + keep * f[a])
        out_f[b] = jnp.where(solid, f[a], (even - odd) + keep * f[b])
    keep = 1.0 - 1.0 / TAU_HEAT
    out_g = [None] * 7
    out_g[0] = jnp.where(solid, g[0], keep * g[0] + (0.25 / TAU_HEAT) * temp)
    k = (0.125 / TAU_HEAT) * temp
    for a, u in ((1, ux), (3, uy), (5, uz)):
        odd = (4.0 * k) * u
        out_g[a] = jnp.where(solid, g[a + 1], (k + odd) + keep * g[a])
        out_g[a + 1] = jnp.where(solid, g[a], (k - odd) + keep * g[a + 1])
    return out_f, out_g


def pull(store, pop, t, xb, lane):
    cx, cy, cz = ALL_VELOCITY[pop]
    at = PLACE[pop]

    def tile(step):
        return store[at, pl.ds((t + 1 + step) * PITCH + 8 + xb * 8 - cx, 8), :]

    here = tile(0)
    if cy == 1:
        here = jnp.where(lane >= 128 - NZ, tile(-1), here)
    if cy == -1:
        here = jnp.where(lane < NZ, tile(1), here)
    shift = (cy * NZ + cz) % 128
    if shift:
        here = pltpu.roll(here, shift, 1)
    if cz == 1:
        here = jnp.where(lane % NZ == 0, 0.0, here)
    if cz == -1:
        here = jnp.where(lane % NZ == NZ - 1, 0.0, here)
    return here


def own_rows(t, xb):
    return pl.ds((t + 1) * PITCH + 8 + xb * 8, 8)


def natural(t, xb):
    return pl.ds(xb * 8, 8), pl.ds(pl.multiple_of(t * 128, 128), 128)


def temp_rows(t, xb):
    return pl.ds(pl.multiple_of(t * ROWS + xb * 8, 8), 8)


def halves(value):
    high = value.astype(BF16)
    return high, (value - high.astype(F32)).astype(BF16)


def scatter(onehot, columns, flux, spread):
    high, low = halves(flux)
    high, low = high.astype(F32), low.astype(F32)
    at = iota((128, 128), 1)
    for r in range(CAP):
        hit = at == columns[:, r : r + 1]
        rows = slice(r * 128, (r + 1) * 128)
        spread[rows, 0:128] = jnp.where(hit, high[:, r : r + 1], 0.0).astype(BF16)
        spread[rows, 128:256] = jnp.where(hit, low[:, r : r + 1], 0.0).astype(BF16)
    both = jnp.dot(onehot[...], spread[...], preferred_element_type=F32)
    return both[:, :128] + both[:, 128:]


def brick_lookup(brick, brow, blrow):
    out = jnp.zeros((CAP, 128), F32)
    for a in range(16):
        row = jnp.broadcast_to(brick[a : a + 1, :], (CAP, 128))
        out = jnp.where(brow == a, lane_pick(row, blrow), out)
    return out


def store_faces(brick, faces):
    at, row = iota((16, 128), 1), iota((16, 128), 0)
    mine = ((at >> 3) & 7) == (row & 7)
    wanted = {
        2: at & 7,
        3: 56 + (at & 7),
        4: (at & 7) * 8,
        5: (at & 7) * 8 + 7,
    }
    faces[12:16, :] = jnp.zeros((4, 128), F32)
    for b in range(2):
        faces[b : b + 1, :] = brick[b * 8 : b * 8 + 1, :]
        faces[2 + b : 3 + b, :] = brick[b * 8 + 7 : b * 8 + 8, :]
    for s, index in wanted.items():
        got = jnp.where(mine, lane_pick(brick, index), 0.0)
        for b in range(2):
            faces[s * 2 + b : s * 2 + b + 1, :] = jnp.sum(
                got[b * 8 : b * 8 + 8], axis=0, keepdims=True
            )


def conduct(brick, ghost, loss):
    at, row = iota((16, 128), 1), iota((16, 128), 0)
    x = row & 7

    def ghost_rows(s):
        return jnp.where(row < 8, ghost[s * 2 : s * 2 + 1, :], ghost[s * 2 + 1 : s * 2 + 2, :])

    over_z = x * 8 + (at & 7)
    over_y = x * 8 + ((at >> 3) & 7)
    beside = [
        jnp.where(x == 0, ghost_rows(0), pltpu.roll(brick, 1, 0)),
        jnp.where(x == 7, ghost_rows(1), pltpu.roll(brick, 15, 0)),
        jnp.where(at < 8, lane_pick(ghost_rows(2), over_z), pltpu.roll(brick, 8, 1)),
        jnp.where(at >= 56, lane_pick(ghost_rows(3), over_z), pltpu.roll(brick, 120, 1)),
        jnp.where((at & 7) == 0, lane_pick(ghost_rows(4), over_y), pltpu.roll(brick, 1, 1)),
        jnp.where((at & 7) == 7, lane_pick(ghost_rows(5), over_y), pltpu.roll(brick, 127, 1)),
    ]
    here = COND_BASE * (1.0 + COND_SLOPE * brick)
    spread = jnp.zeros((16, 128), F32)
    for other in beside:
        spread += 0.5 * (here + COND_BASE * (1.0 + COND_SLOPE * other)) * (other - brick)
    phase = 1.0 / (1.0 + jnp.exp(-(brick - MELT) / MELT_WIDTH))
    capacity = 1.0 + LATENT * phase * (1.0 - phase) / MELT_WIDTH
    return jnp.where(at < 64, brick + (spread - BRICK_LOSS * loss) / capacity, 0.0)


def steps_kernel(
    flow,
    heat,
    solid,
    brick_in,
    arow_ref,
    lrow_ref,
    lcol_ref,
    oh_cell,
    brow_ref,
    blrow_ref,
    blcol_ref,
    oh_brick,
    pick_ref,
    second,
    brick_out,
    first,
    temps,
    gain,
    spread,
    msg,
    faces,
    s1,
    r1,
    s2,
    r2,
    xs,
    xr,
    ys,
    yr,
    cs,
    cr,
    s1_send,
    s1_recv,
    s2_send,
    s2_recv,
    halo_send,
    halo_recv,
):
    x, y = lax.axis_index("gx"), lax.axis_index("gy")

    def xn(k):
        return lax.rem(x + (k + GX), GX)

    def yn(k):
        return lax.rem(y + (k + GY), GY)

    barrier = pltpu.get_barrier_semaphore()
    peers = [(x, yn(k)) for k in range(1, GY)] + [(xn(k), y) for k in range(1, GX)]
    peers += [(xn(a), yn(b)) for a in (-1, 1) for b in (-1, 1)]
    for peer in peers:
        pl.semaphore_signal(barrier, inc=1, device_id=peer, device_id_type=MESH)

    lane = iota((8, 128), 1)

    def look_up_faces(brick):
        a, low = arow_ref[...], lrow_ref[...]

        def body(i, out):
            for u in range(8):
                row = i * 8 + u
                line = jnp.broadcast_to(temps[pl.ds(row, 1), :], (CAP, 128))
                out = jnp.where(a == row, lane_pick(line, low), out)
            return out

        found = lax.fori_loop(0, TILES * ROWS // 8, body, jnp.zeros((CAP, 128), F32))
        asked = brick_lookup(brick, brow_ref[...], blrow_ref[...])
        rest = jnp.zeros((128 - 2 * CAP, 128), F32)
        msg[...] = jnp.transpose(jnp.concatenate([found, asked, rest], axis=0))
        store_faces(brick, faces)

    def phase_one(step):
        for k in range(GY):
            s1[step, k * 32 : k * 32 + 16, :] = msg[pl.ds(k, 16, stride=8), :]
            s1[step, k * 32 + 16 : k * 32 + 32, :] = faces[...]
        copies = []
        for k in range(1, GY):
            to = yn(k)
            copies.append(
                pltpu.make_async_remote_copy(
                    src_ref=s1.at[step, pl.ds(pl.multiple_of(to * 32, 32), 32), :],
                    dst_ref=r1.at[step, pl.ds(pl.multiple_of(y * 32, 32), 32), :],
                    send_sem=s1_send.at[step, k],
                    recv_sem=s1_recv.at[step, y],
                    device_id=(x, to),
                    device_id_type=MESH,
                )
            )
            copies[-1].start()
        own = pl.ds(pl.multiple_of(y * 32, 32), 32)
        r1[step, own, :] = s1[step, own, :]
        return copies

    def end_one(step, copies):
        for k in range(1, GY):
            copies[k - 1].wait_send()
            came = yn(k)
            rows = pl.ds(pl.multiple_of(came * 32, 32), 32)
            pltpu.make_async_remote_copy(
                src_ref=s1.at[step, rows, :],
                dst_ref=r1.at[step, rows, :],
                send_sem=s1_send.at[step, k],
                recv_sem=s1_recv.at[step, came],
                device_id=(x, came),
                device_id_type=MESH,
            ).wait_recv()

    def phase_two(step):
        every = jnp.concatenate(
            [r1[step, k * 32 + 16 : k * 32 + 32, :] for k in range(GY)], axis=0
        )
        high = every.astype(BF16)
        low = every - high.astype(F32)
        at = iota((128, 128), 1)
        both = jnp.where(at < 64, high.astype(F32), pltpu.roll(low, 64, 1)).astype(BF16)
        picked = jnp.dot(pick_ref[...], both, preferred_element_type=F32)
        picked = picked + pltpu.roll(picked, 64, 1)
        for j in range(12):
            s2[step, pl.ds(8 + j, 16, stride=24), :] = picked[j * 16 : (j + 1) * 16, :]
        for j in range(12, 16):
            s2[step, pl.ds(8 + j, 16, stride=24), :] = jnp.zeros((16, 128), F32)
        for k in range(GX):
            s2[step, k * 24 : k * 24 + 8, :] = r1[step, pl.ds(k, 8, stride=32), :]
        copies = []
        for k in range(1, GX):
            to = xn(k)
            copies.append(
                pltpu.make_async_remote_copy(
                    src_ref=s2.at[step, pl.ds(pl.multiple_of(to * 24, 8), 24), :],
                    dst_ref=r2.at[step, pl.ds(pl.multiple_of(x * 24, 8), 24), :],
                    send_sem=s2_send.at[step, k],
                    recv_sem=s2_recv.at[step, x],
                    device_id=(to, y),
                    device_id_type=MESH,
                )
            )
            copies[-1].start()
        own = pl.ds(pl.multiple_of(x * 24, 8), 24)
        r2[step, own, :] = s2[step, own, :]
        return copies

    def end_two(step, copies):
        for k in range(1, GX):
            copies[k - 1].wait_send()
            came = xn(k)
            rows = pl.ds(pl.multiple_of(came * 24, 8), 24)
            pltpu.make_async_remote_copy(
                src_ref=s2.at[step, rows, :],
                dst_ref=r2.at[step, rows, :],
                send_sem=s2_send.at[step, k],
                recv_sem=s2_recv.at[step, came],
                device_id=(came, y),
                device_id_type=MESH,
            ).wait_recv()

    def couple(step, brick, store):
        came = jnp.concatenate([r2[step, k * 24 : k * 24 + 8, :] for k in range(GX)], axis=0)
        ghost = r2[step, 8:24, :]
        for k in range(1, GX):
            ghost = ghost + r2[step, k * 24 + 8 : k * 24 + 24, :]
        mine = msg[...]
        to_fluid = WALL_COEF * (pltpu.roll(came, 128 - CAP, 1) - mine)
        gain[...] = scatter(oh_cell, lcol_ref[...], to_fluid, spread)
        lost = WALL_COEF * (pltpu.roll(mine, 128 - CAP, 1) - came)
        loss = scatter(oh_brick, blcol_ref[...], lost, spread)

        @pl.loop(0, TILES)
        def _(t):
            for xb in range(4):
                more = gain[temp_rows(t, xb), :]
                for j in range(7):
                    rows = own_rows(t, xb)
                    at = PLACE[19 + j]
                    store[at, rows, :] = store[at, rows, :] + WEIGHTS_HEAT[j] * more

        return conduct(brick, ghost, loss)

    def send_halo(step, store):
        for side, (group, row) in enumerate(((XP, 39), (XM, 8))):
            for k, pop in enumerate(group):
                xs[step, side, k * 16 : (k + 1) * 16, :] = store[
                    PLACE[pop], pl.ds(PITCH + row, 16, stride=PITCH), :
                ]
        wide = iota((32, 128), 1)
        for side, (group, t, lanes) in enumerate(((YP, TILES, 96), (YM, 1, 0))):
            parts = []
            for k, pop in enumerate(group):
                part = store[PLACE[pop], t * PITCH + 8 : t * PITCH + 40, :]
                turn = ((k % 4) * 32 - lanes) % 128
                parts.append(pltpu.roll(part, turn, 1) if turn else part)
            for q in range(2):
                tile = parts[q * 4]
                for k in range(1, len(parts[q * 4 : q * 4 + 4])):
                    tile = jnp.where(wide >= k * 32, parts[q * 4 + k], tile)
                ys[step, side, q * 32 : (q + 1) * 32, :] = tile
        for c, (pop, dx, dy) in enumerate(CORNERS):
            t, row = (TILES if dy == 1 else 1), (39 if dx == 1 else 8)
            cs[step, c] = jnp.broadcast_to(
                store[PLACE[pop], t * PITCH + row : t * PITCH + row + 1, :], (8, 128)
            )
        plan = [(xs.at[step, 0], xr.at[step, 0], (xn(1), y))]
        plan.append((xs.at[step, 1], xr.at[step, 1], (xn(-1), y)))
        plan.append((ys.at[step, 0], yr.at[step, 0], (x, yn(1))))
        plan.append((ys.at[step, 1], yr.at[step, 1], (x, yn(-1))))
        for c, (_, dx, dy) in enumerate(CORNERS):
            plan.append((cs.at[step, c], cr.at[step, c], (xn(dx), yn(dy))))
        copies = []
        for n, (source, target, peer) in enumerate(plan):
            copies.append(
                pltpu.make_async_remote_copy(
                    src_ref=source,
                    dst_ref=target,
                    send_sem=halo_send.at[step, n],
                    recv_sem=halo_recv.at[step, n],
                    device_id=peer,
                    device_id_type=MESH,
                )
            )
            copies[-1].start()
        return copies

    def end_halo(step, store, copies):
        for copy in copies:
            copy.wait()
        inside = {(1, 0): x > 0, (-1, 0): x < GX - 1, (0, 1): y > 0, (0, -1): y < GY - 1}
        for side, (group, row, way) in enumerate(((XP, 7, 1), (XM, 40, -1))):
            for k, pop in enumerate(group):
                store[PLACE[pop], pl.ds(PITCH + row, 16, stride=PITCH), :] = jnp.where(
                    inside[(way, 0)], xr[step, side, k * 16 : (k + 1) * 16, :], 0.0
                )
        for side, (group, t, lanes, way) in enumerate(((YP, 0, 96, 1), (YM, TILES + 1, 0, -1))):
            for k, pop in enumerate(group):
                part = yr[step, side, (k // 4) * 32 : (k // 4 + 1) * 32, :]
                turn = (lanes - (k % 4) * 32) % 128
                part = pltpu.roll(part, turn, 1) if turn else part
                store[PLACE[pop], t * PITCH + 8 : t * PITCH + 40, :] = jnp.where(
                    inside[(0, way)], part, 0.0
                )
        for c, (pop, dx, dy) in enumerate(CORNERS):
            t, row = (0 if dy == 1 else TILES + 1), (7 if dx == 1 else 40)
            known = inside[(dx, 0)] & inside[(0, dy)]
            store[PLACE[pop], t * PITCH + row : t * PITCH + row + 1, :] = jnp.where(
                known, cr[step, c, 0:1, :], 0.0
            )

    def store_relaxed(store, t, xb, f, g):
        out_f, out_g = collide(f, g, solid[natural(t, xb)] == 1)
        rows = own_rows(t, xb)
        for i in range(19):
            store[PLACE[i], rows, :] = out_f[i]
        for j in range(7):
            store[PLACE[19 + j], rows, :] = out_g[j]

    @pl.loop(0, TILES)
    def _(t):
        for xb in range(4):
            rows, lanes = natural(t, xb)
            g = [heat[j, rows, lanes] for j in range(7)]
            temps[temp_rows(t, xb), :] = g[0] + (
                (g[1] + g[2]) + (g[3] + g[4]) + (g[5] + g[6])
            )

    brick = brick_in[...]
    look_up_faces(brick)
    pl.semaphore_wait(barrier, len(peers))
    copies = phase_one(0)

    def relax_first(low, high):
        @pl.loop(low * 4, high * 4)
        def _(n):
            t, xb = n // 4, n % 4
            rows, lanes = pl.ds(pl.multiple_of(xb * 8, 8), 8), natural(t, 0)[1]
            f = [flow[i, rows, lanes] for i in range(19)]
            g = [heat[j, rows, lanes] for j in range(7)]
            store_relaxed(first, t, xb, f, g)

    relax_first(0, TILES // 2)
    end_one(0, copies)
    copies = phase_two(0)
    relax_first(TILES // 2, TILES)
    end_two(0, copies)
    brick = couple(0, brick, first)
    copies = send_halo(0, first)
    brick_out[...] = brick
    end_halo(0, first, copies)

    @pl.loop(0, TILES)
    def _(t):
        for xb in range(4):
            g = [pull(first, 19 + j, t, xb, lane) for j in range(7)]
            temps[temp_rows(t, xb), :] = g[0] + (
                (g[1] + g[2]) + (g[3] + g[4]) + (g[5] + g[6])
            )

    brick = brick_out[...]
    look_up_faces(brick)
    copies = phase_one(1)

    def relax_second(low, high):
        @pl.loop(low * 4, high * 4)
        def _(n):
            t, xb = n // 4, n % 4
            f = [pull(first, i, t, xb, lane) for i in range(19)]
            g = [pull(first, 19 + j, t, xb, lane) for j in range(7)]
            store_relaxed(second, t, xb, f, g)

    relax_second(0, TILES // 2)
    end_one(1, copies)
    copies = phase_two(1)
    relax_second(TILES // 2, TILES)
    end_two(1, copies)
    brick = couple(1, brick, second)
    copies = send_halo(1, second)
    brick_out[...] = brick
    end_halo(1, second, copies)


def spread_kernel(second, flow_out, heat_out, flow_now, heat_now, sems):
    lane = iota((8, 128), 1)
    copies = []
    for pop in range(26):
        now, out, at = (flow_now, flow_out, pop) if pop < 19 else (heat_now, heat_out, pop - 19)

        @pl.loop(0, TILES)
        def _(t):
            for xb in range(4):
                rows, lanes = natural(t, xb)
                now[at, rows, lanes] = pull(second, pop, t, xb, lane)

        copies.append(pltpu.make_async_copy(now.at[at], out.at[at], sems.at[pop]))
        copies[-1].start()
    for copy in copies:
        copy.wait()


def vmem(count):
    return [pl.BlockSpec(memory_space=pltpu.VMEM)] * count


def body(
    flow_pops,
    heat_pops,
    solid_flag,
    brick_temp,
    brick_ids,
    brick_links,
    face_cell,
    face_owner,
    face_spot,
):
    gx = lax.axis_index("gx")
    shape = jax.ShapeDtypeStruct
    ids = lax.dynamic_slice_in_dim(brick_ids, gx * GY * 2, GY * 2).reshape(GY, 1, 2)
    id_row = jnp.broadcast_to(ids, (GY, 8, 2)).reshape(1, 128)
    tables = pl.pallas_call(
        tables_kernel,
        out_shape=[
            shape((CAP, 128), I32),
            shape((CAP, 128), I32),
            shape((128, 128), I32),
            shape((TILES * ROWS, SLOTS), BF16),
            shape((CAP, 128), I32),
            shape((CAP, 128), I32),
            shape((128, 128), I32),
            shape((16, SLOTS), BF16),
            shape((192, 128), BF16),
        ],
        in_specs=vmem(6),
        out_specs=vmem(9),
        scratch_shapes=[
            pltpu.VMEM((8, 128, 128), F32),
            pltpu.VMEM((8, 128, 128), F32),
            pltpu.VMEM((128, 128), F32),
            pltpu.VMEM((256, 128), F32),
        ],
        compiler_params=pltpu.CompilerParams(vmem_limit_bytes=16 << 20),
    )(
        face_owner.reshape(1024, 128),
        face_spot.reshape(1024, 128),
        face_cell.reshape(1024, 128),
        brick_ids.reshape(256, 1),
        jnp.pad(brick_links, ((0, 0), (0, 122))),
        id_row,
    )
    brick = jnp.pad(brick_temp.reshape(16, 64), ((0, 0), (0, 64)))
    dma = pltpu.SemaphoreType.DMA
    second, brick = pl.pallas_call(
        steps_kernel,
        out_shape=[pltpu.VMEM((26, TALL, 128), F32), shape((16, 128), F32)],
        in_specs=vmem(13),
        out_specs=vmem(2),
        scratch_shapes=[
            pltpu.VMEM((26, TALL, 128), F32),
            pltpu.VMEM((TILES * ROWS, 128), F32),
            pltpu.VMEM((TILES * ROWS, 128), F32),
            pltpu.VMEM((SLOTS, 256), BF16),
            pltpu.VMEM((128, 128), F32),
            pltpu.VMEM((16, 128), F32),
            pltpu.VMEM((2, GY * 32, 128), F32),
            pltpu.VMEM((2, GY * 32, 128), F32),
            pltpu.VMEM((2, GX * 24, 128), F32),
            pltpu.VMEM((2, GX * 24, 128), F32),
            pltpu.VMEM((2, 2, 96, 128), F32),
            pltpu.VMEM((2, 2, 96, 128), F32),
            pltpu.VMEM((2, 2, 64, 128), F32),
            pltpu.VMEM((2, 2, 64, 128), F32),
            pltpu.VMEM((2, 4, 8, 128), F32),
            pltpu.VMEM((2, 4, 8, 128), F32),
            dma((2, GY)),
            dma((2, GY)),
            dma((2, GX)),
            dma((2, GX)),
            dma((2, 8)),
            dma((2, 8)),
        ],
        compiler_params=pltpu.CompilerParams(
            collective_id=0, has_side_effects=True, vmem_limit_bytes=40 << 20
        ),
    )(flow_pops, heat_pops, solid_flag, brick, *tables)
    flow, heat = pl.pallas_call(
        spread_kernel,
        out_shape=[shape(flow_pops.shape, F32), shape(heat_pops.shape, F32)],
        in_specs=vmem(1),
        out_specs=[pl.BlockSpec(memory_space=pl.ANY)] * 2,
        scratch_shapes=[
            pltpu.VMEM(flow_pops.shape, F32),
            pltpu.VMEM(heat_pops.shape, F32),
            dma((26,)),
        ],
        compiler_params=pltpu.CompilerParams(vmem_limit_bytes=24 << 20),
    )(second)
    return flow, heat, brick[:, :64].reshape(brick_temp.shape)


def solution(mesh):
    return jax.shard_map(
        body,
        mesh=mesh,
        in_specs=(
            P(None, "gx", "gy"),
            P(None, "gx", "gy"),
            P("gx", "gy"),
            P(("gx", "gy"), None),
            P(),
            P(),
            P(),
            P(),
            P(),
        ),
        out_specs=(P(None, "gx", "gy"), P(None, "gx", "gy"), P(("gx", "gy"), None)),
        check_vma=False,
    )
```

time: 1950 us -> 99 us (0.05)
  local copies, waits for them, and re-layouts: 1040 us -> 10.9 us
  blocking collectives: 615 us -> 0 us
  other arithmetic: 90.6 us -> 0 us
  Pallas kernels: 0 us -> 85.9 us
  matrix products: 76.7 us -> 0 us
  starting transfers between devices: 75.6 us -> 0 us
  waiting for transfers between devices: 29.3 us -> 0 us
    unnamed x250 -> x13, local copies, waits for them, and re-layouts: 966 us -> 7.71 us
    all_gather x2 -> x0, blocking collectives: 615 us -> none  [body(): lax.all_gather(faces_here.reshape(bricks_here, 6 * BE * BE), ('gx', 'gy')...]
    pallas_call x0 -> x3, Pallas kernels: none -> 85.9 us  [the longest x1 56 us: body(): pl.pallas_call(steps_kernel, out_shape=[pltpu.VMEM((26, TALL, 128), F32),...]
    dot_general x8 -> x0, matrix products: 76.7 us -> none  [the longest x2 55.7 us: body(): jnp.dot(wall_flux.reshape(-1), spot_table, precision=EXACT)]
    unnamed x73 -> x0, other arithmetic: 63.3 us -> none
    all_to_all x4 -> x0, starting transfers between devices: 56 us -> none  [the longest x2 30.7 us: body(): lax.all_to_all(wall_flux, ('gx', 'gy'), split_axis=0, concat_axis=0, tile...]
    gather x14 -> x0, local copies, waits for them, and re-layouts: 38.8 us -> none  [the longest x4 17.9 us: body(): wall_flux = WALL_COEF * (flat_brick[recv_spot] - arrived) * recv_live]
    ppermute x8 -> x0, waiting for transfers between devices: 20.7 us -> none  [the longest x4 17.7 us: with_halo(): lax.ppermute(lax.slice_in_dim(block, 0, width, axis=dim), axis, backward)]
  transfers between devices with their start and end apart: 12 -> 0, of which waited for: 8 -> 0; matrix products, arithmetic and copies ran while one was open for 54% -> 0% of each run, Pallas kernels for 0% -> 0%
where the time goes in v2:
time: 99 us; the launch traced here: 97.6 us
  Pallas kernels  85.9 us (87%)
  local copies, waits for them, and re-layouts  10.9 us (11%)
    pallas_call x1, Pallas kernels, body(): pl.pallas_call(steps_kernel, out_shape=[pltpu.VMEM((26, TALL, 128), F32),...  56 us
    pallas_call x1, Pallas kernels, body(): pl.pallas_call(spread_kernel, out_shape=[shape(flow_pops.shape, F32), sha...  24.5 us
    unnamed x13, local copies, waits for them, and re-layouts  7.71 us
    pallas_call x1, Pallas kernels, body(): pl.pallas_call(tables_kernel, out_shape=[shape((CAP, 128), I32), shape((C...  5.41 us

profile of v2, /device:TPU:1, one launch (start us, length us, event | category | flops | bytes accessed | tf_op | source)
XLA Modules:
  0.0 97.6 jit_solution(18218404487272617760)
XLA Ops:
  0.6 0.8 dynamic_slice.3
  1.4 0.1 broadcast_in_dim.7
  1.5 0.8 reshape.29
  2.2 0.1 reshape.34.id_row
  2.4 0.8 copy.13
  3.2 0.8 copy.14.id_col
  4.1 0.0 copy-start.2
  4.1 1.0 %copy-done.2 = s32[131072,1]{0,1:T(1,128)S(1)} copy-done((s32[131072,1]{0,1:T(1,128)S(1)}, s32[131072,1]{0,1:T(1,128)}, u32[]{:S(2)}) %copy-start.2) | copy-done | bytes 524312
  5.1 0.0 copy-start.3
  5.1 1.0 %copy-done.3 = s32[131072]{0:T(1024)S(1)} copy-done((s32[131072]{0:T(1024)S(1)}, s32[131072]{0:T(1024)}, u32[]{:S(2)}) %copy-start.3) | copy-done | bytes 524312
  6.2 0.0 copy-start.4
  6.2 1.0 %copy-done.4 = s32[131072]{0:T(1024)S(1)} copy-done((s32[131072]{0:T(1024)S(1)}, s32[131072]{0:T(1024)}, u32[]{:S(2)}) %copy-start.4) | copy-done | bytes 524312
  7.2 5.4 %shard_map.112 = (s32[16,128]{1,0:T(8,128)S(1)}, s32[16,128]{1,0:T(8,128)S(1)}, s32[128,128]{1,0:T(8,128)S(1)}, bf16[512,2048]{1,0:T(8,128)(2,1)S(1)}, s32[16,12...) custom-call(s32[1024,128]{1,0:T(8,128)S(1)} %bitcast.5, ...), custom_call_target="tpu_custom_call" | custom-call | tf_op jit(solution)/shard_map/pallas_call | solution.py:693
  12.6 0.0 copy-start
  12.6 1.3 %copy-done = bf16[512,2048]{1,0:T(8,128)(2,1)} copy-done((bf16[512,2048]{1,0:T(8,128)(2,1)}, bf16[512,2048]{1,0:T(8,128)(2,1)S(1)}, u32[]{:S(2)}) %copy-start) | copy-done | bytes 2097176
  13.9 0.0 copy-start.1
  13.9 1.5 %copy-done.1 = f32[7,32,2048]{2,1,0:T(8,128)S(1)} copy-done((f32[7,32,2048]{2,1,0:T(8,128)S(1)}, f32[7,32,2048]{2,1,0:T(8,128)}, u32[]{:S(2)}) %copy-start.1) | copy-done | bytes 1835032
  15.4 0.0 copy-start.5
  15.4 0.9 copy-done.5
  16.4 56.0 %shard_map.113 = (f32[26,864,128]{2,1,0:T(8,128)S(1)}, f32[16,128]{1,0:T(8,128)S(1)}) custom-call(f32[19,32,2048]{2,1,0:T(8,128)} %flow.1, f32[7,32,2048]{2,1,0:T(8,128)S(1)} %copy-done.1, s32[32,2048]{1,0:T(8,128)S(1)} %copy-done.5, f32[16,128]{1,0:T(8,128)S(1)} %pad.8.brick_in, s32[16,128]{1,0:T(8,128)S(1)} %get-tuple-element.16.arow_ref, ...), custom_call_target="tpu_custom_call" | custom-call | tf_op jit(solution)/shard_map/pallas_call | solution.py:725
  72.4 24.5 %shard_map.114 = (f32[19,32,2048]{2,1,0:T(8,128)}, f32[7,32,2048]{2,1,0:T(8,128)}) custom-call(f32[26,864,128]{2,1,0:T(8,128)S(1)} %get-tuple-element.25.second), custom_call_target="tpu_custom_call" | custom-call | tf_op jit(solution)/shard_map/pallas_call | solution.py:758
  96.9 0.7 reshape.35
  (3 shorter events, 0.0 us)
Async XLA Ops:
  4.1 1.0 %copy-start.2 = (s32[131072,1]{0,1:T(1,128)S(1)}, s32[131072,1]{0,1:T(1,128)}, u32[]{:S(2)}) copy-start(s32[131072,1]{0,1:T(1,128)} %param.16) | copy-start | bytes 1572868
  5.1 1.0 %copy-start.3 = (s32[131072]{0:T(1024)S(1)}, s32[131072]{0:T(1024)}, u32[]{:S(2)}) copy-start(s32[131072]{0:T(1024)} %param.17) | copy-start | bytes 1572868
  6.2 1.0 %copy-start.4 = (s32[131072]{0:T(1024)S(1)}, s32[131072]{0:T(1024)}, u32[]{:S(2)}) copy-start(s32[131072]{0:T(1024)} %param.15) | copy-start | bytes 1572868
  12.6 1.3 %copy-start = (bf16[512,2048]{1,0:T(8,128)(2,1)}, bf16[512,2048]{1,0:T(8,128)(2,1)S(1)}, u32[]{:S(2)}) copy-start(bf16[512,2048]{1,0:T(8,128)(2,1)S(1)} %get-tuple-element.19.oh_cell) | copy-start | bytes 6291460
  13.9 1.5 %copy-start.1 = (f32[7,32,2048]{2,1,0:T(8,128)S(1)}, f32[7,32,2048]{2,1,0:T(8,128)}, u32[]{:S(2)}) copy-start(f32[7,32,2048]{2,1,0:T(8,128)} %heat.1) | copy-start | bytes 5505028
  15.4 0.9 copy-start.5

commit v3 on v2

v3 whole, which is shorter than its diff:
```python
import functools

import jax
import jax.numpy as jnp
from jax import lax
from jax.experimental import pallas as pl
from jax.experimental.pallas import tpu as pltpu
from jax.sharding import PartitionSpec as P

MESH = pl.DeviceIdType.MESH
F32, BF16, I32 = jnp.float32, jnp.bfloat16, jnp.int32

VELOCITY = [
    (0, 0, 0),
    (1, 0, 0),
    (-1, 0, 0),
    (0, 1, 0),
    (0, -1, 0),
    (0, 0, 1),
    (0, 0, -1),
    (1, 1, 0),
    (-1, -1, 0),
    (1, -1, 0),
    (-1, 1, 0),
    (1, 0, 1),
    (-1, 0, -1),
    (1, 0, -1),
    (-1, 0, 1),
    (0, 1, 1),
    (0, -1, -1),
    (0, 1, -1),
    (0, -1, 1),
]
SIDE_SWAP = [1, 0, 3, 2, 5, 4]
WEIGHTS_HEAT = [0.25] + [0.125] * 6
TAU_FLOW, TAU_HEAT = 0.8, 0.9
BUOYANCY = 0.002
WALL_COEF = 0.1
BRICK_LOSS = 0.5
COND_BASE, COND_SLOPE = 0.04, 0.1
LATENT, MELT, MELT_WIDTH = 2.0, 4.0, 0.5

GX, GY = 16, 8
DEV = GX * GY
CAP = 16
ROWS, TILES, NZ = 32, 16, 32
PITCH = 48
TALL = (TILES + 2) * PITCH
SLOTS = CAP * DEV

ALL_VELOCITY = VELOCITY + VELOCITY[:7]
SIDES = [([9, 1, 11, 13, 7], 20), ([10, 2, 12, 14, 8], 21)]
SIDES += [([7, 3, 15, 17, 10], 22), ([8, 4, 16, 18, 9], 23)]
CORNERS = [(7, 1, 1), (8, -1, -1), (9, 1, -1), (10, -1, 1)]


def iota(shape, dim):
    return lax.broadcasted_iota(I32, shape, dim)


def lane_pick(rows, index):
    return jnp.take_along_axis(rows, index, axis=1, mode="promise_in_bounds")


def compact(get, key, val, packed):
    square = (128, 128)
    wide_row, wide_lane = iota((128, 256), 0), iota((128, 256), 1)
    prefix = jnp.where(wide_row <= wide_lane, 1.0, 0.0).astype(BF16)
    before = jnp.zeros(square, F32)
    for b in range(8):
        mask, value = get(b)
        counts = jnp.dot(
            jnp.where(mask, 1.0, 0.0).astype(BF16), prefix, preferred_element_type=F32
        )
        key[b] = jnp.where(mask, counts[:, :128] + before, 0.0)
        val[b] = value
        before = before + counts[:, 128:]

    @pl.loop(0, 4)
    def _(c):
        for u in range(4):
            rows = pl.ds(pl.multiple_of(c * 32 + u * 8, 8), 8)
            keys = [key[b, rows, :] for b in range(8)]
            vals = [val[b, rows, :] for b in range(8)]
            at = iota((8, 128), 1)
            out = jnp.zeros((8, 128), F32)
            for r in range(CAP):
                hit = jnp.zeros((8, 128), F32)
                for b in range(8):
                    hit = jnp.where(keys[b] == float(r + 1), vals[b], hit)
                out = jnp.where(at == r, jnp.sum(hit, axis=1, keepdims=True), out)
            packed[rows, :] = out

    return packed[...]


def split_cell(c):
    c = c.astype(I32) - 1
    live = c >= 0
    a = ((c >> 7) & 15) * ROWS + (c >> 11)
    return jnp.where(live, a, -1), c & 127, live


def split_spot(c):
    c = c.astype(I32) - 1
    live = c >= 0
    return jnp.where(live, c >> 6, -1), c & 63, live


def fill_onehots(row, onehot):
    count = onehot.shape[0]
    for r in range(CAP):
        for q in range(0, count, 128):
            size = min(128, count)
            part = iota((size, 128), 0) + q == row[r : r + 1, :]
            onehot[q : q + size, r * 128 : (r + 1) * 128] = jnp.where(part, 1.0, 0.0).astype(BF16)


def fill_pick(x, y, ids, links, wide, by_slot, pick):
    order = jnp.concatenate([ids[0:1, :], ids[1:2, :]], axis=1)
    chosen = jnp.where(iota((256, 256), 0) == order, 1.0, 0.0).astype(BF16)
    wide[...] = jnp.zeros((128, 256), F32)
    wide[0:6, :] = jnp.dot(
        links.astype(F32).astype(BF16), chosen, preferred_element_type=F32
    )
    by_slot[0:128, :] = jnp.transpose(wide[:, 0:128])
    by_slot[128:256, :] = jnp.transpose(wide[:, 128:256])
    at, to_x = iota((16, 128), 1), iota((16, 128), 0)
    half = jnp.where(x >= GX // 2, ids[1:2, :], ids[0:1, :])
    column = lax.rem(x, GX // 2) * 16 + (at >> 4) * 2 + (at & 1)
    here = lane_pick(jnp.broadcast_to(half.astype(F32), (16, 128)), column)
    side = (at & 15) >> 1
    for b in range(2):
        named = by_slot[pl.ds(2 * y + b, 16, stride=16), :]
        for s in range(6):
            j = s * 2 + b
            n = named[:, s : s + 1]
            remote = (n == here) & (side == SIDE_SWAP[s])
            own = (n < 0.0) & (to_x == x) & (at == y * 16 + j)
            pick[j * 16 : (j + 1) * 16, :] = jnp.where(remote | own, 1.0, 0.0).astype(BF16)


def to_rows(brick):
    at = iota((1, 128), 1)
    rows = []
    for b in range(2):
        for x in range(8):
            part = brick[b : b + 1, (x // 2) * 128 : (x // 2 + 1) * 128]
            part = pltpu.roll(part, 64, 1) if x % 2 else part
            rows.append(jnp.where(at < 64, part, 0.0))
    return jnp.concatenate(rows, axis=0)


def from_rows(rows, out):
    turned = pltpu.roll(rows, 64, 1)
    at = iota((1, 128), 1)
    for b in range(2):
        for q in range(4):
            r = b * 8 + q * 2
            out[b : b + 1, q * 128 : (q + 1) * 128] = jnp.where(
                at < 64, rows[r : r + 1, :], turned[r + 1 : r + 2, :]
            )


def collide(f, g, solid):
    pairs = [(1, 2), (3, 4), (5, 6), (7, 8), (9, 10), (11, 12), (13, 14), (15, 16), (17, 18)]
    total = {a: f[a] + f[b] for a, b in pairs}
    diff = {a: f[a] - f[b] for a, b in pairs}
    density = f[0] + (
        (total[1] + total[3])
        + (total[5] + total[7])
        + (total[9] + total[11])
        + (total[13] + total[15])
        + total[17]
    )
    inverse = 1.0 / density
    ux = (diff[1] + diff[7] + diff[9] + diff[11] + diff[13]) * inverse
    uy = (diff[3] + diff[7] - diff[9] + diff[15] + diff[17]) * inverse
    uz = (diff[5] + diff[11] - diff[13] + diff[15] - diff[17]) * inverse
    temp = g[0] + ((g[1] + g[2]) + (g[3] + g[4]) + (g[5] + g[6]))
    sz = uz + (TAU_FLOW * BUOYANCY) * (temp - 1.0) * inverse
    base = 1.0 - 1.5 * (ux * ux + uy * uy + sz * sz)
    keep = 1.0 - 1.0 / TAU_FLOW
    along_of = {1: ux, 3: uy, 5: sz, 7: ux + uy, 9: ux - uy}
    along_of.update({11: ux + sz, 13: ux - sz, 15: uy + sz, 17: uy - sz})
    out_f = [None] * 19
    k0 = density * (1.0 / 3.0 / TAU_FLOW)
    out_f[0] = jnp.where(solid, f[0], keep * f[0] + k0 * base)
    scale = {1: density * (1.0 / 18.0 / TAU_FLOW), 7: density * (1.0 / 36.0 / TAU_FLOW)}
    for a, b in pairs:
        k = scale[1 if a < 7 else 7]
        along = along_of[a]
        even = k * (base + 4.5 * (along * along))
        odd = (3.0 * k) * along
        out_f[a] = jnp.where(solid, f[b], (even + odd) + keep * f[a])
        out_f[b] = jnp.where(solid, f[a], (even - odd) + keep * f[b])
    keep = 1.0 - 1.0 / TAU_HEAT
    out_g = [None] * 7
    out_g[0] = jnp.where(solid, g[0], keep * g[0] + (0.25 / TAU_HEAT) * temp)
    k = (0.125 / TAU_HEAT) * temp
    for a, u in ((1, ux), (3, uy), (5, uz)):
        odd = (4.0 * k) * u
        out_g[a] = jnp.where(solid, g[a + 1], (k + odd) + keep * g[a])
        out_g[a + 1] = jnp.where(solid, g[a], (k - odd) + keep * g[a + 1])
    return out_f, out_g


def pull(store, pop, t, xb, lane):
    cx, cy, cz = ALL_VELOCITY[pop]
    at = pop

    def tile(step):
        return store[at, pl.ds((t + 1 + step) * PITCH + 8 + xb * 8 - cx, 8), :]

    here = tile(0)
    if cy == 1:
        here = jnp.where(lane >= 128 - NZ, tile(-1), here)
    if cy == -1:
        here = jnp.where(lane < NZ, tile(1), here)
    shift = (cy * NZ + cz) % 128
    if shift:
        here = pltpu.roll(here, shift, 1)
    if cz == 1:
        here = jnp.where(lane & (NZ - 1) == 0, 0.0, here)
    if cz == -1:
        here = jnp.where(lane & (NZ - 1) == NZ - 1, 0.0, here)
    return here


def own_rows(t, xb):
    return pl.ds((t + 1) * PITCH + 8 + xb * 8, 8)


def natural(t, xb):
    return pl.ds(xb * 8, 8), pl.ds(pl.multiple_of(t * 128, 128), 128)


def temp_rows(t, xb):
    return pl.ds(pl.multiple_of(t * ROWS + xb * 8, 8), 8)


def halves(value):
    high = value.astype(BF16)
    return high, (value - high.astype(F32)).astype(BF16)


def scatter(onehot, columns, flux, spread):
    high, low = halves(flux)
    high, low = high.astype(F32), low.astype(F32)
    at = iota((128, 128), 1)
    for r in range(CAP):
        hit = at == columns[:, r : r + 1]
        rows = slice(r * 128, (r + 1) * 128)
        spread[rows, 0:128] = jnp.where(hit, high[:, r : r + 1], 0.0).astype(BF16)
        spread[rows, 128:256] = jnp.where(hit, low[:, r : r + 1], 0.0).astype(BF16)
    both = jnp.dot(onehot[...], spread[...], preferred_element_type=F32)
    return both[:, :128] + both[:, 128:]


def brick_lookup(brick, brow, blrow):
    out = jnp.zeros((CAP, 128), F32)
    for a in range(16):
        row = jnp.broadcast_to(brick[a : a + 1, :], (CAP, 128))
        out = jnp.where(brow == a, lane_pick(row, blrow), out)
    return out


def store_faces(brick, faces):
    at, row = iota((16, 128), 1), iota((16, 128), 0)
    mine = ((at >> 3) & 7) == (row & 7)
    wanted = {
        2: at & 7,
        3: 56 + (at & 7),
        4: (at & 7) * 8,
        5: (at & 7) * 8 + 7,
    }
    faces[12:16, :] = jnp.zeros((4, 128), F32)
    for b in range(2):
        faces[b : b + 1, :] = brick[b * 8 : b * 8 + 1, :]
        faces[2 + b : 3 + b, :] = brick[b * 8 + 7 : b * 8 + 8, :]
    for s, index in wanted.items():
        got = jnp.where(mine, lane_pick(brick, index), 0.0)
        for b in range(2):
            faces[s * 2 + b : s * 2 + b + 1, :] = jnp.sum(
                got[b * 8 : b * 8 + 8], axis=0, keepdims=True
            )


def conduct(brick, ghost, loss):
    at, row = iota((16, 128), 1), iota((16, 128), 0)
    x = row & 7

    def ghost_rows(s):
        return jnp.where(row < 8, ghost[s * 2 : s * 2 + 1, :], ghost[s * 2 + 1 : s * 2 + 2, :])

    over_z = x * 8 + (at & 7)
    over_y = x * 8 + ((at >> 3) & 7)
    beside = [
        jnp.where(x == 0, ghost_rows(0), pltpu.roll(brick, 1, 0)),
        jnp.where(x == 7, ghost_rows(1), pltpu.roll(brick, 15, 0)),
        jnp.where(at < 8, lane_pick(ghost_rows(2), over_z), pltpu.roll(brick, 8, 1)),
        jnp.where(at >= 56, lane_pick(ghost_rows(3), over_z), pltpu.roll(brick, 120, 1)),
        jnp.where((at & 7) == 0, lane_pick(ghost_rows(4), over_y), pltpu.roll(brick, 1, 1)),
        jnp.where((at & 7) == 7, lane_pick(ghost_rows(5), over_y), pltpu.roll(brick, 127, 1)),
    ]
    here = COND_BASE * (1.0 + COND_SLOPE * brick)
    spread = jnp.zeros((16, 128), F32)
    for other in beside:
        spread += 0.5 * (here + COND_BASE * (1.0 + COND_SLOPE * other)) * (other - brick)
    phase = 1.0 / (1.0 + jnp.exp(-(brick - MELT) / MELT_WIDTH))
    capacity = 1.0 + LATENT * phase * (1.0 - phase) / MELT_WIDTH
    return jnp.where(at < 64, brick + (spread - BRICK_LOSS * loss) / capacity, 0.0)


def steps_kernel(
    flow_in,
    heat_in,
    solid_in,
    owners_in,
    spots_in,
    cells_in,
    brick_in,
    ids_in,
    links_in,
    second,
    brick_out,
    first,
    flow,
    heat,
    solid,
    owners,
    spots,
    cells,
    brick_flat,
    ids,
    links,
    key,
    val,
    packed,
    wide,
    by_slot,
    pick,
    oh_cell,
    oh_brick,
    arow,
    lrow,
    lcol,
    brow,
    blrow,
    blcol,
    temps,
    gain,
    spread,
    found,
    asked,
    msg,
    faces,
    brick,
    s1,
    r1,
    s2,
    r2,
    xf,
    xfr,
    yf,
    yfr,
    cf,
    cfr,
    xh,
    xhr,
    yh,
    yhr,
    load_sem,
    s1_send,
    s1_recv,
    s2_send,
    s2_recv,
    flow_send,
    flow_recv,
    heat_send,
    heat_recv,
):
    x, y = lax.axis_index("gx"), lax.axis_index("gy")
    me = x * GY + y

    def xn(k):
        return lax.rem(x + (k + GX), GX)

    def yn(k):
        return lax.rem(y + (k + GY), GY)

    own_faces = pl.ds(pl.multiple_of(me * 8, 8), 8)
    loads = {}
    for n, (name, source, target) in enumerate(
        (
            ("owners", owners_in, owners),
            ("cells", cells_in.at[own_faces, :], cells),
            ("spots", spots_in, spots),
            ("heat", heat_in, heat),
            ("brick", brick_in, brick_flat),
            ("ids", ids_in, ids),
            ("links", links_in, links),
            ("solid", solid_in, solid),
            ("flow", flow_in, flow),
        )
    ):
        loads[name] = pltpu.make_async_copy(source, target, load_sem.at[n])
        loads[name].start()

    barrier = pltpu.get_barrier_semaphore()
    peers = [(x, yn(k)) for k in range(1, GY)] + [(xn(k), y) for k in range(1, GX)]
    peers += [(xn(a), yn(b)) for a in (-1, 1) for b in (-1, 1)]
    for peer in peers:
        pl.semaphore_signal(barrier, inc=1, device_id=peer, device_id_type=MESH)

    lane = iota((8, 128), 1)


    def look_up_row(row, outs, u, a, low):
        line = jnp.broadcast_to(temps[pl.ds(row, 1), :], (CAP, 128))
        outs[u % 4] = jnp.where(a == row, lane_pick(line, low), outs[u % 4])

    def look_up_tiles(start, stop, top, bottom):
        a, low = arow[...], lrow[...]

        def tile(t, outs):
            outs = list(outs)
            for u, row in enumerate(range(top, bottom)):
                look_up_row(t * ROWS + row, outs, u, a, low)
            return tuple(outs)

        outs = lax.fori_loop(start, stop, tile, (jnp.zeros((CAP, 128), F32),) * 4)
        return (outs[0] + outs[1]) + (outs[2] + outs[3])

    def look_up_edges():
        a, low = arow[...], lrow[...]
        outs = [jnp.zeros((CAP, 128), F32)] * 4
        for u, t in enumerate(range(1, TILES - 1)):
            for row in (0, ROWS - 1):
                look_up_row(t * ROWS + row, outs, u, a, low)
        return (outs[0] + outs[1]) + (outs[2] + outs[3])

    def ask():
        now = brick[...]
        asked[...] = brick_lookup(now, brow[...], blrow[...])
        store_faces(now, faces)

    def fill_message():
        rest = jnp.zeros((128 - 2 * CAP, 128), F32)
        msg[...] = jnp.transpose(jnp.concatenate([found[...], asked[...], rest], axis=0))


    def one(step, k, to, slot):
        rows = pl.ds(pl.multiple_of(to * 32, 32), 32)
        place = pl.ds(pl.multiple_of(slot * 32, 32), 32)
        return pltpu.make_async_remote_copy(
            src_ref=s1.at[step, rows, :],
            dst_ref=r1.at[step, place, :],
            send_sem=s1_send.at[step, k],
            recv_sem=s1_recv.at[step, slot],
            device_id=(x, to),
            device_id_type=MESH,
        )

    def two(step, k, to, slot):
        rows = pl.ds(pl.multiple_of(to * 24, 8), 24)
        place = pl.ds(pl.multiple_of(slot * 24, 8), 24)
        return pltpu.make_async_remote_copy(
            src_ref=s2.at[step, rows, :],
            dst_ref=r2.at[step, place, :],
            send_sem=s2_send.at[step, k],
            recv_sem=s2_recv.at[step, slot],
            device_id=(to, y),
            device_id_type=MESH,
        )

    def start_one(step):
        for k in range(GY):
            s1[step, k * 32 : k * 32 + 16, :] = msg[pl.ds(k, 16, stride=8), :]
            s1[step, k * 32 + 16 : k * 32 + 32, :] = faces[...]
        for k in range(1, GY):
            one(step, k, yn(k), y).start()
        own = pl.ds(pl.multiple_of(y * 32, 32), 32)
        r1[step, own, :] = s1[step, own, :]

    def end_one(step):
        for k in range(1, GY):
            one(step, k, yn(k), y).wait_send()
        for k in range(1, GY):
            one(step, k, yn(k), yn(k)).wait_recv()

    def start_two(step):
        every = jnp.concatenate(
            [r1[step, k * 32 + 16 : k * 32 + 32, :] for k in range(GY)], axis=0
        )
        high = every.astype(BF16)
        low = every - high.astype(F32)
        at = iota((128, 128), 1)
        both = jnp.where(at < 64, high.astype(F32), pltpu.roll(low, 64, 1)).astype(BF16)
        picked = jnp.dot(pick[...], both, preferred_element_type=F32)
        picked = picked + pltpu.roll(picked, 64, 1)
        for j in range(12):
            s2[step, pl.ds(8 + j, 16, stride=24), :] = picked[j * 16 : (j + 1) * 16, :]
        for j in range(12, 16):
            s2[step, pl.ds(8 + j, 16, stride=24), :] = jnp.zeros((16, 128), F32)
        for k in range(GX):
            s2[step, k * 24 : k * 24 + 8, :] = r1[step, pl.ds(k, 8, stride=32), :]
        for k in range(1, GX):
            two(step, k, xn(k), x).start()
        own = pl.ds(pl.multiple_of(x * 24, 8), 24)
        r2[step, own, :] = s2[step, own, :]

    def end_two(step):
        for k in range(1, GX):
            two(step, k, xn(k), x).wait_send()
        for k in range(1, GX):
            two(step, k, xn(k), xn(k)).wait_recv()

    def arrived(step):
        return jnp.concatenate([r2[step, k * 24 : k * 24 + 8, :] for k in range(GX)], axis=0)

    def heat_faces(step, store):
        flux = WALL_COEF * (pltpu.roll(arrived(step), 128 - CAP, 1) - msg[...])
        gain[...] = scatter(oh_cell, lcol[...], flux, spread)

        @pl.loop(0, TILES)
        def _(t):
            for xb in range(4):
                more = gain[temp_rows(t, xb), :]
                rows = own_rows(t, xb)
                for j in range(7):
                    store[19 + j, rows, :] = store[19 + j, rows, :] + WEIGHTS_HEAT[j] * more

    def cool_bricks(step):
        flux = WALL_COEF * (pltpu.roll(msg[...], 128 - CAP, 1) - arrived(step))
        loss = scatter(oh_brick, blcol[...], flux, spread)
        ghost = r2[step, 8:24, :]
        for k in range(1, GX):
            ghost = ghost + r2[step, k * 24 + 8 : k * 24 + 24, :]
        brick[...] = conduct(brick[...], ghost, loss)


    ways = [(1, 0), (-1, 0), (0, 1), (0, -1)]
    inside = {(1, 0): x > 0, (-1, 0): x < GX - 1, (0, 1): y > 0, (0, -1): y < GY - 1}
    leave_row, leave_tile = (39, 8), (TILES, 1)
    enter_row, enter_tile = (7, 40), (0, TILES + 1)
    edge_lane = (128 - NZ, 0)

    def plan_copies(step, plan, send, recv):
        return [
            pltpu.make_async_remote_copy(
                src_ref=source,
                dst_ref=target,
                send_sem=send.at[step, n],
                recv_sem=recv.at[step, n],
                device_id=peer,
                device_id_type=MESH,
            )
            for n, (source, target, peer) in enumerate(plan)
        ]

    def flow_copies(step):
        plan = []
        for n, (dx, dy) in enumerate(ways):
            source, target = (xf, xfr) if n < 2 else (yf, yfr)
            plan.append((source.at[step, n % 2], target.at[step, n % 2], (xn(dx), yn(dy))))
        for c, (_, dx, dy) in enumerate(CORNERS):
            plan.append((cf.at[step, c], cfr.at[step, c], (xn(dx), yn(dy))))
        return plan_copies(step, plan, flow_send, flow_recv)

    def heat_copies(step):
        plan = []
        for n, (dx, dy) in enumerate(ways):
            source, target = (xh, xhr) if n < 2 else (yh, yhr)
            plan.append((source.at[step, n % 2], target.at[step, n % 2], (xn(dx), yn(dy))))
        return plan_copies(step, plan, heat_send, heat_recv)

    def send_flow_halo(step, store):
        for n in range(2):
            for k, pop in enumerate(SIDES[n][0]):
                rows = pl.ds(PITCH + leave_row[n], 16, stride=PITCH)
                xf[step, n, k * 16 : (k + 1) * 16, :] = store[pop, rows, :]
        at = iota((32, 128), 1)
        for n in range(2):
            top = leave_tile[n] * PITCH + 8
            parts = []
            for k, pop in enumerate(SIDES[2 + n][0]):
                turn = ((k % 4) * NZ - edge_lane[n]) % 128
                part = store[pop, top : top + 32, :]
                parts.append(pltpu.roll(part, turn, 1) if turn else part)
            for k in range(1, 4):
                parts[0] = jnp.where(at >= k * NZ, parts[k], parts[0])
            yf[step, n, 0:32, :] = parts[0]
            yf[step, n, 32:64, :] = parts[4]
        for c, (pop, dx, dy) in enumerate(CORNERS):
            row = leave_tile[dy < 0] * PITCH + leave_row[dx < 0]
            cf[step, c] = jnp.broadcast_to(store[pop, row : row + 1, :], (8, 128))
        for copy in flow_copies(step):
            copy.start()

    def end_flow_halo(step, store):
        for copy in flow_copies(step):
            copy.wait()
        for n in range(2):
            for k, pop in enumerate(SIDES[n][0]):
                rows = pl.ds(PITCH + enter_row[n], 16, stride=PITCH)
                store[pop, rows, :] = jnp.where(
                    inside[ways[n]], xfr[step, n, k * 16 : (k + 1) * 16, :], 0.0
                )
        for n in range(2):
            top = enter_tile[n] * PITCH + 8
            for k, pop in enumerate(SIDES[2 + n][0]):
                part = yfr[step, n, (k // 4) * 32 : (k // 4 + 1) * 32, :]
                turn = (edge_lane[n] - (k % 4) * NZ) % 128
                part = pltpu.roll(part, turn, 1) if turn else part
                store[pop, top : top + 32, :] = jnp.where(inside[ways[2 + n]], part, 0.0)
        for c, (pop, dx, dy) in enumerate(CORNERS):
            row = enter_tile[dy < 0] * PITCH + enter_row[dx < 0]
            known = inside[(dx, 0)] & inside[(0, dy)]
            store[pop, row : row + 1, :] = jnp.where(known, cfr[step, c, 0:1, :], 0.0)

    def send_heat_halo(step, store):
        for n in range(2):
            rows = pl.ds(PITCH + leave_row[n], 16, stride=PITCH)
            xh[step, n] = store[SIDES[n][1], rows, :]
            top = leave_tile[n] * PITCH + 8
            yh[step, n] = store[SIDES[2 + n][1], top : top + 32, :]
        for copy in heat_copies(step):
            copy.start()

    def end_heat_halo(step, store):
        for copy in heat_copies(step):
            copy.wait()
        for n in range(2):
            rows = pl.ds(PITCH + enter_row[n], 16, stride=PITCH)
            store[SIDES[n][1], rows, :] = jnp.where(inside[ways[n]], xhr[step, n], 0.0)
            top = enter_tile[n] * PITCH + 8
            store[SIDES[2 + n][1], top : top + 32, :] = jnp.where(
                inside[ways[2 + n]], yhr[step, n], 0.0
            )


    def store_relaxed(store, t, xb, f, g):
        out_f, out_g = collide(f, g, solid[natural(t, xb)] == 1)
        rows = own_rows(t, xb)
        for i, value in enumerate(out_f + out_g):
            store[i, rows, :] = value

    def relax_first(low, high):
        @pl.loop(low, high)
        def _(t):
            for xb in range(4):
                rows, lanes = natural(t, xb)
                f = [flow[i, rows, lanes] for i in range(19)]
                g = [heat[j, rows, lanes] for j in range(7)]
                store_relaxed(first, t, xb, f, g)

    def relax_second(low, high):
        @pl.loop(low, high)
        def _(t):
            for xb in range(4):
                f = [pull(first, i, t, xb, lane) for i in range(19)]
                g = [pull(first, 19 + j, t, xb, lane) for j in range(7)]
                store_relaxed(second, t, xb, f, g)

    def sum_heat(g):
        return g[0] + ((g[1] + g[2]) + (g[3] + g[4]) + (g[5] + g[6]))

    def pulled_temp(t, xb):
        temps[temp_rows(t, xb), :] = sum_heat([pull(first, 19 + j, t, xb, lane) for j in range(7)])


    square = (128, 128)
    loads["owners"].wait()
    loads["cells"].wait()
    row_index = iota(square, 0)
    own_owner = owners[own_faces, :]
    own_cell = cells[...].astype(F32) + 1.0
    table = compact(
        lambda b: (
            row_index == own_owner[b : b + 1, :],
            jnp.broadcast_to(own_cell[b : b + 1, :], square),
        ),
        key,
        val,
        packed,
    )
    _, low, live = split_cell(table)
    lcol[...] = jnp.where(live, low, -1)
    a, low, live = split_cell(jnp.transpose(table)[:CAP, :])
    arow[...] = a
    lrow[...] = jnp.where(live, low, 0)

    loads["spots"].wait()

    def from_device(b):
        rows = pl.ds(b, 128, stride=8)
        return owners[rows, :] == me, spots[rows, :].astype(F32) + 1.0

    table = compact(from_device, key, val, packed)
    _, low, live = split_spot(table)
    blcol[...] = jnp.where(live, low, -1)
    a, low, live = split_spot(jnp.transpose(table)[:CAP, :])
    brow[...] = a
    blrow[...] = jnp.where(live, low, 0)


    loads["heat"].wait()

    @pl.loop(0, TILES)
    def _(t):
        for xb in range(4):
            rows, lanes = natural(t, xb)
            temps[temp_rows(t, xb), :] = sum_heat([heat[j, rows, lanes] for j in range(7)])

    found[...] = look_up_tiles(0, TILES, 0, ROWS)
    loads["brick"].wait()
    brick[...] = to_rows(brick_flat[...])
    ask()
    fill_message()
    pl.semaphore_wait(barrier, len(peers))
    start_one(0)
    loads["ids"].wait()
    loads["links"].wait()
    fill_pick(x, y, ids[...], links[...], wide, by_slot, pick)
    fill_onehots(arow[...], oh_cell)
    fill_onehots(brow[...], oh_brick)
    loads["solid"].wait()
    loads["flow"].wait()
    relax_first(0, TILES // 4)
    end_one(0)
    start_two(0)
    relax_first(TILES // 4, TILES)
    send_flow_halo(0, first)
    end_two(0)
    heat_faces(0, first)
    send_heat_halo(0, first)
    cool_bricks(0)
    ask()


    @pl.loop(1, TILES - 1)
    def _(t):
        for xb in range(4):
            pulled_temp(t, xb)

    found[...] = look_up_tiles(1, TILES - 1, 1, ROWS - 1)
    end_heat_halo(0, first)

    @pl.loop(1, TILES - 1)
    def _(t):
        for xb in (0, 3):
            pulled_temp(t, xb)

    for t in (0, TILES - 1):
        for xb in range(4):
            pulled_temp(t, xb)
    found[...] = found[...] + (look_up_edges() + look_up_tiles(0, 1, 0, ROWS))
    found[...] = found[...] + look_up_tiles(TILES - 1, TILES, 0, ROWS)
    fill_message()
    start_one(1)
    end_flow_halo(0, first)
    relax_second(0, TILES // 2)
    end_one(1)
    start_two(1)
    relax_second(TILES // 2, TILES)
    send_flow_halo(1, second)
    end_two(1)
    heat_faces(1, second)
    send_heat_halo(1, second)
    cool_bricks(1)
    from_rows(brick[...], brick_out)
    end_flow_halo(1, second)
    end_heat_halo(1, second)


def spread_kernel(second, flow_out, heat_out):
    lane = iota((8, 128), 1)
    step = pl.program_id(0)
    width = flow_out.shape[2] // 128

    @pl.loop(0, width)
    def _(u):
        t = step * width + u
        for xb in range(4):
            rows, lanes = natural(u, xb)
            for i in range(19):
                flow_out[i, rows, lanes] = pull(second, i, t, xb, lane)
            for j in range(7):
                heat_out[j, rows, lanes] = pull(second, 19 + j, t, xb, lane)


def body(
    flow_pops,
    heat_pops,
    solid_flag,
    brick_temp,
    brick_ids,
    brick_links,
    face_cell,
    face_owner,
    face_spot,
):
    shape = jax.ShapeDtypeStruct
    dma = pltpu.SemaphoreType.DMA
    near = pl.BlockSpec(memory_space=pltpu.VMEM)
    far = pl.BlockSpec(memory_space=pltpu.HBM)
    grid = (TILES * ROWS, 128)
    inputs = (
        flow_pops,
        heat_pops,
        solid_flag,
        face_owner.reshape(1024, 128),
        face_spot.reshape(1024, 128),
        face_cell.reshape(1024, 128),
        brick_temp,
        brick_ids.reshape(2, 128),
        brick_links.T,
    )
    second, brick = pl.pallas_call(
        steps_kernel,
        out_shape=[pltpu.VMEM((26, TALL, 128), F32), shape((2, 512), F32)],
        in_specs=[far] * 9,
        out_specs=[near] * 2,
        scratch_shapes=[
            pltpu.VMEM((26, TALL, 128), F32),
            pltpu.VMEM(flow_pops.shape, F32),
            pltpu.VMEM(heat_pops.shape, F32),
            pltpu.VMEM(solid_flag.shape, I32),
            pltpu.VMEM((1024, 128), I32),
            pltpu.VMEM((1024, 128), I32),
            pltpu.VMEM((8, 128), I32),
            pltpu.VMEM((2, 512), F32),
            pltpu.VMEM((2, 128), I32),
            pltpu.VMEM((6, 256), I32),
            pltpu.VMEM((8, 128, 128), F32),
            pltpu.VMEM((8, 128, 128), F32),
            pltpu.VMEM((128, 128), F32),
            pltpu.VMEM((128, 256), F32),
            pltpu.VMEM((256, 128), F32),
            pltpu.VMEM((192, 128), BF16),
            pltpu.VMEM((TILES * ROWS, SLOTS), BF16),
            pltpu.VMEM((16, SLOTS), BF16),
            pltpu.VMEM((CAP, 128), I32),
            pltpu.VMEM((CAP, 128), I32),
            pltpu.VMEM((128, 128), I32),
            pltpu.VMEM((CAP, 128), I32),
            pltpu.VMEM((CAP, 128), I32),
            pltpu.VMEM((128, 128), I32),
            pltpu.VMEM(grid, F32),
            pltpu.VMEM(grid, F32),
            pltpu.VMEM((SLOTS, 256), BF16),
            pltpu.VMEM((CAP, 128), F32),
            pltpu.VMEM((CAP, 128), F32),
            pltpu.VMEM((128, 128), F32),
            pltpu.VMEM((16, 128), F32),
            pltpu.VMEM((16, 128), F32),
            pltpu.VMEM((2, GY * 32, 128), F32),
            pltpu.VMEM((2, GY * 32, 128), F32),
            pltpu.VMEM((2, GX * 24, 128), F32),
            pltpu.VMEM((2, GX * 24, 128), F32),
            pltpu.VMEM((2, 2, 80, 128), F32),
            pltpu.VMEM((2, 2, 80, 128), F32),
            pltpu.VMEM((2, 2, 64, 128), F32),
            pltpu.VMEM((2, 2, 64, 128), F32),
            pltpu.VMEM((2, 4, 8, 128), F32),
            pltpu.VMEM((2, 4, 8, 128), F32),
            pltpu.VMEM((2, 2, 16, 128), F32),
            pltpu.VMEM((2, 2, 16, 128), F32),
            pltpu.VMEM((2, 2, 32, 128), F32),
            pltpu.VMEM((2, 2, 32, 128), F32),
            dma((9,)),
            dma((2, GY)),
            dma((2, GY)),
            dma((2, GX)),
            dma((2, GX)),
            dma((2, 8)),
            dma((2, 8)),
            dma((2, 4)),
            dma((2, 4)),
        ],
        compiler_params=pltpu.CompilerParams(
            collective_id=0, has_side_effects=True, vmem_limit_bytes=40 << 20
        ),
    )(*(pltpu.with_memory_space_constraint(value, pltpu.HBM) for value in inputs))
    width = 256
    flow, heat = pl.pallas_call(
        spread_kernel,
        grid=(TILES * 128 // width,),
        out_shape=[shape(flow_pops.shape, F32), shape(heat_pops.shape, F32)],
        in_specs=[near],
        out_specs=[
            pl.BlockSpec((19, ROWS, width), lambda i: (0, 0, i)),
            pl.BlockSpec((7, ROWS, width), lambda i: (0, 0, i)),
        ],
        compiler_params=pltpu.CompilerParams(vmem_limit_bytes=16 << 20),
    )(second)
    return flow, heat, brick


def solution(mesh):
    return jax.shard_map(
        body,
        mesh=mesh,
        in_specs=(
            P(None, "gx", "gy"),
            P(None, "gx", "gy"),
            P("gx", "gy"),
            P(("gx", "gy"), None),
            P(),
            P(),
            P(),
            P(),
            P(),
        ),
        out_specs=(P(None, "gx", "gy"), P(None, "gx", "gy"), P(("gx", "gy"), None)),
        check_vma=False,
    )
```

time: 99 us -> 52.2 us (0.53); the launches traced: 97.6 us -> 52.1 us
  Pallas kernels: 85.9 us -> 50.8 us
  local copies, waits for them, and re-layouts: 10.9 us -> 0.59 us
    pallas_call x2 -> x1, Pallas kernels: 29.9 us -> 5.15 us  [body(): pl.pallas_call(spread_kernel, grid=(TILES * 128 // width,), out_shape=[sh...]
    pallas_call x1, Pallas kernels: 56 us -> 45.7 us  [body(): pl.pallas_call(steps_kernel, out_shape=[pltpu.VMEM((26, TALL, 128), F32),...]
    unnamed x13 -> x1, local copies, waits for them, and re-layouts: 7.71 us -> 0.59 us
    reshape x4 -> x0, local copies, waits for them, and re-layouts: 2.38 us -> none  [the longest x1 0.81 us: body(): brick_ids.reshape(256, 1)]
where the time goes in v3:
time: 52.2 us; the launch traced here: 52.1 us
  Pallas kernels  50.8 us (97%)
  between operations  0.64 us (1%)
  local copies, waits for them, and re-layouts  0.59 us (1%)
    pallas_call x1, Pallas kernels, body(): pl.pallas_call(steps_kernel, out_shape=[pltpu.VMEM((26, TALL, 128), F32),...  45.7 us
    pallas_call x1, Pallas kernels, body(): pl.pallas_call(spread_kernel, grid=(TILES * 128 // width,), out_shape=[sh...  5.15 us

profile of v3, /device:TPU:1, one launch (start us, length us, event | category | flops | bytes accessed | tf_op | source)
XLA Modules:
  0.0 52.1 jit_solution(7700061208621404820)
XLA Ops:
  0.6 45.7 %shard_map.112 = (f32[26,864,128]{2,1,0:T(8,128)S(1)}, f32[2,512]{1,0:T(2,128)S(1)}) custom-call(f32[19,32,2048]{2,1,0:T(8,128)} %flow_in.1, f32[7,32,2048]{2,1,0:T(8,128)} %heat_in.1, s32[32,2048]{1,0:T(8,128)} %solid_in.1, s32[1024,128]{1,0:T(8,128)} %bitcast.5, s32[1024,128]{1,0:T(8,128)} %bitcast.6, s32[1024,128]{1,0:T(8,128)} %bitcast.7, ...), custom_call_target="tpu_custom_call" | custom-call | tf_op jit(solution)/shard_map/pallas_call | solution.py:820
  46.3 5.1 %shard_map.113 = (f32[19,32,2048]{2,1,0:T(8,128)}, f32[7,32,2048]{2,1,0:T(8,128)}) custom-call(f32[26,864,128]{2,1,0:T(8,128)S(1)} %get-tuple-element.7.second), custom_call_target="tpu_custom_call" | custom-call | tf_op jit(solution)/shard_map/pallas_call | solution.py:887
  51.5 0.6 %copy.13 = f32[2,512]{1,0:T(2,128)} copy(f32[2,512]{1,0:T(2,128)S(1)} %get-tuple-element.16) | data formatting | bytes 8192

commit v4 on v3

--- a/solution.py
+++ b/solution.py
@@ -116,7 +116,12 @@
             onehot[q : q + size, r * 128 : (r + 1) * 128] = jnp.where(part, 1.0, 0.0).astype(BF16)
 
 
-def fill_pick(x, y, ids, links, wide, by_slot, pick):
+def ranked(device):
+    return (((device >> 2) & 1) << 6) | ((device >> 4) << 3) | (((device >> 3) & 1) << 2) | (device & 3)
+
+
+def fill_pick(spot, ids, links, wide, by_slot, pick):
+    core, xc, ylo, q, inner, outer = spot
     order = jnp.concatenate([ids[0:1, :], ids[1:2, :]], axis=1)
     chosen = jnp.where(iota((256, 256), 0) == order, 1.0, 0.0).astype(BF16)
     wide[...] = jnp.zeros((128, 256), F32)
@@ -125,18 +130,24 @@
     )
     by_slot[0:128, :] = jnp.transpose(wide[:, 0:128])
     by_slot[128:256, :] = jnp.transpose(wide[:, 128:256])
-    at, to_x = iota((16, 128), 1), iota((16, 128), 0)
-    half = jnp.where(x >= GX // 2, ids[1:2, :], ids[0:1, :])
-    column = lax.rem(x, GX // 2) * 16 + (at >> 4) * 2 + (at & 1)
+    at, to = iota((16, 128), 1), iota((16, 128), 0)
+    half = jnp.where(q >= 4, ids[1:2, :], ids[0:1, :])
+    from_b, from_inner, side = at >> 6, (at >> 3) & 7, at & 7
+    column = lax.rem(q, 4) * 32 + (from_inner >> 2) * 16 + ylo * 8 + (from_inner & 3) * 2 + from_b
     here = lane_pick(jnp.broadcast_to(half.astype(F32), (16, 128)), column)
-    side = (at & 15) >> 1
     for b in range(2):
-        named = by_slot[pl.ds(2 * y + b, 16, stride=16), :]
+        named = jnp.concatenate(
+            [
+                by_slot[pl.ds((core * 8 + low * 4 + xc) * 2 + b, 8, stride=32), :]
+                for low in range(2)
+            ],
+            axis=0,
+        )
         for s in range(6):
             j = s * 2 + b
             n = named[:, s : s + 1]
             remote = (n == here) & (side == SIDE_SWAP[s])
-            own = (n < 0.0) & (to_x == x) & (at == y * 16 + j)
+            own = (n < 0.0) & (to == outer) & (at == b * 64 + inner * 8 + s)
             pick[j * 16 : (j + 1) * 16, :] = jnp.where(remote | own, 1.0, 0.0).astype(BF16)
 
 
@@ -205,6 +216,25 @@
     return out_f, out_g
 
 
+class Lattice:
+    def __init__(self, flow, heat):
+        self.flow, self.heat = flow, heat
+
+    def at(self, key):
+        pop = key[0]
+        if pop < 19:
+            return self.flow, key
+        return self.heat, (pop - 19,) + tuple(key[1:])
+
+    def __getitem__(self, key):
+        ref, key = self.at(key)
+        return ref[key]
+
+    def __setitem__(self, key, value):
+        ref, key = self.at(key)
+        ref[key] = value
+
+
 def pull(store, pop, t, xb, lane):
     cx, cy, cz = ALL_VELOCITY[pop]
     at = pop
@@ -267,6 +297,7 @@
 
 def store_faces(brick, faces):
     at, row = iota((16, 128), 1), iota((16, 128), 0)
+    line = iota((1, 128), 1)
     mine = ((at >> 3) & 7) == (row & 7)
     wanted = {
         2: at & 7,
@@ -274,24 +305,25 @@
         4: (at & 7) * 8,
         5: (at & 7) * 8 + 7,
     }
-    faces[12:16, :] = jnp.zeros((4, 128), F32)
-    for b in range(2):
-        faces[b : b + 1, :] = brick[b * 8 : b * 8 + 1, :]
-        faces[2 + b : 3 + b, :] = brick[b * 8 + 7 : b * 8 + 8, :]
-    for s, index in wanted.items():
-        got = jnp.where(mine, lane_pick(brick, index), 0.0)
-        for b in range(2):
-            faces[s * 2 + b : s * 2 + b + 1, :] = jnp.sum(
-                got[b * 8 : b * 8 + 8], axis=0, keepdims=True
-            )
+    faces[6:8, :] = jnp.zeros((2, 128), F32)
+    for s in range(6):
+        if s < 2:
+            low, high = brick[7 * s : 7 * s + 1, :], brick[8 + 7 * s : 9 + 7 * s, :]
+        else:
+            got = jnp.where(mine, lane_pick(brick, wanted[s]), 0.0)
+            low = jnp.sum(got[0:8], axis=0, keepdims=True)
+            high = jnp.sum(got[8:16], axis=0, keepdims=True)
+        faces[s : s + 1, :] = jnp.where(line < 64, low, pltpu.roll(high, 64, 1))
 
 
 def conduct(brick, ghost, loss):
     at, row = iota((16, 128), 1), iota((16, 128), 0)
     x = row & 7
 
+    other_brick = pltpu.roll(ghost, 64, 1)
+
     def ghost_rows(s):
-        return jnp.where(row < 8, ghost[s * 2 : s * 2 + 1, :], ghost[s * 2 + 1 : s * 2 + 2, :])
+        return jnp.where(row < 8, ghost[s : s + 1, :], other_brick[s : s + 1, :])
 
     over_z = x * 8 + (at & 7)
     over_y = x * 8 + ((at >> 3) & 7)
@@ -322,9 +354,11 @@
     brick_in,
     ids_in,
     links_in,
-    second,
+    flow_out,
+    second_heat,
     brick_out,
     first,
+    second_flow,
     flow,
     heat,
     solid,
@@ -337,6 +371,7 @@
     key,
     val,
     packed,
+    reordered,
     wide,
     by_slot,
     pick,
@@ -382,6 +417,21 @@
 ):
     x, y = lax.axis_index("gx"), lax.axis_index("gy")
     me = x * GY + y
+    core, q = lax.rem(x, 2), x // 2
+    xc, ylo = lax.rem(y, 4), y // 4
+    inner, outer = core * 4 + xc, ylo * 8 + q
+
+    def inner_peer(i):
+        return (q * 2 + i // 4, ylo * 4 + lax.rem(i, 4))
+
+    def outer_peer(h):
+        return (lax.rem(h, 8) * 2 + core, (h // 8) * 4 + xc)
+
+    def inner_next(k):
+        return lax.rem(inner + k, 8)
+
+    def outer_next(k):
+        return lax.rem(outer + k, 16)
 
     def xn(k):
         return lax.rem(x + (k + GX), GX)
@@ -389,6 +439,7 @@
     def yn(k):
         return lax.rem(y + (k + GY), GY)
 
+    second = Lattice(second_flow, second_heat)
     own_faces = pl.ds(pl.multiple_of(me * 8, 8), 8)
     loads = {}
     for n, (name, source, target) in enumerate(
@@ -408,8 +459,9 @@
         loads[name].start()
 
     barrier = pltpu.get_barrier_semaphore()
-    peers = [(x, yn(k)) for k in range(1, GY)] + [(xn(k), y) for k in range(1, GX)]
-    peers += [(xn(a), yn(b)) for a in (-1, 1) for b in (-1, 1)]
+    peers = [inner_peer(inner_next(k)) for k in range(1, 8)]
+    peers += [outer_peer(outer_next(k)) for k in range(1, 16)]
+    peers += [(xn(a), yn(b)) for a in (-1, 0, 1) for b in (-1, 0, 1) if a or b]
     for peer in peers:
         pl.semaphore_signal(barrier, inc=1, device_id=peer, device_id_type=MESH)
 
@@ -420,24 +472,41 @@
         line = jnp.broadcast_to(temps[pl.ds(row, 1), :], (CAP, 128))
         outs[u % 4] = jnp.where(a == row, lane_pick(line, low), outs[u % 4])
 
-    def look_up_tiles(start, stop, top, bottom):
-        a, low = arow[...], lrow[...]
-
-        def tile(t, outs):
-            outs = list(outs)
-            for u, row in enumerate(range(top, bottom)):
-                look_up_row(t * ROWS + row, outs, u, a, low)
-            return tuple(outs)
-
-        outs = lax.fori_loop(start, stop, tile, (jnp.zeros((CAP, 128), F32),) * 4)
-        return (outs[0] + outs[1]) + (outs[2] + outs[3])
+    def look_up(inner_only):
+        parts = []
+        for n in range(4):
+            part = temps[n * 128 : (n + 1) * 128, :]
+            if inner_only:
+                row = iota((128, 128), 0)
+                away = (row & 31 != 0) & (row & 31 != 31)
+                if n == 0:
+                    away = away & (row >= 32)
+                if n == 3:
+                    away = away & (row < 96)
+                part = jnp.where(away, part, 0.0)
+            parts.append(jnp.transpose(part))
+        high, low = halves(jnp.concatenate(parts, axis=1))
+        both = jnp.concatenate([high, low], axis=0)
+        lanes = lrow[...]
+        at = iota((128, 128), 0)
+        for r in range(0, CAP, 2):
+            got = jnp.dot(
+                both, oh_cell[:, r * 128 : (r + 2) * 128], preferred_element_type=F32
+            )
+            got = got[:128] + got[128:]
+            for u in range(2):
+                hit = jnp.where(
+                    at == lanes[r + u : r + u + 1, :], got[:, u * 128 : (u + 1) * 128], 0.0
+                )
+                found[r + u : r + u + 1, :] = jnp.sum(hit, axis=0, keepdims=True)
 
     def look_up_edges():
         a, low = arow[...], lrow[...]
         outs = [jnp.zeros((CAP, 128), F32)] * 4
-        for u, t in enumerate(range(1, TILES - 1)):
-            for row in (0, ROWS - 1):
-                look_up_row(t * ROWS + row, outs, u, a, low)
+        rows = [t * ROWS + row for t in range(1, TILES - 1) for row in (0, ROWS - 1)]
+        rows += [t * ROWS + row for t in (0, TILES - 1) for row in range(ROWS)]
+        for u, row in enumerate(rows):
+            look_up_row(row, outs, u, a, low)
         return (outs[0] + outs[1]) + (outs[2] + outs[3])
 
     def ask():
@@ -445,82 +514,90 @@
         asked[...] = brick_lookup(now, brow[...], blrow[...])
         store_faces(now, faces)
 
-    def fill_message():
+    def fill_message(n, temperatures, bricks):
+        none = jnp.zeros((CAP, 128), F32)
+        parts = [found[...] if temperatures else none, asked[...] if bricks else none]
         rest = jnp.zeros((128 - 2 * CAP, 128), F32)
-        msg[...] = jnp.transpose(jnp.concatenate([found[...], asked[...], rest], axis=0))
-
-
-    def one(step, k, to, slot):
-        rows = pl.ds(pl.multiple_of(to * 32, 32), 32)
-        place = pl.ds(pl.multiple_of(slot * 32, 32), 32)
+        msg[n] = jnp.transpose(jnp.concatenate(parts + [rest], axis=0))
+
+
+    def one(n, k, to, slot):
+        count = 16 if n == 2 else 24
         return pltpu.make_async_remote_copy(
-            src_ref=s1.at[step, rows, :],
-            dst_ref=r1.at[step, place, :],
-            send_sem=s1_send.at[step, k],
-            recv_sem=s1_recv.at[step, slot],
-            device_id=(x, to),
+            src_ref=s1.at[n, pl.ds(pl.multiple_of(to * 24, 8), count), :],
+            dst_ref=r1.at[n, pl.ds(pl.multiple_of(slot * 24, 8), count), :],
+            send_sem=s1_send.at[n, k],
+            recv_sem=s1_recv.at[n, slot],
+            device_id=inner_peer(to),
             device_id_type=MESH,
         )
 
-    def two(step, k, to, slot):
-        rows = pl.ds(pl.multiple_of(to * 24, 8), 24)
-        place = pl.ds(pl.multiple_of(slot * 24, 8), 24)
+    def two(n, k, to, slot):
+        count = 8 if n == 2 else 16
         return pltpu.make_async_remote_copy(
-            src_ref=s2.at[step, rows, :],
-            dst_ref=r2.at[step, place, :],
-            send_sem=s2_send.at[step, k],
-            recv_sem=s2_recv.at[step, slot],
-            device_id=(to, y),
+            src_ref=s2.at[n, pl.ds(pl.multiple_of(to * 16, 8), count), :],
+            dst_ref=r2.at[n, pl.ds(pl.multiple_of(slot * 16, 8), count), :],
+            send_sem=s2_send.at[n, k],
+            recv_sem=s2_recv.at[n, slot],
+            device_id=outer_peer(to),
             device_id_type=MESH,
         )
 
-    def start_one(step):
-        for k in range(GY):
-            s1[step, k * 32 : k * 32 + 16, :] = msg[pl.ds(k, 16, stride=8), :]
-            s1[step, k * 32 + 16 : k * 32 + 32, :] = faces[...]
-        for k in range(1, GY):
-            one(step, k, yn(k), y).start()
-        own = pl.ds(pl.multiple_of(y * 32, 32), 32)
-        r1[step, own, :] = s1[step, own, :]
-
-    def end_one(step):
-        for k in range(1, GY):
-            one(step, k, yn(k), y).wait_send()
-        for k in range(1, GY):
-            one(step, k, yn(k), yn(k)).wait_recv()
-
-    def start_two(step):
-        every = jnp.concatenate(
-            [r1[step, k * 32 + 16 : k * 32 + 32, :] for k in range(GY)], axis=0
-        )
-        high = every.astype(BF16)
-        low = every - high.astype(F32)
-        at = iota((128, 128), 1)
-        both = jnp.where(at < 64, high.astype(F32), pltpu.roll(low, 64, 1)).astype(BF16)
-        picked = jnp.dot(pick[...], both, preferred_element_type=F32)
-        picked = picked + pltpu.roll(picked, 64, 1)
-        for j in range(12):
-            s2[step, pl.ds(8 + j, 16, stride=24), :] = picked[j * 16 : (j + 1) * 16, :]
-        for j in range(12, 16):
-            s2[step, pl.ds(8 + j, 16, stride=24), :] = jnp.zeros((16, 128), F32)
-        for k in range(GX):
-            s2[step, k * 24 : k * 24 + 8, :] = r1[step, pl.ds(k, 8, stride=32), :]
-        for k in range(1, GX):
-            two(step, k, xn(k), x).start()
-        own = pl.ds(pl.multiple_of(x * 24, 8), 24)
-        r2[step, own, :] = s2[step, own, :]
-
-    def end_two(step):
-        for k in range(1, GX):
-            two(step, k, xn(k), x).wait_send()
-        for k in range(1, GX):
-            two(step, k, xn(k), xn(k)).wait_recv()
-
-    def arrived(step):
-        return jnp.concatenate([r2[step, k * 24 : k * 24 + 8, :] for k in range(GX)], axis=0)
-
-    def heat_faces(step, store):
-        flux = WALL_COEF * (pltpu.roll(arrived(step), 128 - CAP, 1) - msg[...])
+    def start_one(n):
+        for k in range(8):
+            s1[n, k * 24 : k * 24 + 16, :] = msg[n, pl.ds(k, 16, stride=8), :]
+            if n < 2:
+                s1[n, k * 24 + 16 : k * 24 + 24, :] = faces[...]
+        for k in range(1, 8):
+            one(n, k, inner_next(k), inner).start()
+        own = pl.ds(pl.multiple_of(inner * 24, 8), 24)
+        r1[n, own, :] = s1[n, own, :]
+
+    def end_one(n):
+        for k in range(1, 8):
+            one(n, k, inner_next(k), inner_next(k)).wait_recv()
+
+    def start_two(n):
+        if n < 2:
+            every = jnp.concatenate(
+                [r1[n, k * 24 + 16 : k * 24 + 24, :] for k in range(8)], axis=0
+            )
+            every = jnp.concatenate([every, pltpu.roll(every, 64, 1)], axis=0)
+            high = every.astype(BF16)
+            low = every - high.astype(F32)
+            at = iota((128, 128), 1)
+            both = jnp.where(at < 64, high.astype(F32), pltpu.roll(low, 64, 1)).astype(BF16)
+            picked = jnp.dot(pick[...], both, preferred_element_type=F32)
+            picked = picked + pltpu.roll(picked, 64, 1)
+            at = iota((16, 128), 1)
+            for s in range(8):
+                pair = jnp.zeros((16, 128), F32)
+                if s < 6:
+                    top = s * 32
+                    pair = jnp.where(at < 64, picked[top : top + 16], picked[top + 16 : top + 32])
+                s2[n, pl.ds(8 + s, 16, stride=16), :] = pair
+        for h in range(16):
+            s2[n, h * 16 : h * 16 + 8, :] = r1[n, pl.ds(h, 8, stride=24), :]
+        for k in range(1, 16):
+            two(n, k, outer_next(k), outer).start()
+        own = pl.ds(pl.multiple_of(outer * 16, 8), 16)
+        r2[n, own, :] = s2[n, own, :]
+
+    def end_two(n):
+        for k in range(1, 16):
+            two(n, k, outer_next(k), outer_next(k)).wait_recv()
+
+    def end_sends(n):
+        for k in range(1, 8):
+            one(n, k, inner_next(k), inner).wait_send()
+        for k in range(1, 16):
+            two(n, k, outer_next(k), outer).wait_send()
+
+    def arrived(n):
+        return jnp.concatenate([r2[n, h * 16 : h * 16 + 8, :] for h in range(16)], axis=0)
+
+    def heat_faces(store, came, mine):
+        flux = WALL_COEF * (pltpu.roll(arrived(came), 128 - CAP, 1) - msg[mine])
         gain[...] = scatter(oh_cell, lcol[...], flux, spread)
 
         @pl.loop(0, TILES)
@@ -531,12 +608,12 @@
                 for j in range(7):
                     store[19 + j, rows, :] = store[19 + j, rows, :] + WEIGHTS_HEAT[j] * more
 
-    def cool_bricks(step):
-        flux = WALL_COEF * (pltpu.roll(msg[...], 128 - CAP, 1) - arrived(step))
+    def cool_bricks(came, mine, layers):
+        flux = WALL_COEF * (pltpu.roll(msg[mine], 128 - CAP, 1) - arrived(came))
         loss = scatter(oh_brick, blcol[...], flux, spread)
-        ghost = r2[step, 8:24, :]
-        for k in range(1, GX):
-            ghost = ghost + r2[step, k * 24 + 8 : k * 24 + 24, :]
+        ghost = r2[layers, 8:16, :]
+        for h in range(1, 16):
+            ghost = ghost + r2[layers, h * 16 + 8 : h * 16 + 16, :]
         brick[...] = conduct(brick[...], ghost, loss)
 
 
@@ -674,11 +751,11 @@
     loads["owners"].wait()
     loads["cells"].wait()
     row_index = iota(square, 0)
-    own_owner = owners[own_faces, :]
+    own_place = ranked(owners[own_faces, :])
     own_cell = cells[...].astype(F32) + 1.0
     table = compact(
         lambda b: (
-            row_index == own_owner[b : b + 1, :],
+            row_index == own_place[b : b + 1, :],
             jnp.broadcast_to(own_cell[b : b + 1, :], square),
         ),
         key,
@@ -698,6 +775,10 @@
         return owners[rows, :] == me, spots[rows, :].astype(F32) + 1.0
 
     table = compact(from_device, key, val, packed)
+    for n in range(32):
+        source = ((n >> 1) & 7) * 16 + (n & 1) * 8 + (n >> 4) * 4
+        reordered[n * 4 : n * 4 + 4, :] = packed[source : source + 4, :]
+    table = reordered[...]
     _, low, live = split_spot(table)
     blcol[...] = jnp.where(live, low, -1)
     a, low, live = split_spot(jnp.transpose(table)[:CAP, :])
@@ -713,17 +794,18 @@
             rows, lanes = natural(t, xb)
             temps[temp_rows(t, xb), :] = sum_heat([heat[j, rows, lanes] for j in range(7)])
 
-    found[...] = look_up_tiles(0, TILES, 0, ROWS)
+    fill_onehots(arow[...], oh_cell)
+    look_up(False)
     loads["brick"].wait()
     brick[...] = to_rows(brick_flat[...])
     ask()
-    fill_message()
+    fill_message(0, True, True)
     pl.semaphore_wait(barrier, len(peers))
     start_one(0)
     loads["ids"].wait()
     loads["links"].wait()
-    fill_pick(x, y, ids[...], links[...], wide, by_slot, pick)
-    fill_onehots(arow[...], oh_cell)
+    place = (core, xc, ylo, q, inner, outer)
+    fill_pick(place, ids[...], links[...], wide, by_slot, pick)
     fill_onehots(brow[...], oh_brick)
     loads["solid"].wait()
     loads["flow"].wait()
@@ -733,61 +815,81 @@
     relax_first(TILES // 4, TILES)
     send_flow_halo(0, first)
     end_two(0)
-    heat_faces(0, first)
+    heat_faces(first, 0, 0)
     send_heat_halo(0, first)
-    cool_bricks(0)
+    cool_bricks(0, 0, 0)
     ask()
-
-
-    @pl.loop(1, TILES - 1)
+    fill_message(1, False, True)
+    start_one(1)
+
+
+    @pl.loop(0, (TILES - 2) // 2)
+    def _(n):
+        for u in range(2):
+            for xb in range(4):
+                pulled_temp(1 + 2 * n + u, xb)
+
+    look_up(True)
+    end_one(1)
+    start_two(1)
+    end_heat_halo(0, first)
+    for t in range(TILES):
+        for xb in range(4):
+            if t in (0, TILES - 1) or xb in (0, 3):
+                pulled_temp(t, xb)
+    found[...] = found[...] + look_up_edges()
+    fill_message(2, True, False)
+    start_one(2)
+    end_flow_halo(0, first)
+    relax_second(0, 8)
+    end_one(2)
+    start_two(2)
+    relax_second(8, TILES)
+    send_flow_halo(1, second)
+    end_two(1)
+    heat_faces(second, 1, 2)
+    send_heat_halo(1, second)
+    end_flow_halo(1, second)
+
+    @pl.loop(0, TILES)
     def _(t):
         for xb in range(4):
-            pulled_temp(t, xb)
-
-    found[...] = look_up_tiles(1, TILES - 1, 1, ROWS - 1)
-    end_heat_halo(0, first)
-
-    @pl.loop(1, TILES - 1)
-    def _(t):
-        for xb in (0, 3):
-            pulled_temp(t, xb)
-
-    for t in (0, TILES - 1):
-        for xb in range(4):
-            pulled_temp(t, xb)
-    found[...] = found[...] + (look_up_edges() + look_up_tiles(0, 1, 0, ROWS))
-    found[...] = found[...] + look_up_tiles(TILES - 1, TILES, 0, ROWS)
-    fill_message()
-    start_one(1)
-    end_flow_halo(0, first)
-    relax_second(0, TILES // 2)
-    end_one(1)
-    start_two(1)
-    relax_second(TILES // 2, TILES)
-    send_flow_halo(1, second)
-    end_two(1)
-    heat_faces(1, second)
-    send_heat_halo(1, second)
-    cool_bricks(1)
+            for i in range(19):
+                rows, lanes = natural(t, xb)
+                flow_out[i, rows, lanes] = pull(second, i, t, xb, lane)
+
+    end_sends(0)
+    end_sends(1)
+    end_two(2)
+    cool_bricks(2, 1, 1)
     from_rows(brick[...], brick_out)
-    end_flow_halo(1, second)
+    end_sends(2)
     end_heat_halo(1, second)
 
 
-def spread_kernel(second, flow_out, heat_out):
+def hand_out_kernel(flow, second_heat, brick, flow_out, heat_out, brick_out, heat, sems):
     lane = iota((8, 128), 1)
-    step = pl.program_id(0)
-    width = flow_out.shape[2] // 128
-
-    @pl.loop(0, width)
-    def _(u):
-        t = step * width + u
-        for xb in range(4):
-            rows, lanes = natural(u, xb)
-            for i in range(19):
-                flow_out[i, rows, lanes] = pull(second, i, t, xb, lane)
-            for j in range(7):
-                heat_out[j, rows, lanes] = pull(second, 19 + j, t, xb, lane)
+    copies = [
+        pltpu.make_async_copy(flow, flow_out, sems.at[0]),
+        pltpu.make_async_copy(brick, brick_out, sems.at[1]),
+    ]
+    for copy in copies:
+        copy.start()
+    store = Lattice(None, second_heat)
+
+    @pl.loop(0, TILES // 4)
+    def _(n):
+        for u in range(4):
+            t = n * 4 + u
+            for xb in range(4):
+                for j in range(7):
+                    rows, lanes = natural(t, xb)
+                    heat[j, rows, lanes] = pull(store, 19 + j, t, xb, lane)
+
+    copies.append(pltpu.make_async_copy(heat, heat_out, sems.at[2]))
+    copies[-1].start()
+    for copy in copies:
+        copy.wait()
 
 
 def body(
@@ -817,13 +919,18 @@
         brick_ids.reshape(2, 128),
         brick_links.T,
     )
-    second, brick = pl.pallas_call(
+    results = pl.pallas_call(
         steps_kernel,
-        out_shape=[pltpu.VMEM((26, TALL, 128), F32), shape((2, 512), F32)],
+        out_shape=[
+            pltpu.VMEM(flow_pops.shape, F32),
+            pltpu.VMEM((7, TALL, 128), F32),
+            pltpu.VMEM(brick_temp.shape, F32),
+        ],
         in_specs=[far] * 9,
-        out_specs=[near] * 2,
+        out_specs=[near] * 3,
         scratch_shapes=[
             pltpu.VMEM((26, TALL, 128), F32),
+            pltpu.VMEM((19, TALL, 128), F32),
             pltpu.VMEM(flow_pops.shape, F32),
             pltpu.VMEM(heat_pops.shape, F32),
             pltpu.VMEM(solid_flag.shape, I32),
@@ -835,6 +942,7 @@
             pltpu.VMEM((6, 256), I32),
             pltpu.VMEM((8, 128, 128), F32),
             pltpu.VMEM((8, 128, 128), F32),
+            pltpu.VMEM((128, 128), F32),
             pltpu.VMEM((128, 128), F32),
             pltpu.VMEM((128, 256), F32),
             pltpu.VMEM((256, 128), F32),
@@ -852,13 +960,13 @@
             pltpu.VMEM((SLOTS, 256), BF16),
             pltpu.VMEM((CAP, 128), F32),
             pltpu.VMEM((CAP, 128), F32),
-            pltpu.VMEM((128, 128), F32),
+            pltpu.VMEM((3, 128, 128), F32),
+            pltpu.VMEM((8, 128), F32),
             pltpu.VMEM((16, 128), F32),
-            pltpu.VMEM((16, 128), F32),
-            pltpu.VMEM((2, GY * 32, 128), F32),
-            pltpu.VMEM((2, GY * 32, 128), F32),
-            pltpu.VMEM((2, GX * 24, 128), F32),
-            pltpu.VMEM((2, GX * 24, 128), F32),
+            pltpu.VMEM((3, 8 * 24, 128), F32),
+            pltpu.VMEM((3, 8 * 24, 128), F32),
+            pltpu.VMEM((3, 16 * 16, 128), F32),
+            pltpu.VMEM((3, 16 * 16, 128), F32),
             pltpu.VMEM((2, 2, 80, 128), F32),
             pltpu.VMEM((2, 2, 80, 128), F32),
             pltpu.VMEM((2, 2, 64, 128), F32),
@@ -870,31 +978,31 @@
             pltpu.VMEM((2, 2, 32, 128), F32),
             pltpu.VMEM((2, 2, 32, 128), F32),
             dma((9,)),
-            dma((2, GY)),
-            dma((2, GY)),
-            dma((2, GX)),
-            dma((2, GX)),
+            dma((3, 8)),
+            dma((3, 8)),
+            dma((3, 16)),
+            dma((3, 16)),
             dma((2, 8)),
             dma((2, 8)),
             dma((2, 4)),
             dma((2, 4)),
         ],
         compiler_params=pltpu.CompilerParams(
-            collective_id=0, has_side_effects=True, vmem_limit_bytes=40 << 20
+            collective_id=0, has_side_effects=True, vmem_limit_bytes=46 << 20
         ),
     )(*(pltpu.with_memory_space_constraint(value, pltpu.HBM) for value in inputs))
-    width = 256
-    flow, heat = pl.pallas_call(
-        spread_kernel,
-        grid=(TILES * 128 // width,),
-        out_shape=[shape(flow_pops.shape, F32), shape(heat_pops.shape, F32)],
-        in_specs=[near],
-        out_specs=[
-            pl.BlockSpec((19, ROWS, width), lambda i: (0, 0, i)),
-            pl.BlockSpec((7, ROWS, width), lambda i: (0, 0, i)),
+    flow, heat, brick = pl.pallas_call(
+        hand_out_kernel,
+        out_shape=[
+            shape(flow_pops.shape, F32),
+            shape(heat_pops.shape, F32),
+            shape(brick_temp.shape, F32),
         ],
-        compiler_params=pltpu.CompilerParams(vmem_limit_bytes=16 << 20),
-    )(second)
+        in_specs=[near] * 3,
+        out_specs=[far] * 3,
+        scratch_shapes=[pltpu.VMEM(heat_pops.shape, F32), dma((3,))],
+        compiler_params=pltpu.CompilerParams(vmem_limit_bytes=8 << 20),
+    )(*results)
     return flow, heat, brick
 
 

time: 52.2 us -> 46.5 us (0.89)
  Pallas kernels: 50.8 us -> 45.8 us
  local copies, waits for them, and re-layouts: 0.59 us -> 0 us
    pallas_call x2, Pallas kernels: 50.8 us -> 45.8 us  [the longest x1 42.9 us: body(): pl.pallas_call(steps_kernel, out_shape=[pltpu.VMEM(flow_pops.shape, F32),...]
    unnamed x1 -> x0, local copies, waits for them, and re-layouts: 0.59 us -> none
where the time goes in v4:
time: 46.5 us; the launch traced here: 46.4 us
  Pallas kernels  45.8 us (98%)
  between operations  0.64 us (1%)
    pallas_call x1, Pallas kernels, body(): pl.pallas_call(steps_kernel, out_shape=[pltpu.VMEM(flow_pops.shape, F32),...  42.9 us
    pallas_call x1, Pallas kernels, body(): pl.pallas_call(hand_out_kernel, out_shape=[shape(flow_pops.shape, F32), s...  2.9 us

profile of v4, /device:TPU:1, one launch (start us, length us, event | category | flops | bytes accessed | tf_op | source)
XLA Modules:
  0.0 46.4 jit_solution(39103674511904296)
XLA Ops:
  0.6 42.9 %shard_map.112 = (f32[19,32,2048]{2,1,0:T(8,128)S(1)}, f32[7,864,128]{2,1,0:T(8,128)S(1)}, f32[2,512]{1,0:T(2,128)S(1)}) custom-call(f32[19,32,2048]{2,1,0:T(8,128)} %flow_in.1, f32[7,32,2048]{2,1,0:T(8,128)} %heat_in.1, s32[32,2048]{1,0:T(8,128)} %solid_in.1, s32[1024,128]{1,0:T(8,128)} %bitcast.5, s32[1024,128]{1,0:T(8,128)} %bitcast.6, ...), custom_call_target="tpu_custom_call" | custom-call | tf_op jit(solution)/shard_map/pallas_call | solution.py:922
  43.5 2.9 %shard_map.113 = (f32[19,32,2048]{2,1,0:T(8,128)}, f32[7,32,2048]{2,1,0:T(8,128)}, f32[2,512]{1,0:T(2,128)}) custom-call(f32[19,32,2048]{2,1,0:T(8,128)S(1)} %get-tuple-element.6.flow, f32[7,864,128]{2,1,0:T(8,128)S(1)} %get-tuple-element.7.second_heat, f32[2,512]{1,0:T(2,128)S(1)} %get-tuple-element.8.brick), custom_call_target="tpu_custom_call" | custom-call | tf_op jit(solution)/shard_map/pallas_call | solution.py:994

commit v5 on v4

--- a/solution.py
+++ b/solution.py
@@ -114,6 +114,16 @@
             size = min(128, count)
             part = iota((size, 128), 0) + q == row[r : r + 1, :]
             onehot[q : q + size, r * 128 : (r + 1) * 128] = jnp.where(part, 1.0, 0.0).astype(BF16)
+
+
+def fill_edges(row, onehot):
+    n = iota((96, 128), 0)
+    last = n - 32 + (TILES - 1) * ROWS
+    sides = jnp.where(n < 80, (n - 64) * ROWS, (n - 80) * ROWS + ROWS - 1)
+    wanted = jnp.where(n < 32, n, jnp.where(n < 64, last, sides))
+    for r in range(CAP):
+        part = wanted == row[r : r + 1, :]
+        onehot[:, r * 128 : (r + 1) * 128] = jnp.where(part, 1.0, 0.0).astype(BF16)
 
 
 def ranked(device):
@@ -274,7 +284,7 @@
     return high, (value - high.astype(F32)).astype(BF16)
 
 
-def scatter(onehot, columns, flux, spread):
+def fill_spread(columns, flux, spread):
     high, low = halves(flux)
     high, low = high.astype(F32), low.astype(F32)
     at = iota((128, 128), 1)
@@ -283,6 +293,9 @@
         rows = slice(r * 128, (r + 1) * 128)
         spread[rows, 0:128] = jnp.where(hit, high[:, r : r + 1], 0.0).astype(BF16)
         spread[rows, 128:256] = jnp.where(hit, low[:, r : r + 1], 0.0).astype(BF16)
+
+
+def gather_spread(onehot, spread):
     both = jnp.dot(onehot[...], spread[...], preferred_element_type=F32)
     return both[:, :128] + both[:, 128:]
 
@@ -356,7 +369,11 @@
     links_in,
     flow_out,
     second_heat,
-    brick_out,
+    brick,
+    lost,
+    layers,
+    blcol,
+    oh_brick,
     first,
     second_flow,
     flow,
@@ -376,21 +393,19 @@
     by_slot,
     pick,
     oh_cell,
-    oh_brick,
+    oh_edge,
     arow,
     lrow,
     lcol,
     brow,
     blrow,
-    blcol,
     temps,
     gain,
+    edge,
     spread,
     found,
-    asked,
     msg,
     faces,
-    brick,
     s1,
     r1,
     s2,
@@ -439,6 +454,14 @@
     def yn(k):
         return lax.rem(y + (k + GY), GY)
 
+    barrier = pltpu.get_barrier_semaphore()
+    peers = [(xn(a), yn(b)) for a in (-1, 1) for b in (-1, 1)]
+    peers += [outer_peer(outer_next(k)) for k in (10, 6, 2, 14, 9, 11, 5, 7, 1, 3, 13, 15, 8, 4, 12)]
+    peers += [(xn(a), yn(b)) for a, b in ((-1, 0), (1, 0), (0, -1), (0, 1))]
+    peers += [inner_peer(inner_next(k)) for k in range(1, 8)]
+    for peer in peers:
+        pl.semaphore_signal(barrier, inc=1, device_id=peer, device_id_type=MESH)
+
     second = Lattice(second_flow, second_heat)
     own_faces = pl.ds(pl.multiple_of(me * 8, 8), 8)
     loads = {}
@@ -446,8 +469,8 @@
         (
             ("owners", owners_in, owners),
             ("cells", cells_in.at[own_faces, :], cells),
+            ("heat", heat_in, heat),
             ("spots", spots_in, spots),
-            ("heat", heat_in, heat),
             ("brick", brick_in, brick_flat),
             ("ids", ids_in, ids),
             ("links", links_in, links),
@@ -456,14 +479,8 @@
         )
     ):
         loads[name] = pltpu.make_async_copy(source, target, load_sem.at[n])
-        loads[name].start()
-
-    barrier = pltpu.get_barrier_semaphore()
-    peers = [inner_peer(inner_next(k)) for k in range(1, 8)]
-    peers += [outer_peer(outer_next(k)) for k in range(1, 16)]
-    peers += [(xn(a), yn(b)) for a in (-1, 0, 1) for b in (-1, 0, 1) if a or b]
-    for peer in peers:
-        pl.semaphore_signal(barrier, inc=1, device_id=peer, device_id_type=MESH)
+        if name not in ("solid", "flow"):
+            loads[name].start()
 
     lane = iota((8, 128), 1)
 
@@ -509,20 +526,16 @@
             look_up_row(row, outs, u, a, low)
         return (outs[0] + outs[1]) + (outs[2] + outs[3])
 
-    def ask():
-        now = brick[...]
-        asked[...] = brick_lookup(now, brow[...], blrow[...])
-        store_faces(now, faces)
-
-    def fill_message(n, temperatures, bricks):
-        none = jnp.zeros((CAP, 128), F32)
-        parts = [found[...] if temperatures else none, asked[...] if bricks else none]
-        rest = jnp.zeros((128 - 2 * CAP, 128), F32)
-        msg[n] = jnp.transpose(jnp.concatenate(parts + [rest], axis=0))
+    def fill_message(n, value):
+        rest = jnp.zeros((128 - CAP, 128), F32)
+        msg[n] = jnp.transpose(jnp.concatenate([value, rest], axis=0))
+
+    def ask_bricks(n):
+        fill_message(n, brick_lookup(brick[...], brow[...], blrow[...]))
 
 
     def one(n, k, to, slot):
-        count = 16 if n == 2 else 24
+        count = 16 if n % 2 else 24
         return pltpu.make_async_remote_copy(
             src_ref=s1.at[n, pl.ds(pl.multiple_of(to * 24, 8), count), :],
             dst_ref=r1.at[n, pl.ds(pl.multiple_of(slot * 24, 8), count), :],
@@ -533,7 +546,7 @@
         )
 
     def two(n, k, to, slot):
-        count = 8 if n == 2 else 16
+        count = 8 if n % 2 else 16
         return pltpu.make_async_remote_copy(
             src_ref=s2.at[n, pl.ds(pl.multiple_of(to * 16, 8), count), :],
             dst_ref=r2.at[n, pl.ds(pl.multiple_of(slot * 16, 8), count), :],
@@ -546,7 +559,7 @@
     def start_one(n):
         for k in range(8):
             s1[n, k * 24 : k * 24 + 16, :] = msg[n, pl.ds(k, 16, stride=8), :]
-            if n < 2:
+            if n % 2 == 0:
                 s1[n, k * 24 + 16 : k * 24 + 24, :] = faces[...]
         for k in range(1, 8):
             one(n, k, inner_next(k), inner).start()
@@ -558,7 +571,7 @@
             one(n, k, inner_next(k), inner_next(k)).wait_recv()
 
     def start_two(n):
-        if n < 2:
+        if n % 2 == 0:
             every = jnp.concatenate(
                 [r1[n, k * 24 + 16 : k * 24 + 24, :] for k in range(8)], axis=0
             )
@@ -596,9 +609,12 @@
     def arrived(n):
         return jnp.concatenate([r2[n, h * 16 : h * 16 + 8, :] for h in range(16)], axis=0)
 
-    def heat_faces(store, came, mine):
-        flux = WALL_COEF * (pltpu.roll(arrived(came), 128 - CAP, 1) - msg[mine])
-        gain[...] = scatter(oh_cell, lcol[...], flux, spread)
+    def heat_sides(bricks, fluid):
+        fill_spread(lcol[...], WALL_COEF * (arrived(bricks) - msg[fluid]), spread)
+        edge[...] = gather_spread(oh_edge, spread)
+
+    def heat_faces(store):
+        gain[...] = gather_spread(oh_cell, spread)
 
         @pl.loop(0, TILES)
         def _(t):
@@ -608,13 +624,16 @@
                 for j in range(7):
                     store[19 + j, rows, :] = store[19 + j, rows, :] + WEIGHTS_HEAT[j] * more
 
-    def cool_bricks(came, mine, layers):
-        flux = WALL_COEF * (pltpu.roll(msg[mine], 128 - CAP, 1) - arrived(came))
-        loss = scatter(oh_brick, blcol[...], flux, spread)
-        ghost = r2[layers, 8:16, :]
+    def ghosts(n):
+        ghost = r2[n, 8:16, :]
         for h in range(1, 16):
-            ghost = ghost + r2[layers, h * 16 + 8 : h * 16 + 16, :]
-        brick[...] = conduct(brick[...], ghost, loss)
+            ghost = ghost + r2[n, h * 16 + 8 : h * 16 + 16, :]
+        return ghost
+
+    def cool_bricks(bricks, fluid, layers):
+        fill_spread(blcol[...], WALL_COEF * (msg[bricks] - arrived(fluid)), spread)
+        loss = gather_spread(oh_brick, spread)
+        brick[...] = conduct(brick[...], ghosts(layers), loss)
 
 
     ways = [(1, 0), (-1, 0), (0, 1), (0, -1)]
@@ -699,9 +718,11 @@
     def send_heat_halo(step, store):
         for n in range(2):
             rows = pl.ds(PITCH + leave_row[n], 16, stride=PITCH)
-            xh[step, n] = store[SIDES[n][1], rows, :]
+            more = WEIGHTS_HEAT[1] * edge[80 - 16 * n : 96 - 16 * n, :]
+            xh[step, n] = store[SIDES[n][1], rows, :] + more
             top = leave_tile[n] * PITCH + 8
-            yh[step, n] = store[SIDES[2 + n][1], top : top + 32, :]
+            more = WEIGHTS_HEAT[1] * edge[32 - 32 * n : 64 - 32 * n, :]
+            yh[step, n] = store[SIDES[2 + n][1], top : top + 32, :] + more
         for copy in heat_copies(step):
             copy.start()
 
@@ -732,13 +753,34 @@
                 g = [heat[j, rows, lanes] for j in range(7)]
                 store_relaxed(first, t, xb, f, g)
 
-    def relax_second(low, high):
-        @pl.loop(low, high)
-        def _(t):
+    def relax_second(t, xb):
+        f = [pull(first, i, t, xb, lane) for i in range(19)]
+        g = [pull(first, 19 + j, t, xb, lane) for j in range(7)]
+        store_relaxed(second, t, xb, f, g)
+
+    def hand_flow(t, xb):
+        rows, lanes = natural(t, xb)
+        for i in range(19):
+            flow_out[i, rows, lanes] = pull(second, i, t, xb, lane)
+
+    def along_sides(act):
+        @pl.loop(0, (TILES - 2) // 2)
+        def _(n):
+            for u in range(2):
+                for xb in (0, 3):
+                    act(1 + 2 * n + u, xb)
+
+        @pl.loop(0, 2)
+        def _(n):
             for xb in range(4):
-                f = [pull(first, i, t, xb, lane) for i in range(19)]
-                g = [pull(first, 19 + j, t, xb, lane) for j in range(7)]
-                store_relaxed(second, t, xb, f, g)
+                act(n * (TILES - 1), xb)
+
+    def inside_sides(act):
+        @pl.loop(0, (TILES - 2) // 2)
+        def _(n):
+            for u in range(2):
+                for xb in (1, 2):
+                    act(1 + 2 * n + u, xb)
 
     def sum_heat(g):
         return g[0] + ((g[1] + g[2]) + (g[3] + g[4]) + (g[5] + g[6]))
@@ -768,6 +810,29 @@
     arow[...] = a
     lrow[...] = jnp.where(live, low, 0)
 
+
+    loads["heat"].wait()
+    loads["solid"].start()
+    loads["flow"].start()
+
+    @pl.loop(0, TILES // 2)
+    def _(n):
+        for u in range(2):
+            for xb in range(4):
+                rows, lanes = natural(n * 2 + u, xb)
+                temps[temp_rows(n * 2 + u, xb), :] = sum_heat(
+                    [heat[j, rows, lanes] for j in range(7)]
+                )
+
+    fill_onehots(arow[...], oh_cell)
+    look_up(False)
+    fill_message(0, found[...])
+    loads["brick"].wait()
+    brick[...] = to_rows(brick_flat[...])
+    store_faces(brick[...], faces)
+    pl.semaphore_wait(barrier, len(peers))
+    start_one(0)
+
     loads["spots"].wait()
 
     def from_device(b):
@@ -785,42 +850,32 @@
     brow[...] = a
     blrow[...] = jnp.where(live, low, 0)
 
-
-    loads["heat"].wait()
-
-    @pl.loop(0, TILES)
-    def _(t):
-        for xb in range(4):
-            rows, lanes = natural(t, xb)
-            temps[temp_rows(t, xb), :] = sum_heat([heat[j, rows, lanes] for j in range(7)])
-
-    fill_onehots(arow[...], oh_cell)
-    look_up(False)
-    loads["brick"].wait()
-    brick[...] = to_rows(brick_flat[...])
-    ask()
-    fill_message(0, True, True)
-    pl.semaphore_wait(barrier, len(peers))
-    start_one(0)
+    ask_bricks(1)
+    start_one(1)
     loads["ids"].wait()
     loads["links"].wait()
     place = (core, xc, ylo, q, inner, outer)
     fill_pick(place, ids[...], links[...], wide, by_slot, pick)
+    end_one(0)
+    start_two(0)
     fill_onehots(brow[...], oh_brick)
+    fill_edges(arow[...], oh_edge)
     loads["solid"].wait()
     loads["flow"].wait()
-    relax_first(0, TILES // 4)
-    end_one(0)
-    start_two(0)
-    relax_first(TILES // 4, TILES)
+    relax_first(0, 2)
+    end_one(1)
+    start_two(1)
+    relax_first(2, TILES)
     send_flow_halo(0, first)
     end_two(0)
-    heat_faces(first, 0, 0)
+    cool_bricks(1, 0, 0)
+    store_faces(brick[...], faces)
+    ask_bricks(2)
+    start_one(2)
+    end_two(1)
+    heat_sides(1, 0)
     send_heat_halo(0, first)
-    cool_bricks(0, 0, 0)
-    ask()
-    fill_message(1, False, True)
-    start_one(1)
+    heat_faces(first)
 
 
     @pl.loop(0, (TILES - 2) // 2)
@@ -830,51 +885,56 @@
                 pulled_temp(1 + 2 * n + u, xb)
 
     look_up(True)
-    end_one(1)
-    start_two(1)
+    end_one(2)
+    start_two(2)
     end_heat_halo(0, first)
     for t in range(TILES):
         for xb in range(4):
             if t in (0, TILES - 1) or xb in (0, 3):
                 pulled_temp(t, xb)
-    found[...] = found[...] + look_up_edges()
-    fill_message(2, True, False)
-    start_one(2)
+    fill_message(3, found[...] + look_up_edges())
+    start_one(3)
     end_flow_halo(0, first)
-    relax_second(0, 8)
-    end_one(2)
-    start_two(2)
-    relax_second(8, TILES)
+    along_sides(relax_second)
     send_flow_halo(1, second)
-    end_two(1)
-    heat_faces(second, 1, 2)
+    end_one(3)
+    start_two(3)
+    inside_sides(relax_second)
+    end_two(2)
+    heat_sides(2, 3)
     send_heat_halo(1, second)
+    heat_faces(second)
+    inside_sides(hand_flow)
+    for n in range(3):
+        end_sends(n)
     end_flow_halo(1, second)
-
-    @pl.loop(0, TILES)
-    def _(t):
-        for xb in range(4):
-            for i in range(19):
-                rows, lanes = natural(t, xb)
-                flow_out[i, rows, lanes] = pull(second, i, t, xb, lane)
-
-    end_sends(0)
-    end_sends(1)
-    end_two(2)
-    cool_bricks(2, 1, 1)
-    from_rows(brick[...], brick_out)
-    end_sends(2)
+    along_sides(hand_flow)
+    end_two(3)
+    lost[...] = WALL_COEF * (msg[2] - arrived(3))
+    layers[...] = ghosts(2)
+    end_sends(3)
     end_heat_halo(1, second)
 
 
-def hand_out_kernel(flow, second_heat, brick, flow_out, heat_out, brick_out, heat, sems):
+def hand_out_kernel(
+    flow,
+    second_heat,
+    brick,
+    lost,
+    layers,
+    blcol,
+    oh_brick,
+    flow_out,
+    heat_out,
+    brick_out,
+    heat,
+    flat,
+    spread,
+    sems,
+):
     lane = iota((8, 128), 1)
-    copies = [
-        pltpu.make_async_copy(flow, flow_out, sems.at[0]),
-        pltpu.make_async_copy(brick, brick_out, sems.at[1]),
-    ]
-    for copy in copies:
-        copy.start()
+    copies = [pltpu.make_async_copy(flow, flow_out, sems.at[0])]
+    copies[-1].start()
     store = Lattice(None, second_heat)
 
     @pl.loop(0, TILES // 4)
@@ -886,7 +946,12 @@
                     rows, lanes = natural(t, xb)
                     heat[j, rows, lanes] = pull(store, 19 + j, t, xb, lane)
 
-    copies.append(pltpu.make_async_copy(heat, heat_out, sems.at[2]))
+    copies.append(pltpu.make_async_copy(heat, heat_out, sems.at[1]))
+    copies[-1].start()
+    fill_spread(blcol[...], lost[...], spread)
+    loss = gather_spread(oh_brick, spread)
+    from_rows(conduct(brick[...], layers[...], loss), flat)
+    copies.append(pltpu.make_async_copy(flat, brick_out, sems.at[2]))
     copies[-1].start()
     for copy in copies:
         copy.wait()
@@ -924,10 +989,14 @@
         out_shape=[
             pltpu.VMEM(flow_pops.shape, F32),
             pltpu.VMEM((7, TALL, 128), F32),
-            pltpu.VMEM(brick_temp.shape, F32),
+            pltpu.VMEM((16, 128), F32),
+            pltpu.VMEM((128, 128), F32),
+            pltpu.VMEM((8, 128), F32),
+            pltpu.VMEM((128, 128), I32),
+            pltpu.VMEM((16, SLOTS), BF16),
         ],
         in_specs=[far] * 9,
-        out_specs=[near] * 3,
+        out_specs=[near] * 7,
         scratch_shapes=[
             pltpu.VMEM((26, TALL, 128), F32),
             pltpu.VMEM((19, TALL, 128), F32),
@@ -948,25 +1017,23 @@
             pltpu.VMEM((256, 128), F32),
             pltpu.VMEM((192, 128), BF16),
             pltpu.VMEM((TILES * ROWS, SLOTS), BF16),
-            pltpu.VMEM((16, SLOTS), BF16),
+            pltpu.VMEM((96, SLOTS), BF16),
             pltpu.VMEM((CAP, 128), I32),
             pltpu.VMEM((CAP, 128), I32),
             pltpu.VMEM((128, 128), I32),
             pltpu.VMEM((CAP, 128), I32),
             pltpu.VMEM((CAP, 128), I32),
-            pltpu.VMEM((128, 128), I32),
             pltpu.VMEM(grid, F32),
             pltpu.VMEM(grid, F32),
+            pltpu.VMEM((96, 128), F32),
             pltpu.VMEM((SLOTS, 256), BF16),
             pltpu.VMEM((CAP, 128), F32),
-            pltpu.VMEM((CAP, 128), F32),
-            pltpu.VMEM((3, 128, 128), F32),
+            pltpu.VMEM((4, 128, 128), F32),
             pltpu.VMEM((8, 128), F32),
-            pltpu.VMEM((16, 128), F32),
-            pltpu.VMEM((3, 8 * 24, 128), F32),
-            pltpu.VMEM((3, 8 * 24, 128), F32),
-            pltpu.VMEM((3, 16 * 16, 128), F32),
-            pltpu.VMEM((3, 16 * 16, 128), F32),
+            pltpu.VMEM((4, 8 * 24, 128), F32),
+            pltpu.VMEM((4, 8 * 24, 128), F32),
+            pltpu.VMEM((4, 16 * 16, 128), F32),
+            pltpu.VMEM((4, 16 * 16, 128), F32),
             pltpu.VMEM((2, 2, 80, 128), F32),
             pltpu.VMEM((2, 2, 80, 128), F32),
             pltpu.VMEM((2, 2, 64, 128), F32),
@@ -978,10 +1045,10 @@
             pltpu.VMEM((2, 2, 32, 128), F32),
             pltpu.VMEM((2, 2, 32, 128), F32),
             dma((9,)),
-            dma((3, 8)),
-            dma((3, 8)),
-            dma((3, 16)),
-            dma((3, 16)),
+            dma((4, 8)),
+            dma((4, 8)),
+            dma((4, 16)),
+            dma((4, 16)),
             dma((2, 8)),
             dma((2, 8)),
             dma((2, 4)),
@@ -998,9 +1065,14 @@
             shape(heat_pops.shape, F32),
             shape(brick_temp.shape, F32),
         ],
-        in_specs=[near] * 3,
+        in_specs=[near] * 7,
         out_specs=[far] * 3,
-        scratch_shapes=[pltpu.VMEM(heat_pops.shape, F32), dma((3,))],
+        scratch_shapes=[
+            pltpu.VMEM(heat_pops.shape, F32),
+            pltpu.VMEM(brick_temp.shape, F32),
+            pltpu.VMEM((SLOTS, 256), BF16),
+            dma((3,)),
+        ],
         compiler_params=pltpu.CompilerParams(vmem_limit_bytes=8 << 20),
     )(*results)
     return flow, heat, brick

time: 46.5 us -> 42.6 us (0.916)
  Pallas kernels: 45.8 us -> 41.9 us
    pallas_call x1, Pallas kernels: 42.9 us -> 39 us  [body(): pl.pallas_call(steps_kernel, out_shape=[pltpu.VMEM(flow_pops.shape, F32),...]
where the time goes in v5:
time: 42.6 us; the launch traced here: 42.5 us
  Pallas kernels  41.9 us (98%)
  between operations  0.64 us (2%)
    pallas_call x1, Pallas kernels, body(): pl.pallas_call(steps_kernel, out_shape=[pltpu.VMEM(flow_pops.shape, F32),...  39 us
    pallas_call x1, Pallas kernels, body(): pl.pallas_call(hand_out_kernel, out_shape=[shape(flow_pops.shape, F32), s...  2.9 us

profile of v5, /device:TPU:1, one launch (start us, length us, event | category | flops | bytes accessed | tf_op | source)
XLA Modules:
  0.0 42.5 jit_solution(9099864694331740330)
XLA Ops:
  0.6 39.0 %shard_map.112 = (f32[19,32,2048]{2,1,0:T(8,128)S(1)}, f32[7,864,128]{2,1,0:T(8,128)S(1)}, f32[16,128]{1,0:T(8,128)S(1)}, f32[128,128]{1,0:T(8,128)S(1)}, f32[8,...) custom-call(f32[19,32,2048]{2,1,0:T(8,128)} %flow_in.1, f32[7,32,2048]{2,1,0:T(8,128)} %heat_in.1, ...), custom_call_target="tpu_custom_call" | custom-call | tf_op jit(solution)/shard_map/pallas_call | solution.py:987
  39.6 2.9 %shard_map.113 = (f32[19,32,2048]{2,1,0:T(8,128)}, f32[7,32,2048]{2,1,0:T(8,128)}, f32[2,512]{1,0:T(2,128)}) custom-call(f32[19,32,2048]{2,1,0:T(8,128)S(1)} %get-tuple-element.10.flow, f32[7,864,128]{2,1,0:T(8,128)S(1)} %get-tuple-element.11.second_heat, f32[16,128]{1,0:T(8,128)S(1)} %get-tuple-element.12.brick, f32[128,128]{1,0:T(8,128)S(1)} %get-tuple-element.13.lost, ...), custom_call_target="tpu_custom_call" | custom-call | tf_op jit(solution)/shard_map/pallas_call | solution.py:1061

commit v6 on v5

--- a/solution.py
+++ b/solution.py
@@ -94,6 +94,33 @@
     return packed[...]
 
 
+def compact_own(place, cell):
+    square = (128, 128)
+    wide_row, wide_lane = iota((128, 256), 0), iota((128, 256), 1)
+    prefix = jnp.where(wide_row <= wide_lane, 1.0, 0.0).astype(BF16)
+    device, rank = iota(square, 0), iota((CAP, 128), 0).astype(F32) + 1.0
+    before = jnp.zeros(square, F32)
+    masks, values = [], []
+    for b in range(8):
+        mask = device == place[b : b + 1, :]
+        masks.append(jnp.where(mask, 1.0, 0.0).astype(BF16))
+        counts = jnp.dot(masks[-1], prefix, preferred_element_type=F32)
+        own = jnp.where(mask, counts[:, :128] + before, 0.0)
+        before = before + counts[:, 128:]
+        match = rank == jnp.sum(own, axis=0, keepdims=True)
+        high = (cell[b : b + 1, :] >> 8).astype(F32)
+        low = (cell[b : b + 1, :] & 255).astype(F32)
+        both = [jnp.where(match, high, 0.0), jnp.where(match, low, 0.0)]
+        values.append(jnp.concatenate(both, axis=0).astype(BF16))
+    out = lax.dot_general(
+        jnp.concatenate(values, axis=1),
+        jnp.concatenate(masks, axis=1),
+        (((1,), (1,)), ((), ())),
+        preferred_element_type=F32,
+    )
+    return out[:CAP] * 256.0 + out[CAP:]
+
+
 def split_cell(c):
     c = c.astype(I32) - 1
     live = c >= 0
@@ -208,11 +235,14 @@
     k0 = density * (1.0 / 3.0 / TAU_FLOW)
     out_f[0] = jnp.where(solid, f[0], keep * f[0] + k0 * base)
     scale = {1: density * (1.0 / 18.0 / TAU_FLOW), 7: density * (1.0 / 36.0 / TAU_FLOW)}
+    level = {a: k * base for a, k in scale.items()}
+    bend = {a: 4.5 * k for a, k in scale.items()}
+    lean = {a: 3.0 * k for a, k in scale.items()}
     for a, b in pairs:
-        k = scale[1 if a < 7 else 7]
+        kind = 1 if a < 7 else 7
         along = along_of[a]
-        even = k * (base + 4.5 * (along * along))
-        odd = (3.0 * k) * along
+        even = level[kind] + bend[kind] * (along * along)
+        odd = lean[kind] * along
         out_f[a] = jnp.where(solid, f[b], (even + odd) + keep * f[a])
         out_f[b] = jnp.where(solid, f[a], (even - odd) + keep * f[b])
     keep = 1.0 - 1.0 / TAU_HEAT
@@ -454,14 +484,6 @@
     def yn(k):
         return lax.rem(y + (k + GY), GY)
 
-    barrier = pltpu.get_barrier_semaphore()
-    peers = [(xn(a), yn(b)) for a in (-1, 1) for b in (-1, 1)]
-    peers += [outer_peer(outer_next(k)) for k in (10, 6, 2, 14, 9, 11, 5, 7, 1, 3, 13, 15, 8, 4, 12)]
-    peers += [(xn(a), yn(b)) for a, b in ((-1, 0), (1, 0), (0, -1), (0, 1))]
-    peers += [inner_peer(inner_next(k)) for k in range(1, 8)]
-    for peer in peers:
-        pl.semaphore_signal(barrier, inc=1, device_id=peer, device_id_type=MESH)
-
     second = Lattice(second_flow, second_heat)
     own_faces = pl.ds(pl.multiple_of(me * 8, 8), 8)
     loads = {}
@@ -481,6 +503,14 @@
         loads[name] = pltpu.make_async_copy(source, target, load_sem.at[n])
         if name not in ("solid", "flow"):
             loads[name].start()
+
+    barrier = pltpu.get_barrier_semaphore()
+    peers = [(xn(a), yn(b)) for a in (-1, 1) for b in (-1, 1)]
+    peers += [outer_peer(outer_next(k)) for k in (10, 6, 2, 14, 9, 11, 5, 7, 1, 3, 13, 15, 8, 4, 12)]
+    peers += [(xn(a), yn(b)) for a, b in ((-1, 0), (1, 0), (0, -1), (0, 1))]
+    peers += [inner_peer(inner_next(k)) for k in range(1, 8)]
+    for peer in peers:
+        pl.semaphore_signal(barrier, inc=1, device_id=peer, device_id_type=MESH)
 
     lane = iota((8, 128), 1)
 
@@ -789,24 +819,15 @@
         temps[temp_rows(t, xb), :] = sum_heat([pull(first, 19 + j, t, xb, lane) for j in range(7)])
 
 
-    square = (128, 128)
     loads["owners"].wait()
     loads["cells"].wait()
-    row_index = iota(square, 0)
-    own_place = ranked(owners[own_faces, :])
-    own_cell = cells[...].astype(F32) + 1.0
-    table = compact(
-        lambda b: (
-            row_index == own_place[b : b + 1, :],
-            jnp.broadcast_to(own_cell[b : b + 1, :], square),
-        ),
-        key,
-        val,
-        packed,
+    by_rank = compact_own(ranked(owners[own_faces, :]), cells[...] + 1)
+    table = jnp.transpose(
+        jnp.concatenate([by_rank, jnp.zeros((128 - CAP, 128), F32)], axis=0)
     )
     _, low, live = split_cell(table)
     lcol[...] = jnp.where(live, low, -1)
-    a, low, live = split_cell(jnp.transpose(table)[:CAP, :])
+    a, low, live = split_cell(by_rank)
     arow[...] = a
     lrow[...] = jnp.where(live, low, 0)
 
@@ -884,9 +905,9 @@
             for xb in range(4):
                 pulled_temp(1 + 2 * n + u, xb)
 
-    look_up(True)
     end_one(2)
     start_two(2)
+    look_up(True)
     end_heat_halo(0, first)
     for t in range(TILES):
         for xb in range(4):
@@ -933,8 +954,11 @@
     sems,
 ):
     lane = iota((8, 128), 1)
-    copies = [pltpu.make_async_copy(flow, flow_out, sems.at[0])]
-    copies[-1].start()
+    copies = []
+    for n in range(4):
+        part = pl.ds(n * 5, 5 if n < 3 else 4)
+        copies.append(pltpu.make_async_copy(flow.at[part], flow_out.at[part], sems.at[3 + n]))
+        copies[-1].start()
     store = Lattice(None, second_heat)
 
     @pl.loop(0, TILES // 4)
@@ -1071,7 +1095,7 @@
             pltpu.VMEM(heat_pops.shape, F32),
             pltpu.VMEM(brick_temp.shape, F32),
             pltpu.VMEM((SLOTS, 256), BF16),
-            dma((3,)),
+            dma((7,)),
         ],
         compiler_params=pltpu.CompilerParams(vmem_limit_bytes=8 << 20),
     )(*results)

time: 42.6 us -> 42 us (0.986)
  Pallas kernels: 41.9 us -> 41.2 us
    pallas_call x1, Pallas kernels: 39 us -> 38.3 us  [body(): pl.pallas_call(steps_kernel, out_shape=[pltpu.VMEM(flow_pops.shape, F32),...]
where the time goes in v6:
time: 42 us; the launch traced here: 41.9 us
  Pallas kernels  41.2 us (98%)
  between operations  0.64 us (2%)
    pallas_call x1, Pallas kernels, body(): pl.pallas_call(steps_kernel, out_shape=[pltpu.VMEM(flow_pops.shape, F32),...  38.3 us
    pallas_call x1, Pallas kernels, body(): pl.pallas_call(hand_out_kernel, out_shape=[shape(flow_pops.shape, F32), s...  2.94 us

profile of v6, /device:TPU:1, one launch (start us, length us, event | category | flops | bytes accessed | tf_op | source)
XLA Modules:
  0.0 41.9 jit_solution(16079449746650275234)
XLA Ops:
  0.6 38.3 %shard_map.112 = (f32[19,32,2048]{2,1,0:T(8,128)S(1)}, f32[7,864,128]{2,1,0:T(8,128)S(1)}, f32[16,128]{1,0:T(8,128)S(1)}, f32[128,128]{1,0:T(8,128)S(1)}, f32[8,...) custom-call(f32[19,32,2048]{2,1,0:T(8,128)} %flow_in.1, f32[7,32,2048]{2,1,0:T(8,128)} %heat_in.1, ...), custom_call_target="tpu_custom_call" | custom-call | tf_op jit(solution)/shard_map/pallas_call | solution.py:1011
  38.9 2.9 %shard_map.113 = (f32[19,32,2048]{2,1,0:T(8,128)}, f32[7,32,2048]{2,1,0:T(8,128)}, f32[2,512]{1,0:T(2,128)}) custom-call(f32[19,32,2048]{2,1,0:T(8,128)S(1)} %get-tuple-element.10.flow, f32[7,864,128]{2,1,0:T(8,128)S(1)} %get-tuple-element.11.second_heat, f32[16,128]{1,0:T(8,128)S(1)} %get-tuple-element.12.brick, f32[128,128]{1,0:T(8,128)S(1)} %get-tuple-element.13.lost, ...), custom_call_target="tpu_custom_call" | custom-call | tf_op jit(solution)/shard_map/pallas_call | solution.py:1085

commit v7 on v6

--- a/solution.py
+++ b/solution.py
@@ -564,24 +564,28 @@
         fill_message(n, brick_lookup(brick[...], brow[...], blrow[...]))
 
 
-    def one(n, k, to, slot):
+    def wait_all(buffer, n, rows, sem):
+        part = buffer.at[n, pl.ds(0, rows), :]
+        pltpu.make_async_copy(part, part, sem.at[n]).wait()
+
+    def one(n, to, slot):
         count = 16 if n % 2 else 24
         return pltpu.make_async_remote_copy(
             src_ref=s1.at[n, pl.ds(pl.multiple_of(to * 24, 8), count), :],
             dst_ref=r1.at[n, pl.ds(pl.multiple_of(slot * 24, 8), count), :],
-            send_sem=s1_send.at[n, k],
-            recv_sem=s1_recv.at[n, slot],
+            send_sem=s1_send.at[n],
+            recv_sem=s1_recv.at[n],
             device_id=inner_peer(to),
             device_id_type=MESH,
         )
 
-    def two(n, k, to, slot):
+    def two(n, to, slot):
         count = 8 if n % 2 else 16
         return pltpu.make_async_remote_copy(
             src_ref=s2.at[n, pl.ds(pl.multiple_of(to * 16, 8), count), :],
             dst_ref=r2.at[n, pl.ds(pl.multiple_of(slot * 16, 8), count), :],
-            send_sem=s2_send.at[n, k],
-            recv_sem=s2_recv.at[n, slot],
+            send_sem=s2_send.at[n],
+            recv_sem=s2_recv.at[n],
             device_id=outer_peer(to),
             device_id_type=MESH,
         )
@@ -592,13 +596,12 @@
             if n % 2 == 0:
                 s1[n, k * 24 + 16 : k * 24 + 24, :] = faces[...]
         for k in range(1, 8):
-            one(n, k, inner_next(k), inner).start()
+            one(n, inner_next(k), inner).start()
         own = pl.ds(pl.multiple_of(inner * 24, 8), 24)
         r1[n, own, :] = s1[n, own, :]
 
     def end_one(n):
-        for k in range(1, 8):
-            one(n, k, inner_next(k), inner_next(k)).wait_recv()
+        wait_all(r1, n, 7 * (16 if n % 2 else 24), s1_recv)
 
     def start_two(n):
         if n % 2 == 0:
@@ -622,19 +625,16 @@
         for h in range(16):
             s2[n, h * 16 : h * 16 + 8, :] = r1[n, pl.ds(h, 8, stride=24), :]
         for k in range(1, 16):
-            two(n, k, outer_next(k), outer).start()
+            two(n, outer_next(k), outer).start()
         own = pl.ds(pl.multiple_of(outer * 16, 8), 16)
         r2[n, own, :] = s2[n, own, :]
 
     def end_two(n):
-        for k in range(1, 16):
-            two(n, k, outer_next(k), outer_next(k)).wait_recv()
+        wait_all(r2, n, 15 * (8 if n % 2 else 16), s2_recv)
 
     def end_sends(n):
-        for k in range(1, 8):
-            one(n, k, inner_next(k), inner).wait_send()
-        for k in range(1, 16):
-            two(n, k, outer_next(k), outer).wait_send()
+        wait_all(s1, n, 7 * (16 if n % 2 else 24), s1_send)
+        wait_all(s2, n, 15 * (8 if n % 2 else 16), s2_send)
 
     def arrived(n):
         return jnp.concatenate([r2[n, h * 16 : h * 16 + 8, :] for h in range(16)], axis=0)
@@ -917,9 +917,9 @@
     start_one(3)
     end_flow_halo(0, first)
     along_sides(relax_second)
-    send_flow_halo(1, second)
     end_one(3)
     start_two(3)
+    send_flow_halo(1, second)
     inside_sides(relax_second)
     end_two(2)
     heat_sides(2, 3)
@@ -930,9 +930,9 @@
         end_sends(n)
     end_flow_halo(1, second)
     along_sides(hand_flow)
+    layers[...] = ghosts(2)
     end_two(3)
     lost[...] = WALL_COEF * (msg[2] - arrived(3))
-    layers[...] = ghosts(2)
     end_sends(3)
     end_heat_halo(1, second)
 
@@ -1069,10 +1069,10 @@
             pltpu.VMEM((2, 2, 32, 128), F32),
             pltpu.VMEM((2, 2, 32, 128), F32),
             dma((9,)),
-            dma((4, 8)),
-            dma((4, 8)),
-            dma((4, 16)),
-            dma((4, 16)),
+            dma((4,)),
+            dma((4,)),
+            dma((4,)),
+            dma((4,)),
             dma((2, 8)),
             dma((2, 8)),
             dma((2, 4)),

time: 42 us -> 40.3 us (0.960)
  Pallas kernels: 41.2 us -> 39.5 us
    pallas_call x1, Pallas kernels: 38.3 us -> 36.6 us  [body(): pl.pallas_call(steps_kernel, out_shape=[pltpu.VMEM(flow_pops.shape, F32),...]
where the time goes in v7:
time: 40.3 us; the launch traced here: 40.1 us
  Pallas kernels  39.5 us (98%)
  between operations  0.64 us (2%)
    pallas_call x1, Pallas kernels, body(): pl.pallas_call(steps_kernel, out_shape=[pltpu.VMEM(flow_pops.shape, F32),...  36.6 us
    pallas_call x1, Pallas kernels, body(): pl.pallas_call(hand_out_kernel, out_shape=[shape(flow_pops.shape, F32), s...  2.94 us

profile of v7, /device:TPU:1, one launch (start us, length us, event | category | flops | bytes accessed | tf_op | source)
XLA Modules:
  0.0 40.1 jit_solution(8662657308261392580)
XLA Ops:
  0.6 36.6 %shard_map.112 = (f32[19,32,2048]{2,1,0:T(8,128)S(1)}, f32[7,864,128]{2,1,0:T(8,128)S(1)}, f32[16,128]{1,0:T(8,128)S(1)}, f32[128,128]{1,0:T(8,128)S(1)}, f32[8,...) custom-call(f32[19,32,2048]{2,1,0:T(8,128)} %flow_in.1, f32[7,32,2048]{2,1,0:T(8,128)} %heat_in.1, ...), custom_call_target="tpu_custom_call" | custom-call | tf_op jit(solution)/shard_map/pallas_call | solution.py:1011
  37.2 2.9 %shard_map.113 = (f32[19,32,2048]{2,1,0:T(8,128)}, f32[7,32,2048]{2,1,0:T(8,128)}, f32[2,512]{1,0:T(2,128)}) custom-call(f32[19,32,2048]{2,1,0:T(8,128)S(1)} %get-tuple-element.10.flow, f32[7,864,128]{2,1,0:T(8,128)S(1)} %get-tuple-element.11.second_heat, f32[16,128]{1,0:T(8,128)S(1)} %get-tuple-element.12.brick, f32[128,128]{1,0:T(8,128)S(1)} %get-tuple-element.13.lost, ...), custom_call_target="tpu_custom_call" | custom-call | tf_op jit(solution)/shard_map/pallas_call | solution.py:1085

commit v8 on v7

--- a/solution.py
+++ b/solution.py
@@ -412,6 +412,7 @@
     owners,
     spots,
     cells,
+    own_owners,
     brick_flat,
     ids,
     links,
@@ -489,9 +490,10 @@
     loads = {}
     for n, (name, source, target) in enumerate(
         (
-            ("owners", owners_in, owners),
+            ("own", owners_in.at[own_faces, :], own_owners),
             ("cells", cells_in.at[own_faces, :], cells),
             ("heat", heat_in, heat),
+            ("owners", owners_in, owners),
             ("spots", spots_in, spots),
             ("brick", brick_in, brick_flat),
             ("ids", ids_in, ids),
@@ -819,9 +821,9 @@
         temps[temp_rows(t, xb), :] = sum_heat([pull(first, 19 + j, t, xb, lane) for j in range(7)])
 
 
-    loads["owners"].wait()
+    loads["own"].wait()
     loads["cells"].wait()
-    by_rank = compact_own(ranked(owners[own_faces, :]), cells[...] + 1)
+    by_rank = compact_own(ranked(own_owners[...]), cells[...] + 1)
     table = jnp.transpose(
         jnp.concatenate([by_rank, jnp.zeros((128 - CAP, 128), F32)], axis=0)
     )
@@ -854,6 +856,7 @@
     pl.semaphore_wait(barrier, len(peers))
     start_one(0)
 
+    loads["owners"].wait()
     loads["spots"].wait()
 
     def from_device(b):
@@ -1030,6 +1033,7 @@
             pltpu.VMEM((1024, 128), I32),
             pltpu.VMEM((1024, 128), I32),
             pltpu.VMEM((8, 128), I32),
+            pltpu.VMEM((8, 128), I32),
             pltpu.VMEM((2, 512), F32),
             pltpu.VMEM((2, 128), I32),
             pltpu.VMEM((6, 256), I32),
@@ -1068,7 +1072,7 @@
             pltpu.VMEM((2, 2, 16, 128), F32),
             pltpu.VMEM((2, 2, 32, 128), F32),
             pltpu.VMEM((2, 2, 32, 128), F32),
-            dma((9,)),
+            dma((10,)),
             dma((4,)),
             dma((4,)),
             dma((4,)),

time: 40.3 us -> 40.3 us (level)
  no operation moved by 1% of the time
where the time goes in v8:
time: 40.3 us; the launch traced here: 40.1 us
  Pallas kernels  39.5 us (98%)
  between operations  0.64 us (2%)
    pallas_call x1, Pallas kernels, body(): pl.pallas_call(steps_kernel, out_shape=[pltpu.VMEM(flow_pops.shape, F32),...  36.5 us
    pallas_call x1, Pallas kernels, body(): pl.pallas_call(hand_out_kernel, out_shape=[shape(flow_pops.shape, F32), s...  2.94 us

profile of v8, /device:TPU:1, one launch (start us, length us, event | category | flops | bytes accessed | tf_op | source)
XLA Modules:
  0.0 40.1 jit_solution(6938732699991609276)
XLA Ops:
  0.6 36.5 %shard_map.112 = (f32[19,32,2048]{2,1,0:T(8,128)S(1)}, f32[7,864,128]{2,1,0:T(8,128)S(1)}, f32[16,128]{1,0:T(8,128)S(1)}, f32[128,128]{1,0:T(8,128)S(1)}, f32[8,...) custom-call(f32[19,32,2048]{2,1,0:T(8,128)} %flow_in.1, f32[7,32,2048]{2,1,0:T(8,128)} %heat_in.1, ...), custom_call_target="tpu_custom_call" | custom-call | tf_op jit(solution)/shard_map/pallas_call | solution.py:1014
  37.2 2.9 %shard_map.113 = (f32[19,32,2048]{2,1,0:T(8,128)}, f32[7,32,2048]{2,1,0:T(8,128)}, f32[2,512]{1,0:T(2,128)}) custom-call(f32[19,32,2048]{2,1,0:T(8,128)S(1)} %get-tuple-element.10.flow, f32[7,864,128]{2,1,0:T(8,128)S(1)} %get-tuple-element.11.second_heat, f32[16,128]{1,0:T(8,128)S(1)} %get-tuple-element.12.brick, f32[128,128]{1,0:T(8,128)S(1)} %get-tuple-element.13.lost, ...), custom_call_target="tpu_custom_call" | custom-call | tf_op jit(solution)/shard_map/pallas_call | solution.py:1089
